TPU v7x, 32 devices: a whole 2x2x4 slice. The times are simulated.
32 devices in a mesh: grp: 1, node: 32 (over z, y, x, core).
Axes of the slice: x: 2, y: 2, z: 4, core: 2. Of those that a mesh axis runs over, the one named last changes fastest.
Arguments:
- hidden_in: bfloat16 [256, 7168], P(('grp', 'node')), may hold values from -6 to 6
- expert_ids: int32 [256, 4], P(('grp', 'node')), may hold values from 0 to 5, all different within a row
- gate_weights: float32 [256, 4], P(('grp', 'node')), may hold values from 0.2 to 1
- replica_pick: int32 [256, 4], P(('grp', 'node')), may hold values from 0 to 7
- placement: int32 [8], replicated, may hold values from 0 to 5, as said below
- capacity: int32 [8], replicated, may hold values from 2 to 4, as said below
- w_gate: bfloat16 [7168, 8192], P(None, 'node'), as said below
- w_up: bfloat16 [7168, 8192], P(None, 'node'), as said below
- w_down: bfloat16 [8192, 7168], P('node'), as said below
Outputs:
- mixed: bfloat16 [256, 7168], P(('grp', 'node'))
Inputs may be any that keep to these rules, and one draw needn't show every extreme that they name: `expert_ids`: each row names 4 different experts. `placement`: every expert is hosted by one slot or more. Some slot has capacity 4. `w_gate`: columns s * 1024 to (s + 1) * 1024 - 1 are the gate projection of expert placement[s]; slots that host the same expert hold equal columns. `w_up`: columns s * 1024 to (s + 1) * 1024 - 1 are the up projection of expert placement[s]; slots that host the same expert hold equal columns. `w_down`: rows s * 1024 to (s + 1) * 1024 - 1 are the down projection of expert placement[s]; slots that host the same expert hold equal rows.
All inputs are finite; a program needn't handle non-finite values.
Results may differ from a plain program's by a relative error of at most 0.0058.
Values may be sent and summed in bfloat16 or wider, within the bound.
No kernel may reach another device: no remote copies, remote signals or barrier semaphores. Data moves between devices by JAX's collectives and lax.ppermute only.
A program may use at most 128 MiB of HBM per device.

v0:
```python
import jax
import jax.numpy as jnp
from jax import lax
from jax.sharding import PartitionSpec as P


def choose_slots(expert_ids, replica_pick, placement):
    matches = (placement[None, None, :] == expert_ids[:, :, None]).astype(jnp.int32)
    prior_hits = jnp.cumsum(matches, axis=2) - matches
    hosts = jnp.sum(matches, axis=2)
    wanted = replica_pick % hosts
    slot_ids = jnp.arange(placement.shape[0], dtype=jnp.int32)
    chosen = (matches == 1) & (prior_hits == wanted[:, :, None])
    return jnp.sum(jnp.where(chosen, slot_ids[None, None, :], 0), axis=2)


def expert_rows(row_block, gate_cols, up_cols, down_rows):
    gate_act = jnp.dot(row_block, gate_cols, preferred_element_type=jnp.float32)
    up_act = jnp.dot(row_block, up_cols, preferred_element_type=jnp.float32)
    hidden = (jax.nn.silu(gate_act) * up_act).astype(jnp.bfloat16)
    return jnp.dot(hidden, down_rows, preferred_element_type=jnp.float32)


def per_device(
    hidden_in, expert_ids, gate_weights, replica_pick, placement, capacity, w_gate, w_up, w_down
):
    tok_rows, model_width = hidden_in.shape
    top_count = expert_ids.shape[1]
    node_count = placement.shape[0]
    devices = lax.axis_size("node")
    members = devices // node_count
    per_slot = members * max(1, tok_rows * top_count // (node_count * members))
    share_rows = per_slot // members
    slot_of = choose_slots(expert_ids, replica_pick, placement).reshape(-1)
    onehot = (slot_of[:, None] == jnp.arange(node_count, dtype=jnp.int32)[None, :]).astype(
        jnp.int32
    )
    earlier = jnp.cumsum(onehot, axis=0) - onehot
    rank_of = jnp.sum(onehot * earlier, axis=1)
    limits = jnp.sum(onehot * capacity[None, :], axis=1)
    kept_mask = rank_of < limits
    token_of = jnp.arange(tok_rows * top_count, dtype=jnp.int32) // top_count
    cell_count = node_count * per_slot
    cell_of = slot_of * per_slot + rank_of
    target = jnp.where(kept_mask, cell_of, cell_count)
    cell_tok = jnp.full((cell_count,), tok_rows, jnp.int32).at[target].set(token_of, mode="drop")
    padded = jnp.concatenate([hidden_in, jnp.zeros((1, model_width), hidden_in.dtype)], axis=0)
    send_rows = padded[cell_tok]
    payload = jnp.broadcast_to(
        send_rows.reshape(node_count, 1, per_slot, model_width),
        (node_count, members, per_slot, model_width),
    )
    arrived = lax.all_to_all(
        payload.reshape(devices, per_slot, model_width),
        "node",
        split_axis=0,
        concat_axis=0,
        tiled=True,
    )
    row_grid = arrived.reshape(devices, members, share_rows, model_width)
    flat_rows = row_grid.reshape(-1, model_width)
    partial_value = expert_rows(flat_rows, w_gate, w_up, w_down)
    partial_value = partial_value.reshape(devices, members, share_rows, model_width)
    returned = lax.all_to_all(partial_value, "node", split_axis=0, concat_axis=0, tiled=True)
    summed = jnp.sum(
        returned.reshape(node_count, members, members, share_rows, model_width), axis=1
    )
    table = summed.astype(jnp.bfloat16).reshape(cell_count, model_width)
    picked = table[jnp.minimum(cell_of, cell_count - 1)]
    scale_of = jnp.where(kept_mask, gate_weights.reshape(-1), 0.0)
    mixed = jnp.sum(
        (picked.astype(jnp.float32) * scale_of[:, None]).reshape(tok_rows, top_count, model_width),
        axis=1,
    )
    return mixed.astype(jnp.bfloat16)


def solution(mesh):
    placed = (
        P(("grp", "node"), None),
        P(("grp", "node"), None),
        P(("grp", "node"), None),
        P(("grp", "node"), None),
        P(),
        P(),
        P(None, "node"),
        P(None, "node"),
        P("node", None),
    )
    return jax.shard_map(
        per_device, mesh=mesh, in_specs=placed, out_specs=P(("grp", "node"), None), check_vma=False
    )
```

profile of v0, /device:TPU:0, one launch (start us, length us, event | category | flops | bytes accessed | tf_op | source)
XLA Modules:
  0.0 168.8 jit_solution(11991761709320750881)
XLA Ops:
  0.0 0.8 compare_convert_fusion
  0.8 0.9 convert_reduce_fusion
  1.7 0.7 reduce_window_sum.22
  2.3 0.8 add_select_fusion
  3.1 0.9 select_reduce_fusion.2
  4.0 0.1 copy.20
  4.1 0.1 eq.54
  4.2 0.1 fusion.9
  4.3 0.1 reduce_window_sum.23
  4.3 0.1 copy.21
  4.4 0.1 mul.52
  4.5 0.8 select_reduce_fusion.1
  5.3 0.7 scatter_custom_fusion
  6.1 0.9 concatenate.3
  7.0 0.8 gather_fusion
  7.8 0.2 broadcast_in_dim.53
  8.0 0.5 broadcast_in_dim.54
  8.5 50.3 %all_to_all.10 = bf16[32,4,7168]{2,1,0:T(4,128)(2,1)} all-to-all(bf16[32,4,7168]{2,1,0:T(4,128)(2,1)S(1)} %bitcast.26), channel_id=1, replica_groups=mesh['grp'=1,'node'=32] {'node'}, dimensions={0} | all-to-all | bytes 3670016 | tf_op jit(solution)/shard_map/all_to_all | solution.py:53
  58.8 2.9 %reshape_reshape.3 = bf16[128,7168]{1,0:T(8,128)(2,1)S(1)} reshape(bf16[32,4,7168]{2,1,0:T(4,128)(2,1)} %all_to_all.10) | data formatting | bytes 3670016 | tf_op jit(solution)/shard_map/reshape;reshape | solution.py:61
  61.8 2.7 %fusion.16 = f32[128,256]{1,0:T(8,128)S(1)} fusion(bf16[128,7168]{1,0:T(8,128)(2,1)S(1)} %reshape_reshape.3, bf16[7168,256]{1,0:T(8,128)(2,1)} %param.15), kind=kOutput, calls=%fused_computation.44 | convolution fusion | flops 469762048 | bytes 5636096 | tf_op jit(solution)/shard_map/dot_general | solution.py:18
  64.5 7.1 %fusion.1 = f32[128,7168]{1,0:T(8,128)} fusion(bf16[256,7168]{1,0:T(8,128)(2,1)} %param.17, bf16[128,7168]{1,0:T(8,128)(2,1)S(1)} %reshape_reshape.3, bf16[7168,256]{1,0:T(8,128)(2,1)} %param.16, f32[128,256]{1,0:T(8,128)S(1)} %fusion.16), kind=kOutput, calls=%fused_computation.5 | convolution fusion | flops 939720704 | bytes 12976128 | tf_op jit(solution)/shard_map/dot_general | solution.py:21
  71.6 5.2 %reshape.104 = f32[32,4,1,7168]{3,1,0,2:T(4,128)} reshape(f32[128,7168]{1,0:T(8,128)} %fusion.1) | data formatting | bytes 7340032 | tf_op jit(solution)/shard_map/reshape | solution.py:63
  76.8 0.0 copy-start
  76.8 3.7 %all-to-all-start.1 = ((f32[32,4,1,7168]{3,1,2,0:T(4,128)}), f32[32,4,1,7168]{3,1,2,0:T(4,128)}, u32[]{:S(2)}, u32[]{:S(2)}) async-start(f32[32,4,1,7168]{3,1,2,0:T(4,128)} %bitcast.25), calls=%async_computation.1 | async-start | bytes 7340032 | tf_op jit(solution)/shard_map/all_to_all | solution.py:64
  80.5 0.1 lt.56
  80.6 0.0 copy-done
  80.6 0.1 copy.23
  80.7 82.4 %all-to-all-done.1 = f32[32,4,1,7168]{3,1,2,0:T(4,128)} async-done(((f32[32,4,1,7168]{3,1,2,0:T(4,128)}), f32[32,4,1,7168]{3,1,2,0:T(4,128)}, u32[]{:S(2)}, u32[]{:S(2)}) %all-to-all-start.1) | async-done | bytes 3670048 | tf_op jit(solution)/shard_map/all_to_all | solution.py:64
  163.1 3.2 %reduce_sum.64 = bf16[8,4,7168]{2,1,0:T(4,128)(2,1)S(1)} reduce(f32[8,4,4,7168]{3,2,1,0:T(4,128)} %bitcast.5, f32[]{:T(128)} %constant.49.clone.1), dimensions={1}, to_apply=%region_7.8 | reduce | flops 688128 | bytes 4128772 | tf_op jit(solution)/shard_map/reduce_sum | solution.py:65
  166.3 0.1 convert_element_type.32
  166.4 0.8 gather_fusion.1
  167.3 0.3 reshape.106
  167.6 1.3 multiply_reduce_fusion
  (8 shorter events, 0.0 us)
Async XLA Ops:
  76.8 3.8 %copy-start = (f32[8,4]{0,1:T(4,128)S(1)}, f32[8,4]{0,1:T(4,128)}, u32[]{:S(2)}) copy-start(f32[8,4]{0,1:T(4,128)} %param.11) | copy-start | bytes 388
  76.8 86.4 %all-to-all-start.1 = ((f32[32,4,1,7168]{3,1,2,0:T(4,128)}), f32[32,4,1,7168]{3,1,2,0:T(4,128)}, u32[]{:S(2)}, u32[]{:S(2)}) async-start(f32[32,4,1,7168]{3,1,2,0:T(4,128)} %bitcast.25), calls=%async_computation.1 | async-start | bytes 7340032 | tf_op jit(solution)/shard_map/all_to_all | solution.py:64
where the time goes:
time: 169 us
  waiting for transfers between devices  82.4 us (49%)
  blocking collectives  50.3 us (30%)
  local copies, waits for them, and re-layouts  13 us (8%)
  matrix products  9.82 us (6%)
  other arithmetic  9.49 us (6%)
  starting transfers between devices  3.73 us (2%)
    all_to_all x1, waiting for transfers between devices, per_device(): lax.all_to_all(partial_value, 'node', split_axis=0, concat_axis=0, tiled=...  82.4 us
    all_to_all x1, blocking collectives, per_device(): lax.all_to_all(payload.reshape(devices, per_slot, model_width), 'node', s...  50.3 us
    dot_general x1, matrix products, expert_rows(): return jnp.dot(hidden, down_rows, preferred_element_type=jnp.float32)  7.13 us
    reshape x1, local copies, waits for them, and re-layouts, per_device(): partial_value.reshape(devices, members, share_rows, model_width)  5.16 us
    all_to_all x1, starting transfers between devices, per_device(): lax.all_to_all(partial_value, 'node', split_axis=0, concat_axis=0, tiled=...  3.73 us
  transfers between devices with their start and end apart: 1, of which 1 were waited for; matrix products, arithmetic and copies ran while one was open for 0% of the time, Pallas kernels for 0%

commit v1 on v0

v1 whole, which is shorter than its diff:
```python
import functools

import jax
import jax.numpy as jnp
from jax import lax
from jax.sharding import PartitionSpec as P


def route(expert_ids, gate_weights, replica_pick, placement, capacity, slot_label):
    slots = placement.shape[0]
    ids = jnp.arange(slots, dtype=jnp.int32)
    same = (placement[:, None] == placement[None, :]) & (ids[None, :] < ids[:, None])
    turn = jnp.sum(same.astype(jnp.int32), axis=1)
    pick = (slot_label[:, None] == ids[None, :]).astype(jnp.int32)
    place_q = jnp.sum(pick * placement[None, :], axis=1)
    turn_q = jnp.sum(pick * turn[None, :], axis=1)
    cap_q = jnp.sum(pick * capacity[None, :], axis=1)
    match = expert_ids[:, :, None] == place_q[None, None, :]
    hosts = jnp.sum(match.astype(jnp.int32), axis=2)
    wanted = replica_pick % hosts
    chosen = match & (turn_q[None, None, :] == wanted[:, :, None])
    used = jnp.sum(chosen.astype(jnp.int32), axis=1)
    weight = jnp.sum(jnp.where(chosen, gate_weights[:, :, None], 0.0), axis=1)
    toks = jnp.arange(expert_ids.shape[0], dtype=jnp.int32)
    rank = jnp.sum(jnp.where((toks[None, :] < toks[:, None])[:, :, None], used[None, :, :], 0), axis=1)
    kept = (used > 0) & (rank < cap_q[None, :])
    return kept, rank, weight


def per_device(
    hidden_in, expert_ids, gate_weights, replica_pick, placement, capacity, w_gate, w_up, w_down
):
    tok_rows, width = hidden_in.shape
    top = expert_ids.shape[1]
    slots = placement.shape[0]
    devices = lax.axis_size("node")
    members = devices // slots
    cells = members * max(1, tok_rows * top // (slots * members))
    bf16, f32 = jnp.bfloat16, jnp.float32
    my_slot = lax.axis_index("node") // members
    order = jnp.arange(slots, dtype=jnp.int32)

    def send(value, flip):
        return lax.ppermute(value, "node", [(d, d ^ flip) for d in range(devices)])

    kept, rank, weight = route(
        expert_ids, gate_weights, replica_pick, placement, capacity, order ^ my_slot
    )
    cell = jnp.arange(cells, dtype=jnp.int32)
    spot = kept.T[:, None, :] & (rank.T[:, None, :] == cell[None, :, None])
    pack = spot.astype(bf16).reshape(slots * cells, tok_rows)
    scale = jnp.where(spot, weight.T[:, None, :], 0.0).reshape(slots * cells, tok_rows).T
    packed = jnp.dot(pack, hidden_in, preferred_element_type=f32).astype(bf16)
    packed = packed.reshape(slots, cells, width)
    parts = [packed[q] if q == 0 else send(packed[q], q * members) for q in range(slots)]
    mine = jnp.concatenate(parts, axis=0)
    flips = [2, 1]
    rows = mine
    for flip in flips:
        rows = jnp.concatenate([rows, send(rows, flip)], axis=0)
    gate_act = jnp.dot(rows, w_gate, preferred_element_type=f32)
    up_act = jnp.dot(rows, w_up, preferred_element_type=f32)
    hid = (jax.nn.silu(gate_act) * up_act).astype(bf16)
    out = jnp.dot(hid, w_down, preferred_element_type=f32)
    for flip in reversed(flips):
        half = out.shape[0] // 2
        out = out[:half] + send(out[half:].astype(bf16), flip).astype(f32)
    out = out.astype(bf16).reshape(slots, cells, width)
    back = [out[q] if q == 0 else send(out[q], q * members) for q in range(slots)]
    back = jnp.concatenate(back, axis=0)
    mixed = jnp.dot(scale, back.astype(f32), precision=lax.Precision.HIGHEST, preferred_element_type=f32)
    return mixed.astype(bf16)


def solution(mesh):
    split = P(("grp", "node"), None)
    placed = (split, split, split, split, P(), P(), P(None, "node"), P(None, "node"), P("node", None))
    return jax.shard_map(per_device, mesh=mesh, in_specs=placed, out_specs=split, check_vma=False)
```

time: 169 us -> 87.3 us (0.52)
  blocking collectives: 50.3 us -> 0 us
  waiting for transfers between devices: 82.4 us -> 35.3 us
  starting transfers between devices: 3.73 us -> 27.5 us
  local copies, waits for them, and re-layouts: 13 us -> 6.41 us
  other arithmetic: 9.49 us -> 6.32 us
    all_to_all x1 -> x0, waiting for transfers between devices: 82.4 us -> none  [per_device(): lax.all_to_all(partial_value, 'node', split_axis=0, concat_axis=0, tiled=...]
    all_to_all x1 -> x0, blocking collectives: 50.3 us -> none  [per_device(): lax.all_to_all(payload.reshape(devices, per_slot, model_width), 'node', s...]
    ppermute x0 -> x18, waiting for transfers between devices: none -> 35.3 us  [send(): return lax.ppermute(value, 'node', [(d, d ^ flip) for d in range(devices)])]
    ppermute x0 -> x18, starting transfers between devices: none -> 27.5 us  [send(): return lax.ppermute(value, 'node', [(d, d ^ flip) for d in range(devices)])]
    reshape x1 -> x0, local copies, waits for them, and re-layouts: 5.16 us -> none  [per_device(): partial_value.reshape(devices, members, share_rows, model_width)]
    all_to_all x1 -> x0, starting transfers between devices: 3.73 us -> none  [per_device(): lax.all_to_all(partial_value, 'node', split_axis=0, concat_axis=0, tiled=...]
    reduce_sum x5 -> x6, other arithmetic: 7.1 us -> 3.62 us  [the longest x1 0.91 us: route(): turn = jnp.sum(same.astype(jnp.int32), axis=1)]
    another operation x1 -> x0, local copies, waits for them, and re-layouts: 2.94 us -> none  [per_device(): flat_rows = row_grid.reshape(-1, model_width)]
  transfers between devices with their start and end apart: 1 -> 18, of which waited for: 1 -> 9; matrix products, arithmetic and copies ran while one was open for 0% -> 0% of each run, Pallas kernels for 0% -> 0%
where the time goes in v1:
time: 87.3 us; the launch traced here: 86.9 us
  waiting for transfers between devices  35.3 us (40%)
  starting transfers between devices  27.5 us (32%)
  matrix products  11 us (13%)
  local copies, waits for them, and re-layouts  6.41 us (7%)
  other arithmetic  6.32 us (7%)
    ppermute x18, waiting for transfers between devices, send(): return lax.ppermute(value, 'node', [(d, d ^ flip) for d in range(devices)])  35.3 us
    ppermute x18, starting transfers between devices, send(): return lax.ppermute(value, 'node', [(d, d ^ flip) for d in range(devices)])  27.5 us
    dot_general x1, matrix products, per_device(): out = jnp.dot(hid, w_down, preferred_element_type=f32)  7.09 us
    concatenate x2, local copies, waits for them, and re-layouts, per_device(): rows = jnp.concatenate([rows, send(rows, flip)], axis=0)  2.87 us
    dot_general x1, matrix products, per_device(): gate_act = jnp.dot(rows, w_gate, preferred_element_type=f32)  2.68 us
  transfers between devices with their start and end apart: 18, of which 9 were waited for; matrix products, arithmetic and copies ran while one was open for 0% of the time, Pallas kernels for 0%

profile of v1, /device:TPU:0, one launch (start us, length us, event | category | flops | bytes accessed | tf_op | source)
XLA Modules:
  0.0 86.9 jit_solution(5444725288343532612)
XLA Ops:
  0.0 0.9 %convert_reduce_fusion.1 = s32[8]{0:T(128)S(1)} fusion(s32[8]{0:T(128)} %param.13), kind=kLoop, calls=%fused_computation.22 | loop fusion | flops 312 | bytes 64 | tf_op jit(solution)/shard_map/reduce_sum | solution.py:13
  0.9 0.9 %select_reduce_fusion.2 = (s32[8]{0:T(128)S(1)}, s32[8]{0:T(128)S(1)}, s32[8]{0:T(128)S(1)}) fusion(s32[8]{0:T(128)} %param.14, s32[8]{0:T(128)S(1)} %iota_xor_fusion, s32[8]{0:T(128)S(1)} %convert_reduce_fusion.1, s32[8]{0:T(128)} %param.13), kind=kLoop, calls=%fused_computation.20 | loop fusion | flops 424 | bytes 224 | tf_op jit(solution)/shard_map/reduce_sum | solution.py:17
  1.8 0.9 %fusion.3 = s32[8,4]{0,1:T(4,128)S(1)} fusion(s32[8]{0:T(128)S(1)} %get-tuple-element.7, s32[8,4]{0,1:T(4,128)} %param.10), kind=kLoop, calls=%fused_computation.13 | loop fusion | flops 736 | bytes 288 | tf_op jit(solution)/shard_map/reduce_sum | solution.py:19
  2.7 0.8 add_select_fusion
  3.5 0.6 copy-done.7
  4.1 0.8 convert_reduce_fusion
  4.9 0.1 select_reduce_fusion
  5.0 0.1 copy.21
  5.1 0.1 copy.20
  5.2 0.1 eq.95
  5.3 0.1 compare_and_fusion.1
  5.4 0.2 convolution_convert_fusion
  5.6 0.2 fusion.9
  5.8 3.1 %collective-permute-start = (bf16[4,7168]{1,0:T(4,128)(2,1)S(1)}, bf16[4,7168]{1,0:T(4,128)(2,1)S(1)}, u32[]{:S(2)}, u32[]{:S(2)}) collective-permute-start(bf16[4,7168]{1,0:T(4,128)(2,1)S(1)} %get-tuple-element.22), channel_id=1, source_target_pairs={{0,4},{1,5},{2,6},{3,7},{4,0},{5,1},{6,2},{7,3},{8,12},{9,13},{10,... | collective-permute-start | bytes 172040 | tf_op jit(solution)/shard_map/ppermute | solution.py:44
  8.8 1.6 %collective-permute-start.1 = (bf16[4,7168]{1,0:T(4,128)(2,1)S(1)}, bf16[4,7168]{1,0:T(4,128)(2,1)S(1)}, u32[]{:S(2)}, u32[]{:S(2)}) collective-permute-start(bf16[4,7168]{1,0:T(4,128)(2,1)S(1)} %get-tuple-element.21), channel_id=1, source_target_pairs={{0,8},{1,9},{2,10},{3,11},{4,12},{5,13},{6,14},{7,15},{8,0},{9,1},... | collective-permute-start | bytes 172040 | tf_op jit(solution)/shard_map/ppermute | solution.py:44
  10.4 0.0 collective-permute-start.2
  10.4 3.0 %collective-permute-start.3 = (bf16[4,7168]{1,0:T(4,128)(2,1)S(1)}, bf16[4,7168]{1,0:T(4,128)(2,1)S(1)}, u32[]{:S(2)}, u32[]{:S(2)}) collective-permute-start(bf16[4,7168]{1,0:T(4,128)(2,1)S(1)} %get-tuple-element.19), channel_id=1, source_target_pairs={{0,16},{1,17},{2,18},{3,19},{4,20},{5,21},{6,22},{7,23},{8,24},{9,... | collective-permute-start | bytes 172040 | tf_op jit(solution)/shard_map/ppermute | solution.py:44
  13.4 1.3 %collective-permute-start.4 = (bf16[4,7168]{1,0:T(4,128)(2,1)S(1)}, bf16[4,7168]{1,0:T(4,128)(2,1)S(1)}, u32[]{:S(2)}, u32[]{:S(2)}) collective-permute-start(bf16[4,7168]{1,0:T(4,128)(2,1)S(1)} %get-tuple-element.18), channel_id=1, source_target_pairs={{0,20},{1,21},{2,22},{3,23},{4,16},{5,17},{6,18},{7,19},{8,28},{9,... | collective-permute-start | bytes 172040 | tf_op jit(solution)/shard_map/ppermute | solution.py:44
  14.7 0.0 collective-permute-done
  14.7 3.6 %collective-permute-start.5 = (bf16[4,7168]{1,0:T(4,128)(2,1)S(1)}, bf16[4,7168]{1,0:T(4,128)(2,1)S(1)}, u32[]{:S(2)}, u32[]{:S(2)}) collective-permute-start(bf16[4,7168]{1,0:T(4,128)(2,1)S(1)} %get-tuple-element.17), channel_id=1, source_target_pairs={{0,24},{1,25},{2,26},{3,27},{4,28},{5,29},{6,30},{7,31},{8,16},{9,... | collective-permute-start | bytes 172040 | tf_op jit(solution)/shard_map/ppermute | solution.py:44
  18.3 0.0 collective-permute-done.1
  18.3 0.0 collective-permute-start.6
  18.3 0.0 collective-permute-done.2
  18.3 0.0 collective-permute-done.3
  18.3 4.3 %collective-permute-done.4 = bf16[4,7168]{1,0:T(4,128)(2,1)S(1)} collective-permute-done((bf16[4,7168]{1,0:T(4,128)(2,1)S(1)}, bf16[4,7168]{1,0:T(4,128)(2,1)S(1)}, u32[]{:S(2)}, u32[]{:S(2)}) %collective-permute-start.4) | collective-permute-done | bytes 57376 | tf_op jit(solution)/shard_map/ppermute | solution.py:44
  22.6 0.0 collective-permute-done.5
  22.6 2.6 %collective-permute-done.6 = bf16[4,7168]{1,0:T(4,128)(2,1)S(1)} collective-permute-done((bf16[4,7168]{1,0:T(4,128)(2,1)S(1)}, bf16[4,7168]{1,0:T(4,128)(2,1)S(1)}, u32[]{:S(2)}, u32[]{:S(2)}) %collective-permute-start.6) | collective-permute-done | bytes 57376 | tf_op jit(solution)/shard_map/ppermute | solution.py:44
  25.2 0.3 concatenate.14
  25.5 1.6 %collective-permute-start.7 = (bf16[32,7168]{1,0:T(8,128)(2,1)S(1)}, bf16[32,7168]{1,0:T(8,128)(2,1)S(1)}, u32[]{:S(2)}, u32[]{:S(2)}) collective-permute-start(bf16[32,7168]{1,0:T(8,128)(2,1)S(1)} %concatenate.14), channel_id=1, source_target_pairs={{0,2},{1,3},{2,0},{3,1},{4,6},{5,7},{6,4},{7,5},{8,10},{9,11},{10,... | collective-permute-start | bytes 1376264 | tf_op jit(solution)/shard_map/ppermute | solution.py:44
  27.1 8.0 %collective-permute-done.7 = bf16[32,7168]{1,0:T(8,128)(2,1)S(1)} collective-permute-done((bf16[32,7168]{1,0:T(8,128)(2,1)S(1)}, bf16[32,7168]{1,0:T(8,128)(2,1)S(1)}, u32[]{:S(2)}, u32[]{:S(2)}) %collective-permute-start.7) | collective-permute-done | bytes 458784 | tf_op jit(solution)/shard_map/ppermute | solution.py:44
  35.1 0.5 concatenate.15
  35.6 0.1 collective-permute-start.8
  35.7 2.4 %collective-permute-done.8 = bf16[64,7168]{1,0:T(8,128)(2,1)S(1)} collective-permute-done((bf16[64,7168]{1,0:T(8,128)(2,1)S(1)}, bf16[64,7168]{1,0:T(8,128)(2,1)S(1)}, u32[]{:S(2)}, u32[]{:S(2)}) %collective-permute-start.8) | collective-permute-done | bytes 917536 | tf_op jit(solution)/shard_map/ppermute | solution.py:44
  38.1 2.4 %concatenate.16 = bf16[128,7168]{1,0:T(8,128)(2,1)S(1)} concatenate(bf16[4,7168]{1,0:T(4,128)(2,1)S(1)} %get-tuple-element.23, bf16[4,7168]{1,0:T(4,128)(2,1)S(1)} %collective-permute-done, bf16[4,7168]{1,0:T(4,128)(2,1)S(1)} %collective-permute-done.1, bf16[4,7168]{1,0:T(4,128)(2,1)S(1)} %collective-permute-done.2, bf16[4,7168]{1,0:T(4,128)(2,1)} %copy-done.1, ...), dimensions={0} | concatenate | bytes 3670016 | tf_op jit(solution)/shard_map/concatenate | solution.py:60
  40.5 2.7 %fusion.12 = f32[128,256]{1,0:T(8,128)S(1)} fusion(bf16[128,7168]{1,0:T(8,128)(2,1)S(1)} %concatenate.16, bf16[7168,256]{1,0:T(8,128)(2,1)} %param.15), kind=kOutput, calls=%fused_computation.34 | convolution fusion | flops 469762048 | bytes 5636096 | tf_op jit(solution)/shard_map/dot_general | solution.py:61
  43.2 7.1 %fusion.1 = f32[128,7168]{1,0:T(8,128)} fusion(bf16[256,7168]{1,0:T(8,128)(2,1)} %param.17, f32[128,256]{1,0:T(8,128)S(1)} %fusion.12, bf16[128,7168]{1,0:T(8,128)(2,1)S(1)} %concatenate.16, bf16[7168,256]{1,0:T(8,128)(2,1)} %param.16), kind=kOutput, calls=%fused_computation.8 | convolution fusion | flops 939720704 | bytes 12976128 | tf_op jit(solution)/shard_map/dot_general | solution.py:64
  50.3 1.6 %slice.124 = bf16[64,7168]{1,0:T(8,128)(2,1)S(1)} slice(f32[128,7168]{1,0:T(8,128)} %fusion.1), slice={[64:128], [0:7168]} | slice | bytes 1835008 | tf_op jit(solution)/shard_map/slice | solution.py:67
  51.9 0.0 copy-start.9
  51.9 0.0 copy-start.14
  52.0 0.2 collective-permute-start.9
  52.2 2.3 %collective-permute-done.9 = bf16[64,7168]{1,0:T(8,128)(2,1)S(1)} collective-permute-done((bf16[64,7168]{1,0:T(8,128)(2,1)S(1)}, bf16[64,7168]{1,0:T(8,128)(2,1)S(1)}, u32[]{:S(2)}, u32[]{:S(2)}) %collective-permute-start.9) | collective-permute-done | bytes 917536 | tf_op jit(solution)/shard_map/ppermute | solution.py:44
  54.5 1.7 %slice_add_fusion = f32[64,7168]{1,0:T(8,128)S(1)} fusion(f32[128,7168]{1,0:T(8,128)} %fusion.1, bf16[64,7168]{1,0:T(8,128)(2,1)S(1)} %collective-permute-done.9), kind=kLoop, calls=%fused_computation.3 | loop fusion | flops 917504 | bytes 4587520 | tf_op jit(solution)/shard_map/add | solution.py:67
  56.3 1.6 %collective-permute-start.10 = (bf16[32,7168]{1,0:T(8,128)(2,1)S(1)}, bf16[32,7168]{1,0:T(8,128)(2,1)S(1)}, u32[]{:S(2)}, u32[]{:S(2)}) collective-permute-start(bf16[32,7168]{1,0:T(8,128)(2,1)S(1)} %slice.125), channel_id=1, source_target_pairs={{0,2},{1,3},{2,0},{3,1},{4,6},{5,7},{6,4},{7,5},{8,10},{9,11},{10,... | collective-permute-start | bytes 1376264 | tf_op jit(solution)/shard_map/ppermute | solution.py:44
  57.8 11.1 %collective-permute-done.10 = bf16[32,7168]{1,0:T(8,128)(2,1)S(1)} collective-permute-done((bf16[32,7168]{1,0:T(8,128)(2,1)S(1)}, bf16[32,7168]{1,0:T(8,128)(2,1)S(1)}, u32[]{:S(2)}, u32[]{:S(2)}) %collective-permute-start.10) | collective-permute-done | bytes 458784 | tf_op jit(solution)/shard_map/ppermute | solution.py:44
  68.9 0.1 fusion
  69.0 0.2 fusion.8
  69.1 0.8 collective-permute-start.11
  70.0 2.5 %collective-permute-start.12 = (bf16[4,7168]{1,0:T(4,128)(2,1)S(1)}, bf16[4,7168]{1,0:T(4,128)(2,1)S(1)}, u32[]{:S(2)}, u32[]{:S(2)}) collective-permute-start(bf16[4,7168]{1,0:T(4,128)(2,1)S(1)} %get-tuple-element.13), channel_id=1, source_target_pairs={{0,8},{1,9},{2,10},{3,11},{4,12},{5,13},{6,14},{7,15},{8,0},{9,1},... | collective-permute-start | bytes 172040 | tf_op jit(solution)/shard_map/ppermute | solution.py:44
  72.5 0.2 collective-permute-start.13
  72.7 3.3 %collective-permute-start.14 = (bf16[4,7168]{1,0:T(4,128)(2,1)S(1)}, bf16[4,7168]{1,0:T(4,128)(2,1)S(1)}, u32[]{:S(2)}, u32[]{:S(2)}) collective-permute-start(bf16[4,7168]{1,0:T(4,128)(2,1)S(1)} %get-tuple-element.11), channel_id=1, source_target_pairs={{0,16},{1,17},{2,18},{3,19},{4,20},{5,21},{6,22},{7,23},{8,24},{9,... | collective-permute-start | bytes 172040 | tf_op jit(solution)/shard_map/ppermute | solution.py:44
  76.0 0.3 collective-permute-start.15
  76.4 0.0 collective-permute-done.11
  76.4 2.2 %collective-permute-start.16 = (bf16[4,7168]{1,0:T(4,128)(2,1)S(1)}, bf16[4,7168]{1,0:T(4,128)(2,1)S(1)}, u32[]{:S(2)}, u32[]{:S(2)}) collective-permute-start(bf16[4,7168]{1,0:T(4,128)(2,1)S(1)} %get-tuple-element.9), channel_id=1, source_target_pairs={{0,24},{1,25},{2,26},{3,27},{4,28},{5,29},{6,30},{7,31},{8,16},{9,... | collective-permute-start | bytes 172040 | tf_op jit(solution)/shard_map/ppermute | solution.py:44
  78.5 0.0 collective-permute-done.12
  78.5 2.2 %collective-permute-start.17 = (bf16[4,7168]{1,0:T(4,128)(2,1)S(1)}, bf16[4,7168]{1,0:T(4,128)(2,1)S(1)}, u32[]{:S(2)}, u32[]{:S(2)}) collective-permute-start(bf16[4,7168]{1,0:T(4,128)(2,1)S(1)} %get-tuple-element.8), channel_id=1, source_target_pairs={{0,28},{1,29},{2,30},{3,31},{4,24},{5,25},{6,26},{7,27},{8,20},{9,... | collective-permute-start | bytes 172040 | tf_op jit(solution)/shard_map/ppermute | solution.py:44
  80.8 0.1 select_reduce_fusion.1
  80.8 0.1 copy.22
  80.9 0.0 collective-permute-done.13
  80.9 0.1 collective-permute-done.14
  81.1 2.9 %collective-permute-done.15 = bf16[4,7168]{1,0:T(4,128)(2,1)S(1)} collective-permute-done((bf16[4,7168]{1,0:T(4,128)(2,1)S(1)}, bf16[4,7168]{1,0:T(4,128)(2,1)S(1)}, u32[]{:S(2)}, u32[]{:S(2)}) %collective-permute-start.15) | collective-permute-done | bytes 57376 | tf_op jit(solution)/shard_map/ppermute | solution.py:44
  83.9 0.0 collective-permute-done.16
  83.9 1.6 %collective-permute-done.17 = bf16[4,7168]{1,0:T(4,128)(2,1)S(1)} collective-permute-done((bf16[4,7168]{1,0:T(4,128)(2,1)S(1)}, bf16[4,7168]{1,0:T(4,128)(2,1)S(1)}, u32[]{:S(2)}, u32[]{:S(2)}) %collective-permute-start.17) | collective-permute-done | bytes 57376 | tf_op jit(solution)/shard_map/ppermute | solution.py:44
  85.5 0.3 concatenate.17
  85.8 1.0 %convolution_convert_fusion.1 = bf16[8,7168]{1,0:T(8,128)(2,1)} fusion(bf16[32,7168]{1,0:T(8,128)(2,1)S(1)} %concatenate.17, pred[32,8]{1,0:T(32,128)(4,1)S(1)} %copy-done.6, f32[32,8]{1,0:T(8,128)S(1)} %bitcast.16), kind=kOutput, calls=%fused_computation.1 | convolution fusion | flops 22077696 | bytes 574720 | tf_op jit(solution)/shard_map/dot_general | solution.py:71
  (35 shorter events, 0.1 us)
Async XLA Ops:
  0.0 5.4 %copy-start = (bf16[8,7168]{1,0:T(8,128)(2,1)S(1)}, bf16[8,7168]{1,0:T(8,128)(2,1)}, u32[]{:S(2)}) copy-start(bf16[8,7168]{1,0:T(8,128)(2,1)} %param.9) | copy-start | bytes 344068
  1.8 3.2 %copy-start.10 = (s32[8]{0:T(128)}, s32[8]{0:T(128)S(1)}, u32[]{:S(2)}) copy-start(s32[8]{0:T(128)S(1)} %get-tuple-element.7) | copy-start | bytes 100
  1.8 3.2 %copy-start.12 = (s32[8]{0:T(128)}, s32[8]{0:T(128)S(1)}, u32[]{:S(2)}) copy-start(s32[8]{0:T(128)S(1)} %get-tuple-element.6) | copy-start | bytes 100
  3.5 0.6 copy-start.7
  5.4 19.8 %copy-start.5 = (pred[32,8]{1,0:T(32,128)(4,1)}, pred[32,8]{1,0:T(32,128)(4,1)S(1)}, u32[]{:S(2)}) copy-start(pred[32,8]{1,0:T(32,128)(4,1)S(1)} %compare_and_fusion.1) | copy-start | bytes 772
  5.8 8.9 %collective-permute-start = (bf16[4,7168]{1,0:T(4,128)(2,1)S(1)}, bf16[4,7168]{1,0:T(4,128)(2,1)S(1)}, u32[]{:S(2)}, u32[]{:S(2)}) collective-permute-start(bf16[4,7168]{1,0:T(4,128)(2,1)S(1)} %get-tuple-element.22), channel_id=1, source_target_pairs={{0,4},{1,5},{2,6},{3,7},{4,0},{5,1},{6,2},{7,3},{8,12},{9,13},{10,... | collective-permute-start | bytes 172040 | tf_op jit(solution)/shard_map/ppermute | solution.py:44
  8.8 9.5 %collective-permute-start.1 = (bf16[4,7168]{1,0:T(4,128)(2,1)S(1)}, bf16[4,7168]{1,0:T(4,128)(2,1)S(1)}, u32[]{:S(2)}, u32[]{:S(2)}) collective-permute-start(bf16[4,7168]{1,0:T(4,128)(2,1)S(1)} %get-tuple-element.21), channel_id=1, source_target_pairs={{0,8},{1,9},{2,10},{3,11},{4,12},{5,13},{6,14},{7,15},{8,0},{9,1},... | collective-permute-start | bytes 172040 | tf_op jit(solution)/shard_map/ppermute | solution.py:44
  10.4 7.9 %collective-permute-start.2 = (bf16[4,7168]{1,0:T(4,128)(2,1)S(1)}, bf16[4,7168]{1,0:T(4,128)(2,1)S(1)}, u32[]{:S(2)}, u32[]{:S(2)}) collective-permute-start(bf16[4,7168]{1,0:T(4,128)(2,1)S(1)} %get-tuple-element.20), channel_id=1, source_target_pairs={{0,12},{1,13},{2,14},{3,15},{4,8},{5,9},{6,10},{7,11},{8,4},{9,5},... | collective-permute-start | bytes 172040 | tf_op jit(solution)/shard_map/ppermute | solution.py:44
  10.4 7.9 %collective-permute-start.3 = (bf16[4,7168]{1,0:T(4,128)(2,1)S(1)}, bf16[4,7168]{1,0:T(4,128)(2,1)S(1)}, u32[]{:S(2)}, u32[]{:S(2)}) collective-permute-start(bf16[4,7168]{1,0:T(4,128)(2,1)S(1)} %get-tuple-element.19), channel_id=1, source_target_pairs={{0,16},{1,17},{2,18},{3,19},{4,20},{5,21},{6,22},{7,23},{8,24},{9,... | collective-permute-start | bytes 172040 | tf_op jit(solution)/shard_map/ppermute | solution.py:44
  13.4 9.2 %collective-permute-start.4 = (bf16[4,7168]{1,0:T(4,128)(2,1)S(1)}, bf16[4,7168]{1,0:T(4,128)(2,1)S(1)}, u32[]{:S(2)}, u32[]{:S(2)}) collective-permute-start(bf16[4,7168]{1,0:T(4,128)(2,1)S(1)} %get-tuple-element.18), channel_id=1, source_target_pairs={{0,20},{1,21},{2,22},{3,23},{4,16},{5,17},{6,18},{7,19},{8,28},{9,... | collective-permute-start | bytes 172040 | tf_op jit(solution)/shard_map/ppermute | solution.py:44
  14.7 7.9 %collective-permute-start.5 = (bf16[4,7168]{1,0:T(4,128)(2,1)S(1)}, bf16[4,7168]{1,0:T(4,128)(2,1)S(1)}, u32[]{:S(2)}, u32[]{:S(2)}) collective-permute-start(bf16[4,7168]{1,0:T(4,128)(2,1)S(1)} %get-tuple-element.17), channel_id=1, source_target_pairs={{0,24},{1,25},{2,26},{3,27},{4,28},{5,29},{6,30},{7,31},{8,16},{9,... | collective-permute-start | bytes 172040 | tf_op jit(solution)/shard_map/ppermute | solution.py:44
  18.3 6.9 %collective-permute-start.6 = (bf16[4,7168]{1,0:T(4,128)(2,1)S(1)}, bf16[4,7168]{1,0:T(4,128)(2,1)S(1)}, u32[]{:S(2)}, u32[]{:S(2)}) collective-permute-start(bf16[4,7168]{1,0:T(4,128)(2,1)S(1)} %get-tuple-element.16), channel_id=1, source_target_pairs={{0,28},{1,29},{2,30},{3,31},{4,24},{5,25},{6,26},{7,27},{8,20},{9,... | collective-permute-start | bytes 172040 | tf_op jit(solution)/shard_map/ppermute | solution.py:44
  18.3 17.3 %copy-start.1 = (bf16[4,7168]{1,0:T(4,128)(2,1)}, bf16[4,7168]{1,0:T(4,128)(2,1)S(1)}, u32[]{:S(2)}) copy-start(bf16[4,7168]{1,0:T(4,128)(2,1)S(1)} %collective-permute-done.3) | copy-start | bytes 172036
  22.6 13.1 %copy-start.2 = (bf16[4,7168]{1,0:T(4,128)(2,1)}, bf16[4,7168]{1,0:T(4,128)(2,1)S(1)}, u32[]{:S(2)}) copy-start(bf16[4,7168]{1,0:T(4,128)(2,1)S(1)} %collective-permute-done.4) | copy-start | bytes 172036
  22.6 13.1 %copy-start.3 = (bf16[4,7168]{1,0:T(4,128)(2,1)}, bf16[4,7168]{1,0:T(4,128)(2,1)S(1)}, u32[]{:S(2)}) copy-start(bf16[4,7168]{1,0:T(4,128)(2,1)S(1)} %collective-permute-done.5) | copy-start | bytes 172036
  25.2 10.5 %copy-start.4 = (bf16[4,7168]{1,0:T(4,128)(2,1)}, bf16[4,7168]{1,0:T(4,128)(2,1)S(1)}, u32[]{:S(2)}) copy-start(bf16[4,7168]{1,0:T(4,128)(2,1)S(1)} %collective-permute-done.6) | copy-start | bytes 172036
  25.5 9.6 %collective-permute-start.7 = (bf16[32,7168]{1,0:T(8,128)(2,1)S(1)}, bf16[32,7168]{1,0:T(8,128)(2,1)S(1)}, u32[]{:S(2)}, u32[]{:S(2)}) collective-permute-start(bf16[32,7168]{1,0:T(8,128)(2,1)S(1)} %concatenate.14), channel_id=1, source_target_pairs={{0,2},{1,3},{2,0},{3,1},{4,6},{5,7},{6,4},{7,5},{8,10},{9,11},{10,... | collective-permute-start | bytes 1376264 | tf_op jit(solution)/shard_map/ppermute | solution.py:44
  35.6 2.5 %collective-permute-start.8 = (bf16[64,7168]{1,0:T(8,128)(2,1)S(1)}, bf16[64,7168]{1,0:T(8,128)(2,1)S(1)}, u32[]{:S(2)}, u32[]{:S(2)}) collective-permute-start(bf16[64,7168]{1,0:T(8,128)(2,1)S(1)} %concatenate.15), channel_id=1, source_target_pairs={{0,1},{1,0},{2,3},{3,2},{4,5},{5,4},{6,7},{7,6},{8,9},{9,8},{10,11... | collective-permute-start | bytes 2752520 | tf_op jit(solution)/shard_map/ppermute | solution.py:44
  51.9 28.8 %copy-start.8 = (s32[8,4]{0,1:T(4,128)S(1)}, s32[8,4]{0,1:T(4,128)}, u32[]{:S(2)}) copy-start(s32[8,4]{0,1:T(4,128)} %copy-done.7) | copy-start | bytes 388
  51.9 28.8 %copy-start.9 = (s32[8,4]{0,1:T(4,128)S(1)}, s32[8,4]{0,1:T(4,128)}, u32[]{:S(2)}) copy-start(s32[8,4]{0,1:T(4,128)} %param.10) | copy-start | bytes 388
  51.9 28.8 %copy-start.11 = (s32[8]{0:T(128)S(1)}, s32[8]{0:T(128)}, u32[]{:S(2)}) copy-start(s32[8]{0:T(128)} %copy-done.10) | copy-start | bytes 100
  51.9 28.8 %copy-start.13 = (s32[8]{0:T(128)S(1)}, s32[8]{0:T(128)}, u32[]{:S(2)}) copy-start(s32[8]{0:T(128)} %copy-done.12) | copy-start | bytes 100
  51.9 28.8 %copy-start.14 = (f32[8,4]{0,1:T(4,128)S(1)}, f32[8,4]{0,1:T(4,128)}, u32[]{:S(2)}) copy-start(f32[8,4]{0,1:T(4,128)} %param.11) | copy-start | bytes 388
  51.9 33.9 %copy-start.6 = (pred[32,8]{1,0:T(32,128)(4,1)S(1)}, pred[32,8]{1,0:T(32,128)(4,1)}, u32[]{:S(2)}) copy-start(pred[32,8]{1,0:T(32,128)(4,1)} %copy-done.5) | copy-start | bytes 772
  52.0 2.5 %collective-permute-start.9 = (bf16[64,7168]{1,0:T(8,128)(2,1)S(1)}, bf16[64,7168]{1,0:T(8,128)(2,1)S(1)}, u32[]{:S(2)}, u32[]{:S(2)}) collective-permute-start(bf16[64,7168]{1,0:T(8,128)(2,1)S(1)} %slice.124), channel_id=1, source_target_pairs={{0,1},{1,0},{2,3},{3,2},{4,5},{5,4},{6,7},{7,6},{8,9},{9,8},{10,11... | collective-permute-start | bytes 2752520 | tf_op jit(solution)/shard_map/ppermute | solution.py:44
  56.3 12.6 %collective-permute-start.10 = (bf16[32,7168]{1,0:T(8,128)(2,1)S(1)}, bf16[32,7168]{1,0:T(8,128)(2,1)S(1)}, u32[]{:S(2)}, u32[]{:S(2)}) collective-permute-start(bf16[32,7168]{1,0:T(8,128)(2,1)S(1)} %slice.125), channel_id=1, source_target_pairs={{0,2},{1,3},{2,0},{3,1},{4,6},{5,7},{6,4},{7,5},{8,10},{9,11},{10,... | collective-permute-start | bytes 1376264 | tf_op jit(solution)/shard_map/ppermute | solution.py:44
  69.1 7.2 %collective-permute-start.11 = (bf16[4,7168]{1,0:T(4,128)(2,1)S(1)}, bf16[4,7168]{1,0:T(4,128)(2,1)S(1)}, u32[]{:S(2)}, u32[]{:S(2)}) collective-permute-start(bf16[4,7168]{1,0:T(4,128)(2,1)S(1)} %get-tuple-element.14), channel_id=1, source_target_pairs={{0,4},{1,5},{2,6},{3,7},{4,0},{5,1},{6,2},{7,3},{8,12},{9,13},{10,... | collective-permute-start | bytes 172040 | tf_op jit(solution)/shard_map/ppermute | solution.py:44
  70.0 8.5 %collective-permute-start.12 = (bf16[4,7168]{1,0:T(4,128)(2,1)S(1)}, bf16[4,7168]{1,0:T(4,128)(2,1)S(1)}, u32[]{:S(2)}, u32[]{:S(2)}) collective-permute-start(bf16[4,7168]{1,0:T(4,128)(2,1)S(1)} %get-tuple-element.13), channel_id=1, source_target_pairs={{0,8},{1,9},{2,10},{3,11},{4,12},{5,13},{6,14},{7,15},{8,0},{9,1},... | collective-permute-start | bytes 172040 | tf_op jit(solution)/shard_map/ppermute | solution.py:44
  72.5 8.4 %collective-permute-start.13 = (bf16[4,7168]{1,0:T(4,128)(2,1)S(1)}, bf16[4,7168]{1,0:T(4,128)(2,1)S(1)}, u32[]{:S(2)}, u32[]{:S(2)}) collective-permute-start(bf16[4,7168]{1,0:T(4,128)(2,1)S(1)} %get-tuple-element.12), channel_id=1, source_target_pairs={{0,12},{1,13},{2,14},{3,15},{4,8},{5,9},{6,10},{7,11},{8,4},{9,5},... | collective-permute-start | bytes 172040 | tf_op jit(solution)/shard_map/ppermute | solution.py:44
  72.7 8.4 %collective-permute-start.14 = (bf16[4,7168]{1,0:T(4,128)(2,1)S(1)}, bf16[4,7168]{1,0:T(4,128)(2,1)S(1)}, u32[]{:S(2)}, u32[]{:S(2)}) collective-permute-start(bf16[4,7168]{1,0:T(4,128)(2,1)S(1)} %get-tuple-element.11), channel_id=1, source_target_pairs={{0,16},{1,17},{2,18},{3,19},{4,20},{5,21},{6,22},{7,23},{8,24},{9,... | collective-permute-start | bytes 172040 | tf_op jit(solution)/shard_map/ppermute | solution.py:44
  76.0 7.9 %collective-permute-start.15 = (bf16[4,7168]{1,0:T(4,128)(2,1)S(1)}, bf16[4,7168]{1,0:T(4,128)(2,1)S(1)}, u32[]{:S(2)}, u32[]{:S(2)}) collective-permute-start(bf16[4,7168]{1,0:T(4,128)(2,1)S(1)} %get-tuple-element.10), channel_id=1, source_target_pairs={{0,20},{1,21},{2,22},{3,23},{4,16},{5,17},{6,18},{7,19},{8,28},{9,... | collective-permute-start | bytes 172040 | tf_op jit(solution)/shard_map/ppermute | solution.py:44
  76.4 7.6 %collective-permute-start.16 = (bf16[4,7168]{1,0:T(4,128)(2,1)S(1)}, bf16[4,7168]{1,0:T(4,128)(2,1)S(1)}, u32[]{:S(2)}, u32[]{:S(2)}) collective-permute-start(bf16[4,7168]{1,0:T(4,128)(2,1)S(1)} %get-tuple-element.9), channel_id=1, source_target_pairs={{0,24},{1,25},{2,26},{3,27},{4,28},{5,29},{6,30},{7,31},{8,16},{9,... | collective-permute-start | bytes 172040 | tf_op jit(solution)/shard_map/ppermute | solution.py:44
  78.5 7.0 %collective-permute-start.17 = (bf16[4,7168]{1,0:T(4,128)(2,1)S(1)}, bf16[4,7168]{1,0:T(4,128)(2,1)S(1)}, u32[]{:S(2)}, u32[]{:S(2)}) collective-permute-start(bf16[4,7168]{1,0:T(4,128)(2,1)S(1)} %get-tuple-element.8), channel_id=1, source_target_pairs={{0,28},{1,29},{2,30},{3,31},{4,24},{5,25},{6,26},{7,27},{8,20},{9,... | collective-permute-start | bytes 172040 | tf_op jit(solution)/shard_map/ppermute | solution.py:44

commit v2 on v1

v2 whole, which is shorter than its diff:
```python
import functools

import jax
import jax.numpy as jnp
from jax import lax
from jax.experimental import pallas as pl
from jax.experimental.pallas import tpu as pltpu
from jax.sharding import PartitionSpec as P

BF16, F32, I32 = jnp.bfloat16, jnp.float32, jnp.int32
VMEM = pl.BlockSpec(memory_space=pltpu.VMEM)
SMEM = pl.BlockSpec(memory_space=pltpu.SMEM)
HBM = pl.BlockSpec(memory_space=pltpu.HBM)


def shape(dims, dtype):
    return jax.ShapeDtypeStruct(dims, dtype)


def call(kernel, outs, ins, name, flops=0, moved=0, limit=24, scratch=()):
    return pl.pallas_call(
        kernel,
        out_shape=outs,
        in_specs=ins,
        out_specs=[VMEM] * len(outs),
        scratch_shapes=list(scratch),
        compiler_params=pltpu.CompilerParams(vmem_limit_bytes=limit << 20),
        cost_estimate=pl.CostEstimate(flops=flops, bytes_accessed=moved, transcendentals=0),
        name=name,
    )


def cuts(width, count):
    tiles = width // 128
    edges = [128 * (tiles * i // count) for i in range(count + 1)]
    return list(zip(edges[:-1], edges[1:]))


def route_kernel(cells, ranges, slot_ref, ids_ref, gate_ref, pick_ref, place_ref, cap_ref, rows_ref, *outs):
    top, toks = ids_ref.shape
    slots = place_ref.shape[1]
    total = slots * cells
    cell = lax.broadcasted_iota(I32, (total, slots), 0)
    slot = lax.broadcasted_iota(I32, (total, slots), 1)
    label = jnp.bitwise_xor(cell // cells, slot_ref[0])
    here = slot == label
    place = jnp.broadcast_to(place_ref[...], (total, slots))
    caps = jnp.broadcast_to(cap_ref[...], (total, slots))
    place_c = jnp.sum(jnp.where(here, place, 0), axis=1, keepdims=True)
    cap_c = jnp.sum(jnp.where(here, caps, 0), axis=1, keepdims=True)
    same = place == place_c
    turn_c = jnp.sum(jnp.where(same & (slot < label), 1, 0), axis=1, keepdims=True)
    hosts_c = jnp.sum(jnp.where(same, 1, 0), axis=1, keepdims=True).astype(F32)
    used = jnp.zeros((total, toks), F32)
    weight = jnp.zeros((total, toks), F32)
    for k in range(top):
        pick = pick_ref[k : k + 1, :].astype(F32)
        wanted = pick - hosts_c * jnp.floor((pick + 0.5) / hosts_c)
        chosen = (ids_ref[k : k + 1, :] == place_c) & (wanted.astype(I32) == turn_c)
        used = jnp.where(chosen, 1.0, used)
        weight = jnp.where(chosen, gate_ref[k : k + 1, :], weight)
    earlier = lax.broadcasted_iota(I32, (toks, toks), 0) < lax.broadcasted_iota(I32, (toks, toks), 1)
    rank = jnp.dot(used, earlier.astype(F32), preferred_element_type=F32).astype(I32)
    seat = lax.broadcasted_iota(I32, (total, toks), 0) % cells
    spot = (used > 0.5) & (rank < cap_c) & (rank == seat)
    outs[-1][...] = jnp.where(spot, weight, 0.0)
    pack = spot.astype(F32).astype(BF16)
    high = slots // 2
    block = 2 * cells
    for i, (lo, hi) in enumerate(ranges):
        packed = jnp.dot(pack, rows_ref[:, lo:hi], preferred_element_type=F32)
        for z in range(high):
            outs[i * high + z][...] = packed[z * block : (z + 1) * block].astype(BF16)


def split_kernel(cells, *refs):
    ins, (own_ref, oth_ref) = refs[:-2], refs[-2:]
    vals = [r[...].astype(F32) for r in ins]
    own_ref[...] = jnp.concatenate([v[:cells] for v in vals], axis=0).astype(BF16)
    oth_ref[...] = jnp.concatenate([v[cells:] for v in vals], axis=0).astype(BF16)


def merge_kernel(cells, keep_ref, core_ref, x_ref, y_ref, d_ref, *outs):
    own = keep_ref[...] + core_ref[...].astype(F32) + x_ref[...].astype(F32)
    oth = y_ref[...].astype(F32) + d_ref[...].astype(F32)
    for z, out in enumerate(outs):
        part = slice(z * cells, (z + 1) * cells)
        out[...] = jnp.concatenate([own[part], oth[part]], axis=0).astype(BF16)


def fetch_kernel(count, *refs):
    ins, outs, sem = refs[:count], refs[count : 2 * count], refs[2 * count]
    copies = [pltpu.make_async_copy(a, b, sem.at[i]) for i, (a, b) in enumerate(zip(ins, outs))]
    for c in copies:
        c.start()
    for c in copies:
        c.wait()


def up_kernel(blocks, base, first, last, *refs):
    rows, rest = refs[:blocks], refs[blocks:]
    gate_ref, up_ref, rest = rest[0], rest[1], rest[2:]
    if first:
        old_g = old_u = None
    else:
        old_g, old_u, rest = rest[0], rest[1], rest[2:]
    if last:
        hid_ref, acc_g, acc_u = rest
    else:
        acc_g, acc_u = rest
    width = rows[0].shape[1]
    if first:
        acc_g[...] = jnp.zeros_like(acc_g)
        acc_u[...] = jnp.zeros_like(acc_u)
    else:
        acc_g[...] = old_g[...]
        acc_u[...] = old_u[...]
    step = 512 if width % 512 == 0 else (256 if width % 256 == 0 else 128)

    def body(i, unused):
        at = pl.multiple_of(i * step, step)
        x = jnp.concatenate([r[:, pl.ds(at, step)] for r in rows], axis=0)
        wat = pl.multiple_of(base + i * step, 128)
        acc_g[...] += jnp.dot(x, gate_ref[pl.ds(wat, step), :], preferred_element_type=F32)
        acc_u[...] += jnp.dot(x, up_ref[pl.ds(wat, step), :], preferred_element_type=F32)
        return unused

    lax.fori_loop(0, width // step, body, 0)
    if last:
        g = acc_g[...]
        hid_ref[...] = (g / (1.0 + jnp.exp(-g)) * acc_u[...]).astype(BF16)


def down_kernel(base, width, hid_ref, down_ref, *outs):
    step = 512 if width % 512 == 0 else (256 if width % 256 == 0 else 128)
    rows = outs[0].shape[0]

    def body(i, unused):
        at = pl.multiple_of(i * step, step)
        wat = pl.multiple_of(base + i * step, 128)
        val = jnp.dot(hid_ref[...], down_ref[:, pl.ds(wat, step)], preferred_element_type=F32)
        for b, out in enumerate(outs):
            out[:, pl.ds(at, step)] = val[b * rows : (b + 1) * rows].astype(out.dtype)
        return unused

    lax.fori_loop(0, width // step, body, 0)


def combine_kernel(high, ranges, scale_ref, *refs):
    out_ref = refs[-1]
    toks = scale_ref.shape[0]
    s = scale_ref[...]
    a = s.astype(BF16)
    left = s - a.astype(F32)
    b = left.astype(BF16)
    c = (left - b.astype(F32)).astype(BF16)
    pieces = jnp.concatenate([v.astype(F32) for v in (a, b, c)], axis=0).astype(BF16)
    for i, (lo, hi) in enumerate(ranges):
        rows = jnp.concatenate([r[...].astype(F32) for r in refs[i * high : (i + 1) * high]], axis=0)
        val = jnp.dot(pieces, rows.astype(BF16), preferred_element_type=F32)
        val = val[:toks] + val[toks : 2 * toks] + val[2 * toks :]
        out_ref[:, lo:hi] = val.astype(BF16)


def per_device(n_in, n_out, hidden_in, expert_ids, gate_weights, replica_pick, placement, capacity, w_gate, w_up, w_down):
    toks, width = hidden_in.shape
    top = expert_ids.shape[1]
    slots = placement.shape[0]
    devices = lax.axis_size("node")
    members = devices // slots
    cells = members * max(1, toks * top // (slots * members))
    high = slots // 2
    fw = w_gate.shape[1]
    rows = high * cells
    my_slot = lax.axis_index("node") // members

    def send(value, flip):
        return lax.ppermute(value, "node", [(d, d ^ flip) for d in range(devices)])

    in_cuts, out_cuts = cuts(width, n_in), cuts(width, n_out)
    route = call(
        functools.partial(route_kernel, cells, in_cuts),
        [shape((2 * cells, hi - lo), BF16) for lo, hi in in_cuts for z in range(high)]
        + [shape((slots * cells, toks), F32)],
        [SMEM] + [VMEM] * 6,
        "route",
    )(my_slot.reshape(1).astype(I32), expert_ids.T, gate_weights.T, replica_pick.T, placement[None, :], capacity[None, :], hidden_in)
    scale = route[-1].T
    wg, wu, wd = call(
        functools.partial(fetch_kernel, 3),
        [shape(w.shape, BF16) for w in (w_gate, w_up, w_down)],
        [HBM] * 3,
        "fetch",
        moved=6 * w_gate.size * 2,
        limit=1,
        scratch=[pltpu.SemaphoreType.DMA((3,))],
    )(w_gate, w_up, w_down)
    acc = ()
    z_order = list(range(high - 1, 0, -1))
    for i, (lo, hi) in enumerate(in_cuts):
        base = route[i * high : (i + 1) * high]
        blocks = {z: send(base[z], 2 * members * z) for z in z_order}
        blocks[0] = base[0]
        own, oth = call(
            functools.partial(split_kernel, cells),
            [shape((rows, hi - lo), BF16)] * 2,
            [VMEM] * high,
            "split",
        )(*[blocks[z] for z in range(high)])
        group = [own, send(own, 2), send(oth, members), send(oth, members + 2)]
        group = group + [send(g, 1) for g in group]
        first, last = i == 0, i == n_in - 1
        acc = call(
            functools.partial(up_kernel, 8, lo, first, last),
            ([shape((8 * rows, fw), BF16)] if last else []) + [shape((8 * rows, fw), F32)] * 2,
            [VMEM] * (10 + len(acc)),
            "up",
            flops=4 * 8 * rows * fw * (hi - lo),
        )(*group, wg, wu, *acc)
    hid = acc[0]
    finals = []
    for lo, hi in out_cuts:
        outs = call(
            functools.partial(down_kernel, lo, hi - lo),
            [shape((rows, hi - lo), F32)] * 4 + [shape((rows, hi - lo), BF16)] * 4,
            [VMEM] * 2,
            "down",
            flops=2 * 8 * rows * fw * (hi - lo),
        )(hid, wd)
        keep, give = outs[:4], outs[4:]
        got = [send(give[b], 1) for b in (3, 2, 1, 0)][::-1]
        half = [(keep[b] + got[b].astype(F32)).astype(BF16) for b in (1, 2, 3)]
        dg, yg, xg = send(half[2], members + 2), send(half[1], members), send(half[0], 2)
        done = call(
            functools.partial(merge_kernel, cells),
            [shape((2 * cells, hi - lo), BF16)] * high,
            [VMEM] * 5,
            "merge",
        )(keep[0], got[0], xg, yg, dg)
        back = {z: send(done[z], 2 * members * z) for z in z_order}
        back[0] = done[0]
        finals += [back[z] for z in range(high)]
    (mixed,) = call(
        functools.partial(combine_kernel, high, out_cuts),
        [shape((toks, width), BF16)],
        [VMEM] * (1 + len(finals)),
        "combine",
    )(scale, *finals)
    return mixed


def solution(mesh):
    split = P(("grp", "node"), None)
    placed = (split, split, split, split, P(), P(), P(None, "node"), P(None, "node"), P("node", None))
    body = functools.partial(per_device, 1, 1)
    return jax.shard_map(body, mesh=mesh, in_specs=placed, out_specs=split, check_vma=False)
```

time: 87.3 us -> 75.6 us (0.87)
  matrix products: 11 us -> 0 us
  Pallas kernels: 0 us -> 9.31 us
  starting transfers between devices: 27.5 us -> 19.7 us
  other arithmetic: 6.32 us -> 0.12 us
  local copies, waits for them, and re-layouts: 6.41 us -> 10.4 us
    dot_general x4 -> x0, matrix products: 11 us -> none  [the longest x1 7.09 us: per_device(): out = jnp.dot(hid, w_down, preferred_element_type=f32)]
    unnamed x30 -> x18, local copies, waits for them, and re-layouts: 0.65 us -> 10.4 us
    pallas_call x0 -> x7, Pallas kernels: none -> 9.31 us  [the longest x1 4.07 us: per_device(): call(functools.partial(up_kernel, 8, lo, first, last), ([shape((8 * rows,...]
    ppermute x18 -> x20, starting transfers between devices: 27.5 us -> 19.7 us  [send(): return lax.ppermute(value, 'node', [(d, d ^ flip) for d in range(devices)])]
    reduce_sum x6 -> x0, other arithmetic: 3.62 us -> none  [the longest x1 0.91 us: route(): turn = jnp.sum(same.astype(jnp.int32), axis=1)]
    concatenate x4 -> x0, local copies, waits for them, and re-layouts: 3.49 us -> none  [the longest x2 2.87 us: per_device(): rows = jnp.concatenate([rows, send(rows, flip)], axis=0)]
    slice x4 -> x0, local copies, waits for them, and re-layouts: 1.95 us -> none  [the longest x2 1.64 us: per_device(): out = out[:half] + send(out[half:].astype(bf16), flip).astype(f32)]
    add x1 -> x0, other arithmetic: 1.7 us -> none  [per_device(): out = out[:half] + send(out[half:].astype(bf16), flip).astype(f32)]
  transfers between devices with their start and end apart: 18 -> 20, of which waited for: 9 -> 10; matrix products, arithmetic and copies ran while one was open for 0% -> 0% of each run, Pallas kernels for 0% -> 1%
where the time goes in v2:
time: 75.6 us; the launch traced here: 75.2 us
  waiting for transfers between devices  35.6 us (47%)
  starting transfers between devices  19.7 us (26%)
  local copies, waits for them, and re-layouts  10.4 us (14%)
  Pallas kernels  9.31 us (12%)
    ppermute x20, waiting for transfers between devices, send(): return lax.ppermute(value, 'node', [(d, d ^ flip) for d in range(devices)])  35.6 us
    ppermute x20, starting transfers between devices, send(): return lax.ppermute(value, 'node', [(d, d ^ flip) for d in range(devices)])  19.7 us
    unnamed x18, local copies, waits for them, and re-layouts  10.4 us
    pallas_call x1, Pallas kernels, per_device(): call(functools.partial(up_kernel, 8, lo, first, last), ([shape((8 * rows,...  4.07 us
    pallas_call x1, Pallas kernels, per_device(): call(functools.partial(down_kernel, lo, hi - lo), [shape((rows, hi - lo),...  2.7 us
  transfers between devices with their start and end apart: 20, of which 10 were waited for; matrix products, arithmetic and copies ran while one was open for 0% of the time, Pallas kernels for 1%

profile of v2, /device:TPU:0, one launch (start us, length us, event | category | flops | bytes accessed | tf_op | source)
XLA Modules:
  0.0 75.2 jit_solution(15184874215996636232)
XLA Ops:
  0.0 0.0 copy-start.3
  0.0 0.9 %copy-done.3 = bf16[8,7168]{1,0:T(8,128)(2,1)S(1)} copy-done((bf16[8,7168]{1,0:T(8,128)(2,1)S(1)}, bf16[8,7168]{1,0:T(8,128)(2,1)}, u32[]{:S(2)}) %copy-start.3) | copy-done | bytes 114712
  0.9 0.0 copy-start.4
  0.9 0.7 copy-done.4
  1.6 0.0 copy-start.5
  1.6 0.7 copy-done.5
  2.3 0.0 copy-start.6
  2.3 0.7 copy-done.6
  2.9 0.0 copy-start.7
  2.9 0.7 copy-done.7
  3.6 0.0 copy-start.8
  3.6 0.7 copy-done.8
  4.3 0.5 route.1
  4.8 3.1 %collective-permute-start = (bf16[8,7168]{1,0:T(8,128)(2,1)S(1)}, bf16[8,7168]{1,0:T(8,128)(2,1)S(1)}, u32[]{:S(2)}, u32[]{:S(2)}) collective-permute-start(bf16[8,7168]{1,0:T(8,128)(2,1)S(1)} %get-tuple-element.30), channel_id=1, source_target_pairs={{0,8},{1,9},{2,10},{3,11},{4,12},{5,13},{6,14},{7,15},{8,0},{9,1},... | collective-permute-start | bytes 344072 | tf_op jit(solution)/shard_map/ppermute | solution.py:178
  7.9 2.6 %collective-permute-start.1 = (bf16[8,7168]{1,0:T(8,128)(2,1)S(1)}, bf16[8,7168]{1,0:T(8,128)(2,1)S(1)}, u32[]{:S(2)}, u32[]{:S(2)}) collective-permute-start(bf16[8,7168]{1,0:T(8,128)(2,1)S(1)} %get-tuple-element.31), channel_id=1, source_target_pairs={{0,16},{1,17},{2,18},{3,19},{4,20},{5,21},{6,22},{7,23},{8,24},{9,... | collective-permute-start | bytes 344072 | tf_op jit(solution)/shard_map/ppermute | solution.py:178
  10.5 0.0 collective-permute-start.2
  10.5 0.6 collective-permute-done.refs_1_
  11.1 8.5 %collective-permute-done.1.refs_2_ = bf16[8,7168]{1,0:T(8,128)(2,1)S(1)} collective-permute-done((bf16[8,7168]{1,0:T(8,128)(2,1)S(1)}, bf16[8,7168]{1,0:T(8,128)(2,1)S(1)}, u32[]{:S(2)}, u32[]{:S(2)}) %collective-permute-start.1) | collective-permute-done | bytes 114720 | tf_op jit(solution)/shard_map/ppermute | solution.py:178
  19.6 0.0 collective-permute-done.2.refs_3_
  19.6 0.1 split.1
  19.7 2.5 %collective-permute-start.5 = (bf16[16,7168]{1,0:T(8,128)(2,1)S(1)}, bf16[16,7168]{1,0:T(8,128)(2,1)S(1)}, u32[]{:S(2)}, u32[]{:S(2)}) collective-permute-start(bf16[16,7168]{1,0:T(8,128)(2,1)S(1)} %get-tuple-element.34), channel_id=1, source_target_pairs={{0,6},{1,7},{2,4},{3,5},{4,2},{5,3},{6,0},{7,1},{8,14},{9,15},{10,... | collective-permute-start | bytes 688136 | tf_op jit(solution)/shard_map/ppermute | solution.py:178
  22.3 0.5 collective-permute-start.4
  22.8 0.5 collective-permute-start.3
  23.3 0.0 collective-permute-start.6
  23.3 5.0 %collective-permute-done.5.refs_3_ = bf16[16,7168]{1,0:T(8,128)(2,1)S(1)} collective-permute-done((bf16[16,7168]{1,0:T(8,128)(2,1)S(1)}, bf16[16,7168]{1,0:T(8,128)(2,1)S(1)}, u32[]{:S(2)}, u32[]{:S(2)}) %collective-permute-start.5) | collective-permute-done | bytes 229408 | tf_op jit(solution)/shard_map/ppermute | solution.py:178
  28.4 0.0 collective-permute-start.9
  28.4 2.3 %collective-permute-done.4.refs_2_ = bf16[16,7168]{1,0:T(8,128)(2,1)S(1)} collective-permute-done((bf16[16,7168]{1,0:T(8,128)(2,1)S(1)}, bf16[16,7168]{1,0:T(8,128)(2,1)S(1)}, u32[]{:S(2)}, u32[]{:S(2)}) %collective-permute-start.4) | collective-permute-done | bytes 229408 | tf_op jit(solution)/shard_map/ppermute | solution.py:178
  30.7 0.0 collective-permute-start.8
  30.7 0.1 collective-permute-done.3.refs_1_
  30.8 0.4 collective-permute-start.7
  31.2 0.0 copy-start
  31.2 2.0 %copy-done = bf16[7168,256]{1,0:T(8,128)(2,1)S(1)} copy-done((bf16[7168,256]{1,0:T(8,128)(2,1)S(1)}, bf16[7168,256]{1,0:T(8,128)(2,1)}, u32[]{:S(2)}) %copy-start) | copy-done | bytes 3670040
  33.3 2.0 %copy-done.1 = bf16[7168,256]{1,0:T(8,128)(2,1)S(1)} copy-done((bf16[7168,256]{1,0:T(8,128)(2,1)S(1)}, bf16[7168,256]{1,0:T(8,128)(2,1)}, u32[]{:S(2)}) %copy-start.1) | copy-done | bytes 3670040
  35.3 2.0 %copy-done.2 = bf16[256,7168]{1,0:T(8,128)(2,1)S(1)} copy-done((bf16[256,7168]{1,0:T(8,128)(2,1)S(1)}, bf16[256,7168]{1,0:T(8,128)(2,1)}, u32[]{:S(2)}) %copy-start.2) | copy-done | bytes 3670040
  37.3 0.8 %fetch.1 = (bf16[7168,256]{1,0:T(8,128)(2,1)S(1)}, bf16[7168,256]{1,0:T(8,128)(2,1)S(1)}, bf16[256,7168]{1,0:T(8,128)(2,1)S(1)}) custom-call(bf16[7168,256]{1,0:T(8,128)(2,1)S(1)} %copy-done, bf16[7168,256]{1,0:T(8,128)(2,1)S(1)} %copy-done.1, bf16[256,7168]{1,0:T(8,128)(2,1)S(1)} %copy-done.2), custom_call_target="tpu_custom_call" | custom-call | bytes 22020096 | tf_op jit(solution)/shard_map/fetch/pallas_call | solution.py:189
  38.1 0.0 collective-permute-done.6.refs_4_
  38.1 0.0 collective-permute-done.9.refs_7_
  38.1 0.0 collective-permute-done.8.refs_6_
  38.1 0.0 collective-permute-done.7.refs_5_
  38.1 4.1 %up.1 = (bf16[128,256]{1,0:T(8,128)(2,1)S(1)}, f32[128,256]{1,0:T(8,128)}, f32[128,256]{1,0:T(8,128)}) custom-call(bf16[16,7168]{1,0:T(8,128)(2,1)S(1)} %get-tuple-element.33.refs_0_, bf16[16,7168]{1,0:T(8,128)(2,1)S(1)} %collective-permute-done.3.refs_1_, bf16[16,7168]{1,0:T(8,128)(2,1)S(1)} %collective-permute-done.4.refs_2_, ...), custom_call_target="tpu_custom_call" | custom-call | flops 939524096 | tf_op jit(solution)/shard_map/up/pallas_call | solution.py:213
  42.2 2.7 %down.1 = (f32[16,7168]{1,0:T(8,128)S(1)}, f32[16,7168]{1,0:T(8,128)S(1)}, f32[16,7168]{1,0:T(8,128)S(1)}, f32[16,7168]{1,0:T(8,128)S(1)}, bf16[16,7168]{1,0:T(8...) custom-call(bf16[128,256]{1,0:T(8,128)(2,1)S(1)} %get-tuple-element.37.hid_, ...), custom_call_target="tpu_custom_call" | custom-call | flops 469762048 | tf_op jit(solution)/shard_map/down/pallas_call | solution.py:223
  44.9 0.2 collective-permute-start.11
  45.1 0.4 collective-permute-start.10
  45.5 0.1 collective-permute-start.13
  45.6 0.4 collective-permute-start.15
  46.0 0.5 collective-permute-done.11
  46.5 1.6 %collective-permute-start.12 = (bf16[16,7168]{1,0:T(8,128)(2,1)S(1)}, bf16[16,7168]{1,0:T(8,128)(2,1)S(1)}, u32[]{:S(2)}, u32[]{:S(2)}) collective-permute-start(bf16[16,7168]{1,0:T(8,128)(2,1)S(1)} %add_convert_fusion.2), channel_id=1, source_target_pairs={{0,2},{1,3},{2,0},{3,1},{4,6},{5,7},{6,4},{7,5},{8,10},{9,11},{10,... | collective-permute-start | bytes 688136 | tf_op jit(solution)/shard_map/ppermute | solution.py:178
  48.1 0.0 collective-permute-done.13
  48.1 0.9 %collective-permute-start.14 = (bf16[16,7168]{1,0:T(8,128)(2,1)S(1)}, bf16[16,7168]{1,0:T(8,128)(2,1)S(1)}, u32[]{:S(2)}, u32[]{:S(2)}) collective-permute-start(bf16[16,7168]{1,0:T(8,128)(2,1)S(1)} %add_convert_fusion.1), channel_id=1, source_target_pairs={{0,4},{1,5},{2,6},{3,7},{4,0},{5,1},{6,2},{7,3},{8,12},{9,13},{10,... | collective-permute-start | bytes 688136 | tf_op jit(solution)/shard_map/ppermute | solution.py:178
  49.0 0.0 collective-permute-done.15
  49.1 1.2 %collective-permute-start.16 = (bf16[16,7168]{1,0:T(8,128)(2,1)S(1)}, bf16[16,7168]{1,0:T(8,128)(2,1)S(1)}, u32[]{:S(2)}, u32[]{:S(2)}) collective-permute-start(bf16[16,7168]{1,0:T(8,128)(2,1)S(1)} %add_convert_fusion), channel_id=1, source_target_pairs={{0,6},{1,7},{2,4},{3,5},{4,2},{5,3},{6,0},{7,1},{8,14},{9,15},{10,... | collective-permute-start | bytes 688136 | tf_op jit(solution)/shard_map/ppermute | solution.py:178
  50.3 0.0 collective-permute-done.10.core_ref
  50.3 4.7 %collective-permute-done.12.x_ref = bf16[16,7168]{1,0:T(8,128)(2,1)S(1)} collective-permute-done((bf16[16,7168]{1,0:T(8,128)(2,1)S(1)}, bf16[16,7168]{1,0:T(8,128)(2,1)S(1)}, u32[]{:S(2)}, u32[]{:S(2)}) %collective-permute-start.12) | collective-permute-done | bytes 229408 | tf_op jit(solution)/shard_map/ppermute | solution.py:178
  55.0 5.4 %collective-permute-done.14.y_ref = bf16[16,7168]{1,0:T(8,128)(2,1)S(1)} collective-permute-done((bf16[16,7168]{1,0:T(8,128)(2,1)S(1)}, bf16[16,7168]{1,0:T(8,128)(2,1)S(1)}, u32[]{:S(2)}, u32[]{:S(2)}) %collective-permute-start.14) | collective-permute-done | bytes 229408 | tf_op jit(solution)/shard_map/ppermute | solution.py:178
  60.5 0.0 collective-permute-done.16.d_ref
  60.5 0.2 merge.1
  60.7 2.8 %collective-permute-start.17 = (bf16[8,7168]{1,0:T(8,128)(2,1)S(1)}, bf16[8,7168]{1,0:T(8,128)(2,1)S(1)}, u32[]{:S(2)}, u32[]{:S(2)}) collective-permute-start(bf16[8,7168]{1,0:T(8,128)(2,1)S(1)} %get-tuple-element.48), channel_id=1, source_target_pairs={{0,8},{1,9},{2,10},{3,11},{4,12},{5,13},{6,14},{7,15},{8,0},{9,1},... | collective-permute-start | bytes 344072 | tf_op jit(solution)/shard_map/ppermute | solution.py:178
  63.5 1.1 %collective-permute-start.18 = (bf16[8,7168]{1,0:T(8,128)(2,1)S(1)}, bf16[8,7168]{1,0:T(8,128)(2,1)S(1)}, u32[]{:S(2)}, u32[]{:S(2)}) collective-permute-start(bf16[8,7168]{1,0:T(8,128)(2,1)S(1)} %get-tuple-element.49), channel_id=1, source_target_pairs={{0,16},{1,17},{2,18},{3,19},{4,20},{5,21},{6,22},{7,23},{8,24},{9,... | collective-permute-start | bytes 344072 | tf_op jit(solution)/shard_map/ppermute | solution.py:178
  64.6 1.4 %collective-permute-start.19 = (bf16[8,7168]{1,0:T(8,128)(2,1)S(1)}, bf16[8,7168]{1,0:T(8,128)(2,1)S(1)}, u32[]{:S(2)}, u32[]{:S(2)}) collective-permute-start(bf16[8,7168]{1,0:T(8,128)(2,1)S(1)} %get-tuple-element.50), channel_id=1, source_target_pairs={{0,24},{1,25},{2,26},{3,27},{4,28},{5,29},{6,30},{7,31},{8,16},{9,... | collective-permute-start | bytes 344072 | tf_op jit(solution)/shard_map/ppermute | solution.py:178
  66.0 0.1 copy.10
  66.0 1.4 %collective-permute-done.17.refs_1_ = bf16[8,7168]{1,0:T(8,128)(2,1)S(1)} collective-permute-done((bf16[8,7168]{1,0:T(8,128)(2,1)S(1)}, bf16[8,7168]{1,0:T(8,128)(2,1)S(1)}, u32[]{:S(2)}, u32[]{:S(2)}) %collective-permute-start.17) | collective-permute-done | bytes 114720 | tf_op jit(solution)/shard_map/ppermute | solution.py:178
  67.4 6.9 %collective-permute-done.18.refs_2_ = bf16[8,7168]{1,0:T(8,128)(2,1)S(1)} collective-permute-done((bf16[8,7168]{1,0:T(8,128)(2,1)S(1)}, bf16[8,7168]{1,0:T(8,128)(2,1)S(1)}, u32[]{:S(2)}, u32[]{:S(2)}) %collective-permute-start.18) | collective-permute-done | bytes 114720 | tf_op jit(solution)/shard_map/ppermute | solution.py:178
  74.3 0.0 collective-permute-done.19.refs_3_
  74.3 0.9 %combine.1 = bf16[8,7168]{1,0:T(8,128)(2,1)} custom-call(f32[8,32]{1,0:T(8,128)S(1)} %bitcast.7, bf16[8,7168]{1,0:T(8,128)(2,1)S(1)} %get-tuple-element.47.refs_0_, bf16[8,7168]{1,0:T(8,128)(2,1)S(1)} %collective-permute-done.17.refs_1_, bf16[8,7168]{1,0:T(8,128)(2,1)S(1)} %collective-permute-done.18.refs_2_, bf16[8,7168]{1,0:T(8,128)(2,1)S(1)} %collective-permute-done.19.refs_3_), custom_call_target="tpu_custom_call" | custom-call | tf_op jit(solution)/shard_map/combine/pallas_call | solution.py:243
  (5 shorter events, 0.1 us)
Async XLA Ops:
  0.0 0.9 %copy-start.3 = (bf16[8,7168]{1,0:T(8,128)(2,1)S(1)}, bf16[8,7168]{1,0:T(8,128)(2,1)}, u32[]{:S(2)}) copy-start(bf16[8,7168]{1,0:T(8,128)(2,1)} %rows_ref.1) | copy-start | bytes 344068
  0.9 0.7 copy-start.4
  1.6 0.7 copy-start.5
  2.3 0.7 copy-start.6
  2.9 0.7 copy-start.7
  3.6 0.7 copy-start.8
  4.8 6.2 %collective-permute-start = (bf16[8,7168]{1,0:T(8,128)(2,1)S(1)}, bf16[8,7168]{1,0:T(8,128)(2,1)S(1)}, u32[]{:S(2)}, u32[]{:S(2)}) collective-permute-start(bf16[8,7168]{1,0:T(8,128)(2,1)S(1)} %get-tuple-element.30), channel_id=1, source_target_pairs={{0,8},{1,9},{2,10},{3,11},{4,12},{5,13},{6,14},{7,15},{8,0},{9,1},... | collective-permute-start | bytes 344072 | tf_op jit(solution)/shard_map/ppermute | solution.py:178
  7.9 11.7 %collective-permute-start.1 = (bf16[8,7168]{1,0:T(8,128)(2,1)S(1)}, bf16[8,7168]{1,0:T(8,128)(2,1)S(1)}, u32[]{:S(2)}, u32[]{:S(2)}) collective-permute-start(bf16[8,7168]{1,0:T(8,128)(2,1)S(1)} %get-tuple-element.31), channel_id=1, source_target_pairs={{0,16},{1,17},{2,18},{3,19},{4,20},{5,21},{6,22},{7,23},{8,24},{9,... | collective-permute-start | bytes 344072 | tf_op jit(solution)/shard_map/ppermute | solution.py:178
  10.5 9.1 %collective-permute-start.2 = (bf16[8,7168]{1,0:T(8,128)(2,1)S(1)}, bf16[8,7168]{1,0:T(8,128)(2,1)S(1)}, u32[]{:S(2)}, u32[]{:S(2)}) collective-permute-start(bf16[8,7168]{1,0:T(8,128)(2,1)S(1)} %get-tuple-element.32), channel_id=1, source_target_pairs={{0,24},{1,25},{2,26},{3,27},{4,28},{5,29},{6,30},{7,31},{8,16},{9,... | collective-permute-start | bytes 344072 | tf_op jit(solution)/shard_map/ppermute | solution.py:178
  19.7 8.6 %collective-permute-start.5 = (bf16[16,7168]{1,0:T(8,128)(2,1)S(1)}, bf16[16,7168]{1,0:T(8,128)(2,1)S(1)}, u32[]{:S(2)}, u32[]{:S(2)}) collective-permute-start(bf16[16,7168]{1,0:T(8,128)(2,1)S(1)} %get-tuple-element.34), channel_id=1, source_target_pairs={{0,6},{1,7},{2,4},{3,5},{4,2},{5,3},{6,0},{7,1},{8,14},{9,15},{10,... | collective-permute-start | bytes 688136 | tf_op jit(solution)/shard_map/ppermute | solution.py:178
  22.3 8.4 %collective-permute-start.4 = (bf16[16,7168]{1,0:T(8,128)(2,1)S(1)}, bf16[16,7168]{1,0:T(8,128)(2,1)S(1)}, u32[]{:S(2)}, u32[]{:S(2)}) collective-permute-start(bf16[16,7168]{1,0:T(8,128)(2,1)S(1)} %get-tuple-element.34), channel_id=1, source_target_pairs={{0,4},{1,5},{2,6},{3,7},{4,0},{5,1},{6,2},{7,3},{8,12},{9,13},{10,... | collective-permute-start | bytes 688136 | tf_op jit(solution)/shard_map/ppermute | solution.py:178
  22.8 8.1 %collective-permute-start.3 = (bf16[16,7168]{1,0:T(8,128)(2,1)S(1)}, bf16[16,7168]{1,0:T(8,128)(2,1)S(1)}, u32[]{:S(2)}, u32[]{:S(2)}) collective-permute-start(bf16[16,7168]{1,0:T(8,128)(2,1)S(1)} %get-tuple-element.33.refs_0_), channel_id=1, source_target_pairs={{0,2},{1,3},{2,0},{3,1},{4,6},{5,7},{6,4},{7,5},{8,10},{9,11},{10,... | collective-permute-start | bytes 688136 | tf_op jit(solution)/shard_map/ppermute | solution.py:178
  23.3 14.8 %collective-permute-start.6 = (bf16[16,7168]{1,0:T(8,128)(2,1)S(1)}, bf16[16,7168]{1,0:T(8,128)(2,1)S(1)}, u32[]{:S(2)}, u32[]{:S(2)}) collective-permute-start(bf16[16,7168]{1,0:T(8,128)(2,1)S(1)} %get-tuple-element.33.refs_0_), channel_id=1, source_target_pairs={{0,1},{1,0},{2,3},{3,2},{4,5},{5,4},{6,7},{7,6},{8,9},{9,8},{10,11... | collective-permute-start | bytes 688136 | tf_op jit(solution)/shard_map/ppermute | solution.py:178
  28.4 9.8 %collective-permute-start.9 = (bf16[16,7168]{1,0:T(8,128)(2,1)S(1)}, bf16[16,7168]{1,0:T(8,128)(2,1)S(1)}, u32[]{:S(2)}, u32[]{:S(2)}) collective-permute-start(bf16[16,7168]{1,0:T(8,128)(2,1)S(1)} %collective-permute-done.5.refs_3_), channel_id=1, source_target_pairs={{0,1},{1,0},{2,3},{3,2},{4,5},{5,4},{6,7},{7,6},{8,9},{9,8},{10,11... | collective-permute-start | bytes 688136 | tf_op jit(solution)/shard_map/ppermute | solution.py:178
  30.7 7.4 %collective-permute-start.8 = (bf16[16,7168]{1,0:T(8,128)(2,1)S(1)}, bf16[16,7168]{1,0:T(8,128)(2,1)S(1)}, u32[]{:S(2)}, u32[]{:S(2)}) collective-permute-start(bf16[16,7168]{1,0:T(8,128)(2,1)S(1)} %collective-permute-done.4.refs_2_), channel_id=1, source_target_pairs={{0,1},{1,0},{2,3},{3,2},{4,5},{5,4},{6,7},{7,6},{8,9},{9,8},{10,11... | collective-permute-start | bytes 688136 | tf_op jit(solution)/shard_map/ppermute | solution.py:178
  30.8 7.3 %collective-permute-start.7 = (bf16[16,7168]{1,0:T(8,128)(2,1)S(1)}, bf16[16,7168]{1,0:T(8,128)(2,1)S(1)}, u32[]{:S(2)}, u32[]{:S(2)}) collective-permute-start(bf16[16,7168]{1,0:T(8,128)(2,1)S(1)} %collective-permute-done.3.refs_1_), channel_id=1, source_target_pairs={{0,1},{1,0},{2,3},{3,2},{4,5},{5,4},{6,7},{7,6},{8,9},{9,8},{10,11... | collective-permute-start | bytes 688136 | tf_op jit(solution)/shard_map/ppermute | solution.py:178
  31.2 2.0 %copy-start = (bf16[7168,256]{1,0:T(8,128)(2,1)S(1)}, bf16[7168,256]{1,0:T(8,128)(2,1)}, u32[]{:S(2)}) copy-start(bf16[7168,256]{1,0:T(8,128)(2,1)} %refs_0_.1) | copy-start | bytes 11010052
  33.3 2.0 %copy-start.1 = (bf16[7168,256]{1,0:T(8,128)(2,1)S(1)}, bf16[7168,256]{1,0:T(8,128)(2,1)}, u32[]{:S(2)}) copy-start(bf16[7168,256]{1,0:T(8,128)(2,1)} %refs_1_.1) | copy-start | bytes 11010052
  35.3 2.0 %copy-start.2 = (bf16[256,7168]{1,0:T(8,128)(2,1)S(1)}, bf16[256,7168]{1,0:T(8,128)(2,1)}, u32[]{:S(2)}) copy-start(bf16[256,7168]{1,0:T(8,128)(2,1)} %refs_2_.1) | copy-start | bytes 11010052
  44.9 1.6 %collective-permute-start.11 = (bf16[16,7168]{1,0:T(8,128)(2,1)S(1)}, bf16[16,7168]{1,0:T(8,128)(2,1)S(1)}, u32[]{:S(2)}, u32[]{:S(2)}) collective-permute-start(bf16[16,7168]{1,0:T(8,128)(2,1)S(1)} %get-tuple-element.42), channel_id=1, source_target_pairs={{0,1},{1,0},{2,3},{3,2},{4,5},{5,4},{6,7},{7,6},{8,9},{9,8},{10,11... | collective-permute-start | bytes 688136 | tf_op jit(solution)/shard_map/ppermute | solution.py:178
  45.1 5.2 %collective-permute-start.10 = (bf16[16,7168]{1,0:T(8,128)(2,1)S(1)}, bf16[16,7168]{1,0:T(8,128)(2,1)S(1)}, u32[]{:S(2)}, u32[]{:S(2)}) collective-permute-start(bf16[16,7168]{1,0:T(8,128)(2,1)S(1)} %get-tuple-element.40), channel_id=1, source_target_pairs={{0,1},{1,0},{2,3},{3,2},{4,5},{5,4},{6,7},{7,6},{8,9},{9,8},{10,11... | collective-permute-start | bytes 688136 | tf_op jit(solution)/shard_map/ppermute | solution.py:178
  45.5 2.6 %collective-permute-start.13 = (bf16[16,7168]{1,0:T(8,128)(2,1)S(1)}, bf16[16,7168]{1,0:T(8,128)(2,1)S(1)}, u32[]{:S(2)}, u32[]{:S(2)}) collective-permute-start(bf16[16,7168]{1,0:T(8,128)(2,1)S(1)} %get-tuple-element.44), channel_id=1, source_target_pairs={{0,1},{1,0},{2,3},{3,2},{4,5},{5,4},{6,7},{7,6},{8,9},{9,8},{10,11... | collective-permute-start | bytes 688136 | tf_op jit(solution)/shard_map/ppermute | solution.py:178
  45.6 3.4 %collective-permute-start.15 = (bf16[16,7168]{1,0:T(8,128)(2,1)S(1)}, bf16[16,7168]{1,0:T(8,128)(2,1)S(1)}, u32[]{:S(2)}, u32[]{:S(2)}) collective-permute-start(bf16[16,7168]{1,0:T(8,128)(2,1)S(1)} %get-tuple-element.46), channel_id=1, source_target_pairs={{0,1},{1,0},{2,3},{3,2},{4,5},{5,4},{6,7},{7,6},{8,9},{9,8},{10,11... | collective-permute-start | bytes 688136 | tf_op jit(solution)/shard_map/ppermute | solution.py:178
  46.5 8.5 %collective-permute-start.12 = (bf16[16,7168]{1,0:T(8,128)(2,1)S(1)}, bf16[16,7168]{1,0:T(8,128)(2,1)S(1)}, u32[]{:S(2)}, u32[]{:S(2)}) collective-permute-start(bf16[16,7168]{1,0:T(8,128)(2,1)S(1)} %add_convert_fusion.2), channel_id=1, source_target_pairs={{0,2},{1,3},{2,0},{3,1},{4,6},{5,7},{6,4},{7,5},{8,10},{9,11},{10,... | collective-permute-start | bytes 688136 | tf_op jit(solution)/shard_map/ppermute | solution.py:178
  48.1 12.3 %collective-permute-start.14 = (bf16[16,7168]{1,0:T(8,128)(2,1)S(1)}, bf16[16,7168]{1,0:T(8,128)(2,1)S(1)}, u32[]{:S(2)}, u32[]{:S(2)}) collective-permute-start(bf16[16,7168]{1,0:T(8,128)(2,1)S(1)} %add_convert_fusion.1), channel_id=1, source_target_pairs={{0,4},{1,5},{2,6},{3,7},{4,0},{5,1},{6,2},{7,3},{8,12},{9,13},{10,... | collective-permute-start | bytes 688136 | tf_op jit(solution)/shard_map/ppermute | solution.py:178
  49.1 11.4 %collective-permute-start.16 = (bf16[16,7168]{1,0:T(8,128)(2,1)S(1)}, bf16[16,7168]{1,0:T(8,128)(2,1)S(1)}, u32[]{:S(2)}, u32[]{:S(2)}) collective-permute-start(bf16[16,7168]{1,0:T(8,128)(2,1)S(1)} %add_convert_fusion), channel_id=1, source_target_pairs={{0,6},{1,7},{2,4},{3,5},{4,2},{5,3},{6,0},{7,1},{8,14},{9,15},{10,... | collective-permute-start | bytes 688136 | tf_op jit(solution)/shard_map/ppermute | solution.py:178
  60.7 6.7 %collective-permute-start.17 = (bf16[8,7168]{1,0:T(8,128)(2,1)S(1)}, bf16[8,7168]{1,0:T(8,128)(2,1)S(1)}, u32[]{:S(2)}, u32[]{:S(2)}) collective-permute-start(bf16[8,7168]{1,0:T(8,128)(2,1)S(1)} %get-tuple-element.48), channel_id=1, source_target_pairs={{0,8},{1,9},{2,10},{3,11},{4,12},{5,13},{6,14},{7,15},{8,0},{9,1},... | collective-permute-start | bytes 344072 | tf_op jit(solution)/shard_map/ppermute | solution.py:178
  63.5 10.8 %collective-permute-start.18 = (bf16[8,7168]{1,0:T(8,128)(2,1)S(1)}, bf16[8,7168]{1,0:T(8,128)(2,1)S(1)}, u32[]{:S(2)}, u32[]{:S(2)}) collective-permute-start(bf16[8,7168]{1,0:T(8,128)(2,1)S(1)} %get-tuple-element.49), channel_id=1, source_target_pairs={{0,16},{1,17},{2,18},{3,19},{4,20},{5,21},{6,22},{7,23},{8,24},{9,... | collective-permute-start | bytes 344072 | tf_op jit(solution)/shard_map/ppermute | solution.py:178
  64.6 9.7 %collective-permute-start.19 = (bf16[8,7168]{1,0:T(8,128)(2,1)S(1)}, bf16[8,7168]{1,0:T(8,128)(2,1)S(1)}, u32[]{:S(2)}, u32[]{:S(2)}) collective-permute-start(bf16[8,7168]{1,0:T(8,128)(2,1)S(1)} %get-tuple-element.50), channel_id=1, source_target_pairs={{0,24},{1,25},{2,26},{3,27},{4,28},{5,29},{6,30},{7,31},{8,16},{9,... | collective-permute-start | bytes 344072 | tf_op jit(solution)/shard_map/ppermute | solution.py:178

commit v3 on v2

--- a/solution.py
+++ b/solution.py
@@ -36,7 +36,28 @@
     return list(zip(edges[:-1], edges[1:]))
 
 
-def route_kernel(cells, ranges, slot_ref, ids_ref, gate_ref, pick_ref, place_ref, cap_ref, rows_ref, *outs):
+def sweep(part, base, width, unrolled):
+    step = max(t for t in (1024, 896, 512, 256, 128) if width % t == 0)
+    if unrolled:
+        for at in range(0, width, step):
+            part(at, base + at, step)
+        return
+
+    def body(i, unused):
+        part(pl.multiple_of(i * step, 128), pl.multiple_of(base + i * step, 128), step)
+        return unused
+
+    lax.fori_loop(0, width // step, body, 0)
+
+
+def route_kernel(cells, ranges, slot_ref, *refs):
+    ins, outs, held, sem = refs[:6], refs[6:-7], refs[-7:-1], refs[-1]
+    copies = [pltpu.make_async_copy(a, b, sem.at[i]) for i, (a, b) in enumerate(zip(ins, held))]
+    for c in copies:
+        c.start()
+    for c in copies:
+        c.wait()
+    ids_ref, gate_ref, pick_ref, place_ref, cap_ref, rows_ref = held
     top, toks = ids_ref.shape
     slots = place_ref.shape[1]
     total = slots * cells
@@ -74,7 +95,7 @@
 
 
 def split_kernel(cells, *refs):
-    ins, (own_ref, oth_ref) = refs[:-2], refs[-2:]
+    ins, (own_ref, oth_ref) = refs[:-3], refs[-2:]
     vals = [r[...].astype(F32) for r in ins]
     own_ref[...] = jnp.concatenate([v[:cells] for v in vals], axis=0).astype(BF16)
     oth_ref[...] = jnp.concatenate([v[cells:] for v in vals], axis=0).astype(BF16)
@@ -89,7 +110,7 @@
 
 
 def fetch_kernel(count, *refs):
-    ins, outs, sem = refs[:count], refs[count : 2 * count], refs[2 * count]
+    ins, outs, sem = refs[:count], refs[count + 1 : 2 * count + 1], refs[2 * count + 1]
     copies = [pltpu.make_async_copy(a, b, sem.at[i]) for i, (a, b) in enumerate(zip(ins, outs))]
     for c in copies:
         c.start()
@@ -115,35 +136,27 @@
     else:
         acc_g[...] = old_g[...]
         acc_u[...] = old_u[...]
-    step = 512 if width % 512 == 0 else (256 if width % 256 == 0 else 128)
-
-    def body(i, unused):
-        at = pl.multiple_of(i * step, step)
+
+    def part(at, wat, step):
         x = jnp.concatenate([r[:, pl.ds(at, step)] for r in rows], axis=0)
-        wat = pl.multiple_of(base + i * step, 128)
         acc_g[...] += jnp.dot(x, gate_ref[pl.ds(wat, step), :], preferred_element_type=F32)
         acc_u[...] += jnp.dot(x, up_ref[pl.ds(wat, step), :], preferred_element_type=F32)
-        return unused
-
-    lax.fori_loop(0, width // step, body, 0)
+
+    sweep(part, base, width, blocks * rows[0].shape[0] <= 256)
     if last:
         g = acc_g[...]
         hid_ref[...] = (g / (1.0 + jnp.exp(-g)) * acc_u[...]).astype(BF16)
 
 
 def down_kernel(base, width, hid_ref, down_ref, *outs):
-    step = 512 if width % 512 == 0 else (256 if width % 256 == 0 else 128)
     rows = outs[0].shape[0]
 
-    def body(i, unused):
-        at = pl.multiple_of(i * step, step)
-        wat = pl.multiple_of(base + i * step, 128)
+    def part(at, wat, step):
         val = jnp.dot(hid_ref[...], down_ref[:, pl.ds(wat, step)], preferred_element_type=F32)
         for b, out in enumerate(outs):
             out[:, pl.ds(at, step)] = val[b * rows : (b + 1) * rows].astype(out.dtype)
-        return unused
-
-    lax.fori_loop(0, width // step, body, 0)
+
+    sweep(part, base, width, len(outs) * rows <= 256)
 
 
 def combine_kernel(high, ranges, scale_ref, *refs):
@@ -178,23 +191,26 @@
         return lax.ppermute(value, "node", [(d, d ^ flip) for d in range(devices)])
 
     in_cuts, out_cuts = cuts(width, n_in), cuts(width, n_out)
+    inputs = (expert_ids.T, gate_weights.T, replica_pick.T, placement[None, :], capacity[None, :], hidden_in)
     route = call(
         functools.partial(route_kernel, cells, in_cuts),
         [shape((2 * cells, hi - lo), BF16) for lo, hi in in_cuts for z in range(high)]
         + [shape((slots * cells, toks), F32)],
-        [SMEM] + [VMEM] * 6,
+        [SMEM] + [HBM] * 6,
         "route",
-    )(my_slot.reshape(1).astype(I32), expert_ids.T, gate_weights.T, replica_pick.T, placement[None, :], capacity[None, :], hidden_in)
+        limit=60,
+        scratch=[pltpu.VMEM(a.shape, a.dtype) for a in inputs] + [pltpu.SemaphoreType.DMA((6,))],
+    )(my_slot.reshape(1).astype(I32), *inputs)
     scale = route[-1].T
     wg, wu, wd = call(
         functools.partial(fetch_kernel, 3),
         [shape(w.shape, BF16) for w in (w_gate, w_up, w_down)],
-        [HBM] * 3,
+        [HBM] * 4,
         "fetch",
         moved=6 * w_gate.size * 2,
-        limit=1,
+        limit=40,
         scratch=[pltpu.SemaphoreType.DMA((3,))],
-    )(w_gate, w_up, w_down)
+    )(w_gate, w_up, w_down, route[-1])
     acc = ()
     z_order = list(range(high - 1, 0, -1))
     for i, (lo, hi) in enumerate(in_cuts):
@@ -204,9 +220,9 @@
         own, oth = call(
             functools.partial(split_kernel, cells),
             [shape((rows, hi - lo), BF16)] * 2,
-            [VMEM] * high,
+            [VMEM] * high + [pl.BlockSpec(memory_space=pl.ANY)],
             "split",
-        )(*[blocks[z] for z in range(high)])
+        )(*[blocks[z] for z in range(high)], wd)
         group = [own, send(own, 2), send(oth, members), send(oth, members + 2)]
         group = group + [send(g, 1) for g in group]
         first, last = i == 0, i == n_in - 1
@@ -252,5 +268,5 @@
 def solution(mesh):
     split = P(("grp", "node"), None)
     placed = (split, split, split, split, P(), P(), P(None, "node"), P(None, "node"), P("node", None))
-    body = functools.partial(per_device, 1, 1)
+    body = functools.partial(per_device, 1, 2)
     return jax.shard_map(body, mesh=mesh, in_specs=placed, out_specs=split, check_vma=False)

time: 75.6 us -> 62.4 us (0.83)
  waiting for transfers between devices: 35.6 us -> 19.8 us
  starting transfers between devices: 19.7 us -> 30.7 us
  local copies, waits for them, and re-layouts: 10.4 us -> 0.79 us
  Pallas kernels: 9.31 us -> 10.6 us
    ppermute x20 -> x30, waiting for transfers between devices: 35.6 us -> 19.8 us  [send(): return lax.ppermute(value, 'node', [(d, d ^ flip) for d in range(devices)])]
    ppermute x20 -> x30, starting transfers between devices: 19.7 us -> 30.7 us  [send(): return lax.ppermute(value, 'node', [(d, d ^ flip) for d in range(devices)])]
    unnamed x18 -> x6, local copies, waits for them, and re-layouts: 10.4 us -> 0.72 us
    pallas_call x1, Pallas kernels: 0.76 us -> 4.25 us  [per_device(): call(functools.partial(fetch_kernel, 3), [shape(w.shape, BF16) for w in (...]
    pallas_call x1, Pallas kernels: 4.07 us -> 1.83 us  [per_device(): call(functools.partial(up_kernel, 8, lo, first, last), ([shape((8 * rows,...]
    pallas_call x1 -> x2, Pallas kernels: 2.7 us -> 0.9 us  [per_device(): call(functools.partial(down_kernel, lo, hi - lo), [shape((rows, hi - lo),...]
    pallas_call x1, Pallas kernels: 0.55 us -> 2.34 us  [per_device(): call(functools.partial(route_kernel, cells, in_cuts), [shape((2 * cells,...]
  transfers between devices with their start and end apart: 20 -> 30, of which waited for: 10 -> 13; matrix products, arithmetic and copies ran while one was open for 0% -> 0% of each run, Pallas kernels for 1% -> 8%
where the time goes in v3:
time: 62.4 us; the launch traced here: 62.2 us
  starting transfers between devices  30.7 us (49%)
  waiting for transfers between devices  19.8 us (32%)
  Pallas kernels  10.6 us (17%)
  local copies, waits for them, and re-layouts  0.79 us (1%)
    ppermute x30, starting transfers between devices, send(): return lax.ppermute(value, 'node', [(d, d ^ flip) for d in range(devices)])  30.7 us
    ppermute x30, waiting for transfers between devices, send(): return lax.ppermute(value, 'node', [(d, d ^ flip) for d in range(devices)])  19.8 us
    pallas_call x1, Pallas kernels, per_device(): call(functools.partial(fetch_kernel, 3), [shape(w.shape, BF16) for w in (...  4.25 us
    pallas_call x1, Pallas kernels, per_device(): call(functools.partial(route_kernel, cells, in_cuts), [shape((2 * cells,...  2.34 us
    pallas_call x1, Pallas kernels, per_device(): call(functools.partial(up_kernel, 8, lo, first, last), ([shape((8 * rows,...  1.83 us
  transfers between devices with their start and end apart: 30, of which 13 were waited for; matrix products, arithmetic and copies ran while one was open for 0% of the time, Pallas kernels for 8%

profile of v3, /device:TPU:0, one launch (start us, length us, event | category | flops | bytes accessed | tf_op | source)
XLA Modules:
  0.0 62.2 jit_solution(6373715463969796492)
XLA Ops:
  0.0 2.3 %route.1 = (bf16[8,7168]{1,0:T(8,128)(2,1)}, bf16[8,7168]{1,0:T(8,128)(2,1)}, bf16[8,7168]{1,0:T(8,128)(2,1)}, bf16[8,7168]{1,0:T(8,128)(2,1)}, f32[32,8]{1,0:T(8,128)}) custom-call(s32[1]{0:T(128)} %bitcast.slot_ref, s32[4,8]{1,0:T(4,128)} %bitcast.8, f32[4,8]{1,0:T(4,128)} %bitcast.9, s32[4,8]{1,0:T(4,128)} %bitcast.10, s32[1,8]{1,0:T(1,128)} %bitcast.11, ...), custom_call_target="tpu_custom_call" | custom-call | tf_op jit(solution)/shard_map/route/pallas_call | solution.py:195
  2.4 3.1 %collective-permute-start = (bf16[8,7168]{1,0:T(8,128)(2,1)}, bf16[8,7168]{1,0:T(8,128)(2,1)S(1)}, u32[]{:S(2)}, u32[]{:S(2)}) collective-permute-start(bf16[8,7168]{1,0:T(8,128)(2,1)} %get-tuple-element.42), channel_id=1, source_target_pairs={{0,8},{1,9},{2,10},{3,11},{4,12},{5,13},{6,14},{7,15},{8,0},{9,1},... | collective-permute-start | bytes 344072 | tf_op jit(solution)/shard_map/ppermute | solution.py:191
  5.4 2.6 %collective-permute-start.1 = (bf16[8,7168]{1,0:T(8,128)(2,1)}, bf16[8,7168]{1,0:T(8,128)(2,1)S(1)}, u32[]{:S(2)}, u32[]{:S(2)}) collective-permute-start(bf16[8,7168]{1,0:T(8,128)(2,1)} %get-tuple-element.43), channel_id=1, source_target_pairs={{0,16},{1,17},{2,18},{3,19},{4,20},{5,21},{6,22},{7,23},{8,24},{9,... | collective-permute-start | bytes 344072 | tf_op jit(solution)/shard_map/ppermute | solution.py:191
  8.0 0.7 %copy-done.1 = f32[32,8]{1,0:T(8,128)S(1)} copy-done((f32[32,8]{1,0:T(8,128)S(1)}, f32[32,8]{1,0:T(8,128)}, u32[]{:S(2)}) %copy-start.1) | copy-done | bytes 1048
  8.8 4.3 %fetch.1 = (bf16[7168,256]{1,0:T(8,128)(2,1)S(1)}, bf16[7168,256]{1,0:T(8,128)(2,1)S(1)}, bf16[256,7168]{1,0:T(8,128)(2,1)S(1)}) custom-call(bf16[7168,256]{1,0:T(8,128)(2,1)} %refs_0_.1, bf16[7168,256]{1,0:T(8,128)(2,1)} %refs_1_.1, bf16[256,7168]{1,0:T(8,128)(2,1)} %refs_2_.1, f32[32,8]{1,0:T(8,128)S(1)} %copy-done.1), custom_call_target="tpu_custom_call" | custom-call | bytes 22020096 | tf_op jit(solution)/shard_map/fetch/pallas_call | solution.py:205
  13.0 0.0 collective-permute-done.refs_1_
  13.0 4.3 %collective-permute-done.1.refs_2_ = bf16[8,7168]{1,0:T(8,128)(2,1)S(1)} collective-permute-done((bf16[8,7168]{1,0:T(8,128)(2,1)}, bf16[8,7168]{1,0:T(8,128)(2,1)S(1)}, u32[]{:S(2)}, u32[]{:S(2)}) %collective-permute-start.1) | collective-permute-done | bytes 114720 | tf_op jit(solution)/shard_map/ppermute | solution.py:191
  17.3 0.0 collective-permute-done.2.refs_3_
  17.3 0.1 split.1
  17.5 2.5 %collective-permute-start.5 = (bf16[16,7168]{1,0:T(8,128)(2,1)S(1)}, bf16[16,7168]{1,0:T(8,128)(2,1)S(1)}, u32[]{:S(2)}, u32[]{:S(2)}) collective-permute-start(bf16[16,7168]{1,0:T(8,128)(2,1)S(1)} %get-tuple-element.47), channel_id=1, source_target_pairs={{0,6},{1,7},{2,4},{3,5},{4,2},{5,3},{6,0},{7,1},{8,14},{9,15},{10,... | collective-permute-start | bytes 688136 | tf_op jit(solution)/shard_map/ppermute | solution.py:191
  20.0 0.5 collective-permute-start.4
  20.5 0.5 collective-permute-start.3
  21.1 5.0 %collective-permute-done.5.refs_3_ = bf16[16,7168]{1,0:T(8,128)(2,1)S(1)} collective-permute-done((bf16[16,7168]{1,0:T(8,128)(2,1)S(1)}, bf16[16,7168]{1,0:T(8,128)(2,1)S(1)}, u32[]{:S(2)}, u32[]{:S(2)}) %collective-permute-start.5) | collective-permute-done | bytes 229408 | tf_op jit(solution)/shard_map/ppermute | solution.py:191
  26.1 2.3 %collective-permute-done.4.refs_2_ = bf16[16,7168]{1,0:T(8,128)(2,1)S(1)} collective-permute-done((bf16[16,7168]{1,0:T(8,128)(2,1)S(1)}, bf16[16,7168]{1,0:T(8,128)(2,1)S(1)}, u32[]{:S(2)}, u32[]{:S(2)}) %collective-permute-start.4) | collective-permute-done | bytes 229408 | tf_op jit(solution)/shard_map/ppermute | solution.py:191
  28.5 0.1 collective-permute-done.3.refs_1_
  28.6 0.4 collective-permute-start.7
  29.0 0.0 collective-permute-done.6.refs_4_
  29.0 0.0 collective-permute-done.9.refs_7_
  29.0 1.0 %collective-permute-done.8.refs_6_ = bf16[16,7168]{1,0:T(8,128)(2,1)S(1)} collective-permute-done((bf16[16,7168]{1,0:T(8,128)(2,1)S(1)}, bf16[16,7168]{1,0:T(8,128)(2,1)S(1)}, u32[]{:S(2)}, u32[]{:S(2)}) %collective-permute-start.8) | collective-permute-done | bytes 229408 | tf_op jit(solution)/shard_map/ppermute | solution.py:191
  29.9 0.3 collective-permute-done.7.refs_5_
  30.3 1.8 %up.1 = (bf16[128,256]{1,0:T(8,128)(2,1)S(1)}, f32[128,256]{1,0:T(8,128)}, f32[128,256]{1,0:T(8,128)}) custom-call(bf16[16,7168]{1,0:T(8,128)(2,1)S(1)} %get-tuple-element.46.refs_0_, bf16[16,7168]{1,0:T(8,128)(2,1)S(1)} %collective-permute-done.3.refs_1_, bf16[16,7168]{1,0:T(8,128)(2,1)S(1)} %collective-permute-done.4.refs_2_, ...), custom_call_target="tpu_custom_call" | custom-call | flops 939524096 | tf_op jit(solution)/shard_map/up/pallas_call | solution.py:229
  32.1 0.4 down.3
  32.5 0.2 collective-permute-start.21
  32.8 0.3 collective-permute-start.20
  33.1 0.2 collective-permute-start.23
  33.3 0.3 collective-permute-start.25
  33.6 0.5 down.2
  34.1 0.2 collective-permute-start.10
  34.3 0.0 collective-permute-done.21
  34.3 0.3 collective-permute-start.11
  34.7 0.0 collective-permute-done.23
  34.7 0.2 collective-permute-start.13
  35.0 0.0 collective-permute-done.25
  35.0 0.4 collective-permute-start.15
  35.4 0.2 collective-permute-done.11
  35.7 1.5 %collective-permute-start.22 = (bf16[16,3584]{1,0:T(8,128)(2,1)S(1)}, bf16[16,3584]{1,0:T(8,128)(2,1)S(1)}, u32[]{:S(2)}, u32[]{:S(2)}) collective-permute-start(bf16[16,3584]{1,0:T(8,128)(2,1)S(1)} %add_convert_fusion.2), channel_id=1, source_target_pairs={{0,2},{1,3},{2,0},{3,1},{4,6},{5,7},{6,4},{7,5},{8,10},{9,11},{10,... | collective-permute-start | bytes 344072 | tf_op jit(solution)/shard_map/ppermute | solution.py:191
  37.2 0.9 %collective-permute-start.24 = (bf16[16,3584]{1,0:T(8,128)(2,1)S(1)}, bf16[16,3584]{1,0:T(8,128)(2,1)S(1)}, u32[]{:S(2)}, u32[]{:S(2)}) collective-permute-start(bf16[16,3584]{1,0:T(8,128)(2,1)S(1)} %add_convert_fusion.1), channel_id=1, source_target_pairs={{0,4},{1,5},{2,6},{3,7},{4,0},{5,1},{6,2},{7,3},{8,12},{9,13},{10,... | collective-permute-start | bytes 344072 | tf_op jit(solution)/shard_map/ppermute | solution.py:191
  38.1 0.0 collective-permute-done.15
  38.1 1.2 %collective-permute-start.26 = (bf16[16,3584]{1,0:T(8,128)(2,1)S(1)}, bf16[16,3584]{1,0:T(8,128)(2,1)S(1)}, u32[]{:S(2)}, u32[]{:S(2)}) collective-permute-start(bf16[16,3584]{1,0:T(8,128)(2,1)S(1)} %add_convert_fusion), channel_id=1, source_target_pairs={{0,6},{1,7},{2,4},{3,5},{4,2},{5,3},{6,0},{7,1},{8,14},{9,15},{10,... | collective-permute-start | bytes 344072 | tf_op jit(solution)/shard_map/ppermute | solution.py:191
  39.4 1.6 %collective-permute-start.12 = (bf16[16,3584]{1,0:T(8,128)(2,1)S(1)}, bf16[16,3584]{1,0:T(8,128)(2,1)S(1)}, u32[]{:S(2)}, u32[]{:S(2)}) collective-permute-start(bf16[16,3584]{1,0:T(8,128)(2,1)S(1)} %add_convert_fusion.5), channel_id=1, source_target_pairs={{0,2},{1,3},{2,0},{3,1},{4,6},{5,7},{6,4},{7,5},{8,10},{9,11},{10,... | collective-permute-start | bytes 344072 | tf_op jit(solution)/shard_map/ppermute | solution.py:191
  40.9 0.1 collective-permute-done.22.x_ref
  41.1 2.0 %collective-permute-start.14 = (bf16[16,3584]{1,0:T(8,128)(2,1)S(1)}, bf16[16,3584]{1,0:T(8,128)(2,1)S(1)}, u32[]{:S(2)}, u32[]{:S(2)}) collective-permute-start(bf16[16,3584]{1,0:T(8,128)(2,1)S(1)} %add_convert_fusion.4), channel_id=1, source_target_pairs={{0,4},{1,5},{2,6},{3,7},{4,0},{5,1},{6,2},{7,3},{8,12},{9,13},{10,... | collective-permute-start | bytes 344072 | tf_op jit(solution)/shard_map/ppermute | solution.py:191
  43.1 1.7 %collective-permute-done.24.y_ref = bf16[16,3584]{1,0:T(8,128)(2,1)S(1)} collective-permute-done((bf16[16,3584]{1,0:T(8,128)(2,1)S(1)}, bf16[16,3584]{1,0:T(8,128)(2,1)S(1)}, u32[]{:S(2)}, u32[]{:S(2)}) %collective-permute-start.24) | collective-permute-done | bytes 114720 | tf_op jit(solution)/shard_map/ppermute | solution.py:191
  44.8 1.7 %collective-permute-start.16 = (bf16[16,3584]{1,0:T(8,128)(2,1)S(1)}, bf16[16,3584]{1,0:T(8,128)(2,1)S(1)}, u32[]{:S(2)}, u32[]{:S(2)}) collective-permute-start(bf16[16,3584]{1,0:T(8,128)(2,1)S(1)} %add_convert_fusion.3), channel_id=1, source_target_pairs={{0,6},{1,7},{2,4},{3,5},{4,2},{5,3},{6,0},{7,1},{8,14},{9,15},{10,... | collective-permute-start | bytes 344072 | tf_op jit(solution)/shard_map/ppermute | solution.py:191
  46.6 0.0 collective-permute-done.26.d_ref
  46.6 0.1 merge.3
  46.7 2.8 %collective-permute-start.27 = (bf16[8,3584]{1,0:T(8,128)(2,1)S(1)}, bf16[8,3584]{1,0:T(8,128)(2,1)S(1)}, u32[]{:S(2)}, u32[]{:S(2)}) collective-permute-start(bf16[8,3584]{1,0:T(8,128)(2,1)S(1)} %get-tuple-element.72), channel_id=1, source_target_pairs={{0,8},{1,9},{2,10},{3,11},{4,12},{5,13},{6,14},{7,15},{8,0},{9,1},... | collective-permute-start | bytes 172040 | tf_op jit(solution)/shard_map/ppermute | solution.py:191
  49.5 0.0 collective-permute-done.10.core_ref
  49.5 1.1 %collective-permute-start.28 = (bf16[8,3584]{1,0:T(8,128)(2,1)S(1)}, bf16[8,3584]{1,0:T(8,128)(2,1)S(1)}, u32[]{:S(2)}, u32[]{:S(2)}) collective-permute-start(bf16[8,3584]{1,0:T(8,128)(2,1)S(1)} %get-tuple-element.73), channel_id=1, source_target_pairs={{0,16},{1,17},{2,18},{3,19},{4,20},{5,21},{6,22},{7,23},{8,24},{9,... | collective-permute-start | bytes 172040 | tf_op jit(solution)/shard_map/ppermute | solution.py:191
  50.6 0.0 collective-permute-done.12.x_ref
  50.6 1.4 %collective-permute-start.29 = (bf16[8,3584]{1,0:T(8,128)(2,1)S(1)}, bf16[8,3584]{1,0:T(8,128)(2,1)S(1)}, u32[]{:S(2)}, u32[]{:S(2)}) collective-permute-start(bf16[8,3584]{1,0:T(8,128)(2,1)S(1)} %get-tuple-element.74), channel_id=1, source_target_pairs={{0,24},{1,25},{2,26},{3,27},{4,28},{5,29},{6,30},{7,31},{8,16},{9,... | collective-permute-start | bytes 172040 | tf_op jit(solution)/shard_map/ppermute | solution.py:191
  52.0 0.0 collective-permute-done.14.y_ref
  52.0 0.0 collective-permute-done.16.d_ref
  52.1 0.1 merge.2
  52.1 1.3 %collective-permute-start.17 = (bf16[8,3584]{1,0:T(8,128)(2,1)S(1)}, bf16[8,3584]{1,0:T(8,128)(2,1)S(1)}, u32[]{:S(2)}, u32[]{:S(2)}) collective-permute-start(bf16[8,3584]{1,0:T(8,128)(2,1)S(1)} %get-tuple-element.60), channel_id=1, source_target_pairs={{0,8},{1,9},{2,10},{3,11},{4,12},{5,13},{6,14},{7,15},{8,0},{9,1},... | collective-permute-start | bytes 172040 | tf_op jit(solution)/shard_map/ppermute | solution.py:191
  53.5 1.7 %collective-permute-start.18 = (bf16[8,3584]{1,0:T(8,128)(2,1)S(1)}, bf16[8,3584]{1,0:T(8,128)(2,1)S(1)}, u32[]{:S(2)}, u32[]{:S(2)}) collective-permute-start(bf16[8,3584]{1,0:T(8,128)(2,1)S(1)} %get-tuple-element.61), channel_id=1, source_target_pairs={{0,16},{1,17},{2,18},{3,19},{4,20},{5,21},{6,22},{7,23},{8,24},{9,... | collective-permute-start | bytes 172040 | tf_op jit(solution)/shard_map/ppermute | solution.py:191
  55.2 0.0 collective-permute-done.27.refs_5_
  55.2 1.4 %collective-permute-start.19 = (bf16[8,3584]{1,0:T(8,128)(2,1)S(1)}, bf16[8,3584]{1,0:T(8,128)(2,1)S(1)}, u32[]{:S(2)}, u32[]{:S(2)}) collective-permute-start(bf16[8,3584]{1,0:T(8,128)(2,1)S(1)} %get-tuple-element.62), channel_id=1, source_target_pairs={{0,24},{1,25},{2,26},{3,27},{4,28},{5,29},{6,30},{7,31},{8,16},{9,... | collective-permute-start | bytes 172040 | tf_op jit(solution)/shard_map/ppermute | solution.py:191
  56.6 0.1 copy.10
  56.7 0.8 %collective-permute-done.28.refs_6_ = bf16[8,3584]{1,0:T(8,128)(2,1)S(1)} collective-permute-done((bf16[8,3584]{1,0:T(8,128)(2,1)S(1)}, bf16[8,3584]{1,0:T(8,128)(2,1)S(1)}, u32[]{:S(2)}, u32[]{:S(2)}) %collective-permute-start.28) | collective-permute-done | bytes 57376 | tf_op jit(solution)/shard_map/ppermute | solution.py:191
  57.4 0.6 collective-permute-done.17.refs_1_
  58.0 2.1 %collective-permute-done.18.refs_2_ = bf16[8,3584]{1,0:T(8,128)(2,1)S(1)} collective-permute-done((bf16[8,3584]{1,0:T(8,128)(2,1)S(1)}, bf16[8,3584]{1,0:T(8,128)(2,1)S(1)}, u32[]{:S(2)}, u32[]{:S(2)}) %collective-permute-start.18) | collective-permute-done | bytes 57376 | tf_op jit(solution)/shard_map/ppermute | solution.py:191
  60.1 1.1 %collective-permute-done.19.refs_3_ = bf16[8,3584]{1,0:T(8,128)(2,1)S(1)} collective-permute-done((bf16[8,3584]{1,0:T(8,128)(2,1)S(1)}, bf16[8,3584]{1,0:T(8,128)(2,1)S(1)}, u32[]{:S(2)}, u32[]{:S(2)}) %collective-permute-start.19) | collective-permute-done | bytes 57376 | tf_op jit(solution)/shard_map/ppermute | solution.py:191
  61.2 0.9 %combine.1 = bf16[8,7168]{1,0:T(8,128)(2,1)} custom-call(f32[8,32]{1,0:T(8,128)S(1)} %bitcast.7, bf16[8,3584]{1,0:T(8,128)(2,1)S(1)} %get-tuple-element.59.refs_0_, bf16[8,3584]{1,0:T(8,128)(2,1)S(1)} %collective-permute-done.17.refs_1_, bf16[8,3584]{1,0:T(8,128)(2,1)S(1)} %collective-permute-done.18.refs_2_, ...), custom_call_target="tpu_custom_call" | custom-call | tf_op jit(solution)/shard_map/combine/pallas_call | solution.py:259
  (18 shorter events, 0.2 us)
Async XLA Ops:
  2.4 10.7 %collective-permute-start = (bf16[8,7168]{1,0:T(8,128)(2,1)}, bf16[8,7168]{1,0:T(8,128)(2,1)S(1)}, u32[]{:S(2)}, u32[]{:S(2)}) collective-permute-start(bf16[8,7168]{1,0:T(8,128)(2,1)} %get-tuple-element.42), channel_id=1, source_target_pairs={{0,8},{1,9},{2,10},{3,11},{4,12},{5,13},{6,14},{7,15},{8,0},{9,1},... | collective-permute-start | bytes 344072 | tf_op jit(solution)/shard_map/ppermute | solution.py:191
  5.4 11.9 %collective-permute-start.1 = (bf16[8,7168]{1,0:T(8,128)(2,1)}, bf16[8,7168]{1,0:T(8,128)(2,1)S(1)}, u32[]{:S(2)}, u32[]{:S(2)}) collective-permute-start(bf16[8,7168]{1,0:T(8,128)(2,1)} %get-tuple-element.43), channel_id=1, source_target_pairs={{0,16},{1,17},{2,18},{3,19},{4,20},{5,21},{6,22},{7,23},{8,24},{9,... | collective-permute-start | bytes 344072 | tf_op jit(solution)/shard_map/ppermute | solution.py:191
  8.0 9.3 %collective-permute-start.2 = (bf16[8,7168]{1,0:T(8,128)(2,1)}, bf16[8,7168]{1,0:T(8,128)(2,1)S(1)}, u32[]{:S(2)}, u32[]{:S(2)}) collective-permute-start(bf16[8,7168]{1,0:T(8,128)(2,1)} %get-tuple-element.44), channel_id=1, source_target_pairs={{0,24},{1,25},{2,26},{3,27},{4,28},{5,29},{6,30},{7,31},{8,16},{9,... | collective-permute-start | bytes 344072 | tf_op jit(solution)/shard_map/ppermute | solution.py:191
  8.0 0.7 %copy-start.1 = (f32[32,8]{1,0:T(8,128)S(1)}, f32[32,8]{1,0:T(8,128)}, u32[]{:S(2)}) copy-start(f32[32,8]{1,0:T(8,128)} %get-tuple-element.40.refs_3_) | copy-start | bytes 3076
  8.7 8.6 %copy-start = (bf16[8,7168]{1,0:T(8,128)(2,1)S(1)}, bf16[8,7168]{1,0:T(8,128)(2,1)}, u32[]{:S(2)}) copy-start(bf16[8,7168]{1,0:T(8,128)(2,1)} %get-tuple-element.41.refs_0_) | copy-start | bytes 344068
  17.5 8.6 %collective-permute-start.5 = (bf16[16,7168]{1,0:T(8,128)(2,1)S(1)}, bf16[16,7168]{1,0:T(8,128)(2,1)S(1)}, u32[]{:S(2)}, u32[]{:S(2)}) collective-permute-start(bf16[16,7168]{1,0:T(8,128)(2,1)S(1)} %get-tuple-element.47), channel_id=1, source_target_pairs={{0,6},{1,7},{2,4},{3,5},{4,2},{5,3},{6,0},{7,1},{8,14},{9,15},{10,... | collective-permute-start | bytes 688136 | tf_op jit(solution)/shard_map/ppermute | solution.py:191
  20.0 8.4 %collective-permute-start.4 = (bf16[16,7168]{1,0:T(8,128)(2,1)S(1)}, bf16[16,7168]{1,0:T(8,128)(2,1)S(1)}, u32[]{:S(2)}, u32[]{:S(2)}) collective-permute-start(bf16[16,7168]{1,0:T(8,128)(2,1)S(1)} %get-tuple-element.47), channel_id=1, source_target_pairs={{0,4},{1,5},{2,6},{3,7},{4,0},{5,1},{6,2},{7,3},{8,12},{9,13},{10,... | collective-permute-start | bytes 688136 | tf_op jit(solution)/shard_map/ppermute | solution.py:191
  20.5 8.1 %collective-permute-start.3 = (bf16[16,7168]{1,0:T(8,128)(2,1)S(1)}, bf16[16,7168]{1,0:T(8,128)(2,1)S(1)}, u32[]{:S(2)}, u32[]{:S(2)}) collective-permute-start(bf16[16,7168]{1,0:T(8,128)(2,1)S(1)} %get-tuple-element.46.refs_0_), channel_id=1, source_target_pairs={{0,2},{1,3},{2,0},{3,1},{4,6},{5,7},{6,4},{7,5},{8,10},{9,11},{10,... | collective-permute-start | bytes 688136 | tf_op jit(solution)/shard_map/ppermute | solution.py:191
  21.1 7.9 %collective-permute-start.6 = (bf16[16,7168]{1,0:T(8,128)(2,1)S(1)}, bf16[16,7168]{1,0:T(8,128)(2,1)S(1)}, u32[]{:S(2)}, u32[]{:S(2)}) collective-permute-start(bf16[16,7168]{1,0:T(8,128)(2,1)S(1)} %get-tuple-element.46.refs_0_), channel_id=1, source_target_pairs={{0,1},{1,0},{2,3},{3,2},{4,5},{5,4},{6,7},{7,6},{8,9},{9,8},{10,11... | collective-permute-start | bytes 688136 | tf_op jit(solution)/shard_map/ppermute | solution.py:191
  26.1 2.9 %collective-permute-start.9 = (bf16[16,7168]{1,0:T(8,128)(2,1)S(1)}, bf16[16,7168]{1,0:T(8,128)(2,1)S(1)}, u32[]{:S(2)}, u32[]{:S(2)}) collective-permute-start(bf16[16,7168]{1,0:T(8,128)(2,1)S(1)} %collective-permute-done.5.refs_3_), channel_id=1, source_target_pairs={{0,1},{1,0},{2,3},{3,2},{4,5},{5,4},{6,7},{7,6},{8,9},{9,8},{10,11... | collective-permute-start | bytes 688136 | tf_op jit(solution)/shard_map/ppermute | solution.py:191
  28.4 1.5 %collective-permute-start.8 = (bf16[16,7168]{1,0:T(8,128)(2,1)S(1)}, bf16[16,7168]{1,0:T(8,128)(2,1)S(1)}, u32[]{:S(2)}, u32[]{:S(2)}) collective-permute-start(bf16[16,7168]{1,0:T(8,128)(2,1)S(1)} %collective-permute-done.4.refs_2_), channel_id=1, source_target_pairs={{0,1},{1,0},{2,3},{3,2},{4,5},{5,4},{6,7},{7,6},{8,9},{9,8},{10,11... | collective-permute-start | bytes 688136 | tf_op jit(solution)/shard_map/ppermute | solution.py:191
  28.6 1.7 %collective-permute-start.7 = (bf16[16,7168]{1,0:T(8,128)(2,1)S(1)}, bf16[16,7168]{1,0:T(8,128)(2,1)S(1)}, u32[]{:S(2)}, u32[]{:S(2)}) collective-permute-start(bf16[16,7168]{1,0:T(8,128)(2,1)S(1)} %collective-permute-done.3.refs_1_), channel_id=1, source_target_pairs={{0,1},{1,0},{2,3},{3,2},{4,5},{5,4},{6,7},{7,6},{8,9},{9,8},{10,11... | collective-permute-start | bytes 688136 | tf_op jit(solution)/shard_map/ppermute | solution.py:191
  32.5 1.8 %collective-permute-start.21 = (bf16[16,3584]{1,0:T(8,128)(2,1)S(1)}, bf16[16,3584]{1,0:T(8,128)(2,1)S(1)}, u32[]{:S(2)}, u32[]{:S(2)}) collective-permute-start(bf16[16,3584]{1,0:T(8,128)(2,1)S(1)} %get-tuple-element.66), channel_id=1, source_target_pairs={{0,1},{1,0},{2,3},{3,2},{4,5},{5,4},{6,7},{7,6},{8,9},{9,8},{10,11... | collective-permute-start | bytes 344072 | tf_op jit(solution)/shard_map/ppermute | solution.py:191
  32.8 6.6 %collective-permute-start.20 = (bf16[16,3584]{1,0:T(8,128)(2,1)S(1)}, bf16[16,3584]{1,0:T(8,128)(2,1)S(1)}, u32[]{:S(2)}, u32[]{:S(2)}) collective-permute-start(bf16[16,3584]{1,0:T(8,128)(2,1)S(1)} %get-tuple-element.64), channel_id=1, source_target_pairs={{0,1},{1,0},{2,3},{3,2},{4,5},{5,4},{6,7},{7,6},{8,9},{9,8},{10,11... | collective-permute-start | bytes 344072 | tf_op jit(solution)/shard_map/ppermute | solution.py:191
  33.1 1.6 %collective-permute-start.23 = (bf16[16,3584]{1,0:T(8,128)(2,1)S(1)}, bf16[16,3584]{1,0:T(8,128)(2,1)S(1)}, u32[]{:S(2)}, u32[]{:S(2)}) collective-permute-start(bf16[16,3584]{1,0:T(8,128)(2,1)S(1)} %get-tuple-element.68), channel_id=1, source_target_pairs={{0,1},{1,0},{2,3},{3,2},{4,5},{5,4},{6,7},{7,6},{8,9},{9,8},{10,11... | collective-permute-start | bytes 344072 | tf_op jit(solution)/shard_map/ppermute | solution.py:191
  33.3 23.3 %copy-start.2 = (f32[32,8]{1,0:T(8,128)S(1)}, f32[32,8]{1,0:T(8,128)}, u32[]{:S(2)}) copy-start(f32[32,8]{1,0:T(8,128)} %get-tuple-element.40.refs_3_) | copy-start | bytes 3076
  33.3 1.7 %collective-permute-start.25 = (bf16[16,3584]{1,0:T(8,128)(2,1)S(1)}, bf16[16,3584]{1,0:T(8,128)(2,1)S(1)}, u32[]{:S(2)}, u32[]{:S(2)}) collective-permute-start(bf16[16,3584]{1,0:T(8,128)(2,1)S(1)} %get-tuple-element.70), channel_id=1, source_target_pairs={{0,1},{1,0},{2,3},{3,2},{4,5},{5,4},{6,7},{7,6},{8,9},{9,8},{10,11... | collective-permute-start | bytes 344072 | tf_op jit(solution)/shard_map/ppermute | solution.py:191
  34.1 15.4 %collective-permute-start.10 = (bf16[16,3584]{1,0:T(8,128)(2,1)S(1)}, bf16[16,3584]{1,0:T(8,128)(2,1)S(1)}, u32[]{:S(2)}, u32[]{:S(2)}) collective-permute-start(bf16[16,3584]{1,0:T(8,128)(2,1)S(1)} %get-tuple-element.52), channel_id=1, source_target_pairs={{0,1},{1,0},{2,3},{3,2},{4,5},{5,4},{6,7},{7,6},{8,9},{9,8},{10,11... | collective-permute-start | bytes 344072 | tf_op jit(solution)/shard_map/ppermute | solution.py:191
  34.3 1.3 %collective-permute-start.11 = (bf16[16,3584]{1,0:T(8,128)(2,1)S(1)}, bf16[16,3584]{1,0:T(8,128)(2,1)S(1)}, u32[]{:S(2)}, u32[]{:S(2)}) collective-permute-start(bf16[16,3584]{1,0:T(8,128)(2,1)S(1)} %get-tuple-element.54), channel_id=1, source_target_pairs={{0,1},{1,0},{2,3},{3,2},{4,5},{5,4},{6,7},{7,6},{8,9},{9,8},{10,11... | collective-permute-start | bytes 344072 | tf_op jit(solution)/shard_map/ppermute | solution.py:191
  34.7 2.5 %collective-permute-start.13 = (bf16[16,3584]{1,0:T(8,128)(2,1)S(1)}, bf16[16,3584]{1,0:T(8,128)(2,1)S(1)}, u32[]{:S(2)}, u32[]{:S(2)}) collective-permute-start(bf16[16,3584]{1,0:T(8,128)(2,1)S(1)} %get-tuple-element.56), channel_id=1, source_target_pairs={{0,1},{1,0},{2,3},{3,2},{4,5},{5,4},{6,7},{7,6},{8,9},{9,8},{10,11... | collective-permute-start | bytes 344072 | tf_op jit(solution)/shard_map/ppermute | solution.py:191
  35.0 3.1 %collective-permute-start.15 = (bf16[16,3584]{1,0:T(8,128)(2,1)S(1)}, bf16[16,3584]{1,0:T(8,128)(2,1)S(1)}, u32[]{:S(2)}, u32[]{:S(2)}) collective-permute-start(bf16[16,3584]{1,0:T(8,128)(2,1)S(1)} %get-tuple-element.58), channel_id=1, source_target_pairs={{0,1},{1,0},{2,3},{3,2},{4,5},{5,4},{6,7},{7,6},{8,9},{9,8},{10,11... | collective-permute-start | bytes 344072 | tf_op jit(solution)/shard_map/ppermute | solution.py:191
  35.7 5.4 %collective-permute-start.22 = (bf16[16,3584]{1,0:T(8,128)(2,1)S(1)}, bf16[16,3584]{1,0:T(8,128)(2,1)S(1)}, u32[]{:S(2)}, u32[]{:S(2)}) collective-permute-start(bf16[16,3584]{1,0:T(8,128)(2,1)S(1)} %add_convert_fusion.2), channel_id=1, source_target_pairs={{0,2},{1,3},{2,0},{3,1},{4,6},{5,7},{6,4},{7,5},{8,10},{9,11},{10,... | collective-permute-start | bytes 344072 | tf_op jit(solution)/shard_map/ppermute | solution.py:191
  37.2 7.6 %collective-permute-start.24 = (bf16[16,3584]{1,0:T(8,128)(2,1)S(1)}, bf16[16,3584]{1,0:T(8,128)(2,1)S(1)}, u32[]{:S(2)}, u32[]{:S(2)}) collective-permute-start(bf16[16,3584]{1,0:T(8,128)(2,1)S(1)} %add_convert_fusion.1), channel_id=1, source_target_pairs={{0,4},{1,5},{2,6},{3,7},{4,0},{5,1},{6,2},{7,3},{8,12},{9,13},{10,... | collective-permute-start | bytes 344072 | tf_op jit(solution)/shard_map/ppermute | solution.py:191
  38.1 8.4 %collective-permute-start.26 = (bf16[16,3584]{1,0:T(8,128)(2,1)S(1)}, bf16[16,3584]{1,0:T(8,128)(2,1)S(1)}, u32[]{:S(2)}, u32[]{:S(2)}) collective-permute-start(bf16[16,3584]{1,0:T(8,128)(2,1)S(1)} %add_convert_fusion), channel_id=1, source_target_pairs={{0,6},{1,7},{2,4},{3,5},{4,2},{5,3},{6,0},{7,1},{8,14},{9,15},{10,... | collective-permute-start | bytes 344072 | tf_op jit(solution)/shard_map/ppermute | solution.py:191
  39.4 11.2 %collective-permute-start.12 = (bf16[16,3584]{1,0:T(8,128)(2,1)S(1)}, bf16[16,3584]{1,0:T(8,128)(2,1)S(1)}, u32[]{:S(2)}, u32[]{:S(2)}) collective-permute-start(bf16[16,3584]{1,0:T(8,128)(2,1)S(1)} %add_convert_fusion.5), channel_id=1, source_target_pairs={{0,2},{1,3},{2,0},{3,1},{4,6},{5,7},{6,4},{7,5},{8,10},{9,11},{10,... | collective-permute-start | bytes 344072 | tf_op jit(solution)/shard_map/ppermute | solution.py:191
  41.1 11.0 %collective-permute-start.14 = (bf16[16,3584]{1,0:T(8,128)(2,1)S(1)}, bf16[16,3584]{1,0:T(8,128)(2,1)S(1)}, u32[]{:S(2)}, u32[]{:S(2)}) collective-permute-start(bf16[16,3584]{1,0:T(8,128)(2,1)S(1)} %add_convert_fusion.4), channel_id=1, source_target_pairs={{0,4},{1,5},{2,6},{3,7},{4,0},{5,1},{6,2},{7,3},{8,12},{9,13},{10,... | collective-permute-start | bytes 344072 | tf_op jit(solution)/shard_map/ppermute | solution.py:191
  44.8 7.2 %collective-permute-start.16 = (bf16[16,3584]{1,0:T(8,128)(2,1)S(1)}, bf16[16,3584]{1,0:T(8,128)(2,1)S(1)}, u32[]{:S(2)}, u32[]{:S(2)}) collective-permute-start(bf16[16,3584]{1,0:T(8,128)(2,1)S(1)} %add_convert_fusion.3), channel_id=1, source_target_pairs={{0,6},{1,7},{2,4},{3,5},{4,2},{5,3},{6,0},{7,1},{8,14},{9,15},{10,... | collective-permute-start | bytes 344072 | tf_op jit(solution)/shard_map/ppermute | solution.py:191
  46.7 8.5 %collective-permute-start.27 = (bf16[8,3584]{1,0:T(8,128)(2,1)S(1)}, bf16[8,3584]{1,0:T(8,128)(2,1)S(1)}, u32[]{:S(2)}, u32[]{:S(2)}) collective-permute-start(bf16[8,3584]{1,0:T(8,128)(2,1)S(1)} %get-tuple-element.72), channel_id=1, source_target_pairs={{0,8},{1,9},{2,10},{3,11},{4,12},{5,13},{6,14},{7,15},{8,0},{9,1},... | collective-permute-start | bytes 172040 | tf_op jit(solution)/shard_map/ppermute | solution.py:191
  49.5 8.0 %collective-permute-start.28 = (bf16[8,3584]{1,0:T(8,128)(2,1)S(1)}, bf16[8,3584]{1,0:T(8,128)(2,1)S(1)}, u32[]{:S(2)}, u32[]{:S(2)}) collective-permute-start(bf16[8,3584]{1,0:T(8,128)(2,1)S(1)} %get-tuple-element.73), channel_id=1, source_target_pairs={{0,16},{1,17},{2,18},{3,19},{4,20},{5,21},{6,22},{7,23},{8,24},{9,... | collective-permute-start | bytes 172040 | tf_op jit(solution)/shard_map/ppermute | solution.py:191
  50.6 6.8 %collective-permute-start.29 = (bf16[8,3584]{1,0:T(8,128)(2,1)S(1)}, bf16[8,3584]{1,0:T(8,128)(2,1)S(1)}, u32[]{:S(2)}, u32[]{:S(2)}) collective-permute-start(bf16[8,3584]{1,0:T(8,128)(2,1)S(1)} %get-tuple-element.74), channel_id=1, source_target_pairs={{0,24},{1,25},{2,26},{3,27},{4,28},{5,29},{6,30},{7,31},{8,16},{9,... | collective-permute-start | bytes 172040 | tf_op jit(solution)/shard_map/ppermute | solution.py:191
  52.1 5.9 %collective-permute-start.17 = (bf16[8,3584]{1,0:T(8,128)(2,1)S(1)}, bf16[8,3584]{1,0:T(8,128)(2,1)S(1)}, u32[]{:S(2)}, u32[]{:S(2)}) collective-permute-start(bf16[8,3584]{1,0:T(8,128)(2,1)S(1)} %get-tuple-element.60), channel_id=1, source_target_pairs={{0,8},{1,9},{2,10},{3,11},{4,12},{5,13},{6,14},{7,15},{8,0},{9,1},... | collective-permute-start | bytes 172040 | tf_op jit(solution)/shard_map/ppermute | solution.py:191
  53.5 6.6 %collective-permute-start.18 = (bf16[8,3584]{1,0:T(8,128)(2,1)S(1)}, bf16[8,3584]{1,0:T(8,128)(2,1)S(1)}, u32[]{:S(2)}, u32[]{:S(2)}) collective-permute-start(bf16[8,3584]{1,0:T(8,128)(2,1)S(1)} %get-tuple-element.61), channel_id=1, source_target_pairs={{0,16},{1,17},{2,18},{3,19},{4,20},{5,21},{6,22},{7,23},{8,24},{9,... | collective-permute-start | bytes 172040 | tf_op jit(solution)/shard_map/ppermute | solution.py:191
  55.2 6.1 %collective-permute-start.19 = (bf16[8,3584]{1,0:T(8,128)(2,1)S(1)}, bf16[8,3584]{1,0:T(8,128)(2,1)S(1)}, u32[]{:S(2)}, u32[]{:S(2)}) collective-permute-start(bf16[8,3584]{1,0:T(8,128)(2,1)S(1)} %get-tuple-element.62), channel_id=1, source_target_pairs={{0,24},{1,25},{2,26},{3,27},{4,28},{5,29},{6,30},{7,31},{8,16},{9,... | collective-permute-start | bytes 172040 | tf_op jit(solution)/shard_map/ppermute | solution.py:191

commit v4 on v3

v4 whole, which is shorter than its diff:
```python
import functools

import jax
import jax.numpy as jnp
from jax import lax
from jax.experimental import pallas as pl
from jax.experimental.pallas import tpu as pltpu
from jax.sharding import PartitionSpec as P

BF16, F32, I32 = jnp.bfloat16, jnp.float32, jnp.int32
VMEM = pl.BlockSpec(memory_space=pltpu.VMEM)
SMEM = pl.BlockSpec(memory_space=pltpu.SMEM)
HBM = pl.BlockSpec(memory_space=pltpu.HBM)


def shape(dims, dtype):
    return jax.ShapeDtypeStruct(dims, dtype)


def call(kernel, outs, ins, name, flops=0, moved=0, limit=24, scratch=()):
    return pl.pallas_call(
        kernel,
        out_shape=outs,
        in_specs=ins,
        out_specs=[VMEM] * len(outs),
        scratch_shapes=list(scratch),
        compiler_params=pltpu.CompilerParams(vmem_limit_bytes=limit << 20),
        cost_estimate=pl.CostEstimate(flops=flops, bytes_accessed=moved, transcendentals=0),
        name=name,
    )


def sweep(part, base, width, unrolled):
    step = max(t for t in (1024, 896, 512, 256, 128) if width % t == 0)
    if unrolled:
        for at in range(0, width, step):
            part(at, base + at, step)
        return

    def body(i, unused):
        part(pl.multiple_of(i * step, 128), pl.multiple_of(base + i * step, 128), step)
        return unused

    lax.fori_loop(0, width // step, body, 0)


def route_kernel(cells, ranges, slot_ref, *refs):
    ins, outs, held, sem = refs[:6], refs[6:-7], refs[-7:-1], refs[-1]
    copies = [pltpu.make_async_copy(a, b, sem.at[i]) for i, (a, b) in enumerate(zip(ins, held))]
    for c in copies:
        c.start()
    for c in copies:
        c.wait()
    ids_ref, gate_ref, pick_ref, place_ref, cap_ref, rows_ref = held
    top, toks = ids_ref.shape
    slots = place_ref.shape[1]
    total = slots * cells
    cell = lax.broadcasted_iota(I32, (total, slots), 0)
    slot = lax.broadcasted_iota(I32, (total, slots), 1)
    label = jnp.bitwise_xor(cell // cells, slot_ref[0])
    here = slot == label
    place = jnp.broadcast_to(place_ref[...], (total, slots))
    caps = jnp.broadcast_to(cap_ref[...], (total, slots))
    place_c = jnp.sum(jnp.where(here, place, 0), axis=1, keepdims=True)
    cap_c = jnp.sum(jnp.where(here, caps, 0), axis=1, keepdims=True)
    same = place == place_c
    turn_c = jnp.sum(jnp.where(same & (slot < label), 1, 0), axis=1, keepdims=True)
    hosts_c = jnp.sum(jnp.where(same, 1, 0), axis=1, keepdims=True).astype(F32)
    used = jnp.zeros((total, toks), F32)
    weight = jnp.zeros((total, toks), F32)
    for k in range(top):
        pick = pick_ref[k : k + 1, :].astype(F32)
        wanted = pick - hosts_c * jnp.floor((pick + 0.5) / hosts_c)
        chosen = (ids_ref[k : k + 1, :] == place_c) & (wanted.astype(I32) == turn_c)
        used = jnp.where(chosen, 1.0, used)
        weight = jnp.where(chosen, gate_ref[k : k + 1, :], weight)
    earlier = lax.broadcasted_iota(I32, (toks, toks), 0) < lax.broadcasted_iota(I32, (toks, toks), 1)
    rank = jnp.dot(used, earlier.astype(F32), preferred_element_type=F32).astype(I32)
    seat = lax.broadcasted_iota(I32, (total, toks), 0) % cells
    spot = (used > 0.5) & (rank < cap_c) & (rank == seat)
    outs[-1][...] = jnp.where(spot, weight, 0.0)
    pack = spot.astype(F32).astype(BF16)
    high = slots // 2
    block = 2 * cells
    for i, (lo, hi) in enumerate(ranges):
        packed = jnp.dot(pack, rows_ref[:, lo:hi], preferred_element_type=F32)
        for z in range(high):
            outs[i * high + z][...] = packed[z * block : (z + 1) * block].astype(BF16)


def split_kernel(cells, count, *refs):
    own_ref, oth_ref = refs[-2:]
    vals = [r[...].astype(F32) for r in refs[:count]]
    own_ref[...] = jnp.concatenate([v[:cells] for v in vals], axis=0).astype(BF16)
    oth_ref[...] = jnp.concatenate([v[cells:] for v in vals], axis=0).astype(BF16)


def join_kernel(count, *refs):
    refs[-1][...] = jnp.concatenate([r[...].astype(F32) for r in refs[:count]], axis=0).astype(BF16)


def half_kernel(keep_ref, core_ref, *refs):
    outs = refs[-4:]
    rows = outs[0].shape[0]
    for i, out in enumerate(outs):
        part = slice(i * rows, (i + 1) * rows)
        out[...] = (keep_ref[part, :] + core_ref[...].astype(F32)[part]).astype(out.dtype)


def merge_kernel(cells, own_ref, x_ref, y_ref, d_ref, *outs):
    own = own_ref[...] + x_ref[...].astype(F32)
    oth = y_ref[...].astype(F32) + d_ref[...].astype(F32)
    for z, out in enumerate(outs):
        part = slice(z * cells, (z + 1) * cells)
        out[...] = jnp.concatenate([own[part], oth[part]], axis=0).astype(BF16)


def fetch_kernel(count, *refs):
    ins, outs, sem = refs[:count], refs[count + 1 : 2 * count + 1], refs[2 * count + 1]
    copies = [pltpu.make_async_copy(a, b, sem.at[i]) for i, (a, b) in enumerate(zip(ins, outs))]
    for c in copies:
        c.start()
    for c in copies:
        c.wait()


def up_kernel(near, far, *refs):
    rows, (gate_ref, up_ref), (far_hid, near_hid, acc_g, acc_u) = refs[:4], refs[4:6], refs[6:]
    acc_g[...] = jnp.zeros_like(acc_g)
    acc_u[...] = jnp.zeros_like(acc_u)

    def part(at, wat, step):
        x = jnp.concatenate([r[:, pl.ds(at, step)] for r in rows], axis=0)
        acc_g[...] += jnp.dot(x, gate_ref[pl.ds(wat, step), :], preferred_element_type=F32)
        acc_u[...] += jnp.dot(x, up_ref[pl.ds(wat, step), :], preferred_element_type=F32)

    sweep(part, 0, rows[0].shape[1], acc_g.shape[0] <= 256)
    g = acc_g[...]
    hid = (g / (1.0 + jnp.exp(-g)) * acc_u[...]).astype(BF16)
    far_hid[...] = hid[:far]
    near_hid[...] = hid[far:]


def down_kernel(hid_ref, down_ref, keep_ref, give_ref):
    rows = keep_ref.shape[0]

    def part(at, wat, step):
        val = jnp.dot(hid_ref[...], down_ref[:, pl.ds(wat, step)], preferred_element_type=F32)
        keep_ref[:, pl.ds(at, step)] = val[:rows]
        give_ref[:, pl.ds(at, step)] = val[rows:].astype(BF16)

    sweep(part, 0, keep_ref.shape[1], rows <= 128)


def combine_kernel(scale_ref, *refs):
    out_ref = refs[-1]
    toks = scale_ref.shape[0]
    s = scale_ref[...]
    a = s.astype(BF16)
    left = s - a.astype(F32)
    b = left.astype(BF16)
    c = (left - b.astype(F32)).astype(BF16)
    pieces = jnp.concatenate([v.astype(F32) for v in (a, b, c)], axis=0).astype(BF16)
    rows = jnp.concatenate([r[...].astype(F32) for r in refs[:-1]], axis=0).astype(BF16)
    val = jnp.dot(pieces, rows, preferred_element_type=F32)
    out_ref[...] = (val[:toks] + val[toks : 2 * toks] + val[2 * toks :]).astype(BF16)


def per_device(
    hidden_in, expert_ids, gate_weights, replica_pick, placement, capacity, w_gate, w_up, w_down
):
    toks, width = hidden_in.shape
    top = expert_ids.shape[1]
    slots = placement.shape[0]
    devices = lax.axis_size("node")
    members = devices // slots
    cells = members * max(1, toks * top // (slots * members))
    high = slots // 2
    fw = w_gate.shape[1]
    my_slot = lax.axis_index("node") // members
    near, far = range(high // 2), range(high // 2, high)
    rows = high // 2 * cells
    any_ref = pl.BlockSpec(memory_space=pl.ANY)

    def send(value, flip):
        return lax.ppermute(value, "node", [(d, d ^ flip) for d in range(devices)])

    def over_z(block, z):
        return block if z == 0 else send(block, 2 * members * z)

    def split(blocks, when):
        return call(
            functools.partial(split_kernel, cells, len(blocks)),
            [shape((rows, width), BF16)] * 2,
            [VMEM] * len(blocks) + [any_ref] * len(when),
            "split",
        )(*blocks, *when)

    def spread(own, oth):
        d, y, x = send(oth, members + 2), send(oth, members), send(own, 2)
        return own, x, y, d

    def join(blocks, when):
        return call(
            functools.partial(join_kernel, 4),
            [shape((4 * rows, width), BF16)],
            [VMEM] * 4 + [any_ref] * len(when),
            "join",
        )(*blocks, *when)[0]

    inputs = (expert_ids.T, gate_weights.T, replica_pick.T, placement[None, :], capacity[None, :], hidden_in)
    route = call(
        functools.partial(route_kernel, cells, [(0, width)]),
        [shape((2 * cells, width), BF16)] * high + [shape((slots * cells, toks), F32)],
        [SMEM] + [HBM] * 6,
        "route",
        limit=60,
        scratch=[pltpu.VMEM(a.shape, a.dtype) for a in inputs] + [pltpu.SemaphoreType.DMA((6,))],
    )(my_slot.reshape(1).astype(I32), *inputs)
    scale = route[-1].T
    near_z = [over_z(route[z], z) for z in near]
    far_z = [over_z(route[z], z) for z in far]
    near_own, near_oth = split(near_z, ())
    near_rows = spread(near_own, near_oth)
    far_own, far_oth = split(far_z, ())
    far_rows = spread(far_own, far_oth)
    near_all = join(near_rows, (far_own,))
    near_core = send(near_all, 1)
    wg, wu, wd = call(
        functools.partial(fetch_kernel, 3),
        [shape(w.shape, BF16) for w in (w_gate, w_up, w_down)],
        [HBM] * 4,
        "fetch",
        moved=6 * w_gate.size * 2,
        limit=40,
        scratch=[pltpu.SemaphoreType.DMA((3,))],
    )(w_gate, w_up, w_down, near_all)
    far_all = join(far_rows, (wd,))
    far_core = send(far_all, 1)
    far_hid, near_hid, _, _ = call(
        functools.partial(up_kernel, 8 * rows, 8 * rows),
        [shape((8 * rows, fw), BF16)] * 2 + [shape((16 * rows, fw), F32)] * 2,
        [VMEM] * 6,
        "up",
        flops=64 * rows * fw * width,
    )(far_all, far_core, near_all, near_core, wg, wu)

    def down(hid, when):
        return call(
            down_kernel,
            [shape((4 * rows, width), F32), shape((4 * rows, width), BF16)],
            [VMEM] * 2 + [any_ref] * len(when),
            "down",
            flops=16 * rows * fw * width,
        )(hid, wd, *when)

    def half(keep, got, when):
        return call(
            half_kernel,
            [shape((rows, width), F32)] + [shape((rows, width), BF16)] * 3,
            [VMEM] * 2 + [any_ref] * len(when),
            "half",
        )(keep, got, *when)

    def merge(own, x, y, d):
        dg, yg, xg = send(d, members + 2), send(y, members), send(x, 2)
        return call(
            functools.partial(merge_kernel, cells),
            [shape((2 * cells, width), BF16)] * (high // 2),
            [VMEM] * 4,
            "merge",
        )(own, xg, yg, dg)

    far_keep, far_give = down(far_hid, ())
    far_got = send(far_give, 1)
    near_keep, near_give = down(near_hid, ())
    near_got = send(near_give, 1)
    far_done = merge(*half(far_keep, far_got, ()))
    far_back = [over_z(v, z) for v, z in zip(far_done, far)]
    near_done = merge(*half(near_keep, near_got, (far_done[0],)))
    near_back = [over_z(v, z) for v, z in zip(near_done, near)]
    (mixed,) = call(
        combine_kernel,
        [shape((toks, width), BF16)],
        [VMEM] * (1 + high),
        "combine",
    )(scale, *near_back, *far_back)
    return mixed


def solution(mesh):
    split = P(("grp", "node"), None)
    placed = (split, split, split, split, P(), P(), P(None, "node"), P(None, "node"), P("node", None))
    return jax.shard_map(per_device, mesh=mesh, in_specs=placed, out_specs=split, check_vma=False)
```

time: 62.4 us -> 58.3 us (0.934)
  waiting for transfers between devices: 19.8 us -> 17.4 us
  starting transfers between devices: 30.7 us -> 28.4 us
  Pallas kernels: 10.6 us -> 11.3 us
    ppermute x30 -> x22, waiting for transfers between devices: 19.8 us -> 17.4 us  [send(): return lax.ppermute(value, 'node', [(d, d ^ flip) for d in range(devices)])]
    ppermute x30 -> x22, starting transfers between devices: 30.7 us -> 28.4 us  [send(): return lax.ppermute(value, 'node', [(d, d ^ flip) for d in range(devices)])]
    pallas_call x8 -> x13, Pallas kernels: 6.32 us -> 7.08 us  [the longest x1 2.34 us: per_device(): call(functools.partial(route_kernel, cells, [(0, width)]), [shape((2 * ce...]
  transfers between devices with their start and end apart: 30 -> 22, of which waited for: 13 -> 10; matrix products, arithmetic and copies ran while one was open for 0% -> 0% of each run, Pallas kernels for 8% -> 9%
where the time goes in v4:
time: 58.3 us; the launch traced here: 58.2 us
  starting transfers between devices  28.4 us (49%)
  waiting for transfers between devices  17.4 us (30%)
  Pallas kernels  11.3 us (19%)
  local copies, waits for them, and re-layouts  0.97 us (2%)
    ppermute x22, starting transfers between devices, send(): return lax.ppermute(value, 'node', [(d, d ^ flip) for d in range(devices)])  28.4 us
    ppermute x22, waiting for transfers between devices, send(): return lax.ppermute(value, 'node', [(d, d ^ flip) for d in range(devices)])  17.4 us
    pallas_call x1, Pallas kernels, per_device(): call(functools.partial(fetch_kernel, 3), [shape(w.shape, BF16) for w in (...  4.23 us
    pallas_call x1, Pallas kernels, per_device(): call(functools.partial(route_kernel, cells, [(0, width)]), [shape((2 * ce...  2.34 us
    pallas_call x1, Pallas kernels, per_device(): call(functools.partial(up_kernel, 8 * rows, 8 * rows), [shape((8 * rows,...  1.81 us
    pallas_call x2, Pallas kernels, down(): call(down_kernel, [shape((4 * rows, width), F32), shape((4 * rows, width)...  1.5 us
  transfers between devices with their start and end apart: 22, of which 10 were waited for; matrix products, arithmetic and copies ran while one was open for 0% of the time, Pallas kernels for 9%

profile of v4, /device:TPU:0, one launch (start us, length us, event | category | flops | bytes accessed | tf_op | source)
XLA Modules:
  0.0 58.2 jit_solution(13462371779419310318)
XLA Ops:
  0.0 2.3 %route.1 = (bf16[8,7168]{1,0:T(8,128)(2,1)}, bf16[8,7168]{1,0:T(8,128)(2,1)}, bf16[8,7168]{1,0:T(8,128)(2,1)}, bf16[8,7168]{1,0:T(8,128)(2,1)}, f32[32,8]{1,0:T(8,128)}) custom-call(s32[1]{0:T(128)} %bitcast.slot_ref, s32[4,8]{1,0:T(4,128)} %bitcast.8, f32[4,8]{1,0:T(4,128)} %bitcast.9, s32[4,8]{1,0:T(4,128)} %bitcast.10, s32[1,8]{1,0:T(1,128)} %bitcast.11, ...), custom_call_target="tpu_custom_call" | custom-call | tf_op jit(solution)/shard_map/route/pallas_call | solution.py:212
  2.3 3.1 %collective-permute-start.5 = (bf16[8,7168]{1,0:T(8,128)(2,1)}, bf16[8,7168]{1,0:T(8,128)(2,1)S(1)}, u32[]{:S(2)}, u32[]{:S(2)}) collective-permute-start(bf16[8,7168]{1,0:T(8,128)(2,1)} %get-tuple-element.41), channel_id=1, source_target_pairs={{0,8},{1,9},{2,10},{3,11},{4,12},{5,13},{6,14},{7,15},{8,0},{9,1},... | collective-permute-start | bytes 344072 | tf_op jit(solution)/shard_map/ppermute | solution.py:186
  5.4 2.6 %collective-permute-start = (bf16[8,7168]{1,0:T(8,128)(2,1)}, bf16[8,7168]{1,0:T(8,128)(2,1)S(1)}, u32[]{:S(2)}, u32[]{:S(2)}) collective-permute-start(bf16[8,7168]{1,0:T(8,128)(2,1)} %get-tuple-element.36), channel_id=1, source_target_pairs={{0,16},{1,17},{2,18},{3,19},{4,20},{5,21},{6,22},{7,23},{8,24},{9,... | collective-permute-start | bytes 344072 | tf_op jit(solution)/shard_map/ppermute | solution.py:186
  8.0 0.0 collective-permute-start.1
  8.0 0.8 %collective-permute-done.5.refs_1_ = bf16[8,7168]{1,0:T(8,128)(2,1)S(1)} collective-permute-done((bf16[8,7168]{1,0:T(8,128)(2,1)}, bf16[8,7168]{1,0:T(8,128)(2,1)S(1)}, u32[]{:S(2)}, u32[]{:S(2)}) %collective-permute-start.5) | collective-permute-done | bytes 114720 | tf_op jit(solution)/shard_map/ppermute | solution.py:186
  8.8 0.0 copy-start
  8.8 0.9 %copy-done = bf16[8,7168]{1,0:T(8,128)(2,1)S(1)} copy-done((bf16[8,7168]{1,0:T(8,128)(2,1)S(1)}, bf16[8,7168]{1,0:T(8,128)(2,1)}, u32[]{:S(2)}) %copy-start) | copy-done | bytes 114712
  9.7 0.1 split.3
  9.8 2.9 %collective-permute-start.6 = (bf16[8,7168]{1,0:T(8,128)(2,1)S(1)}, bf16[8,7168]{1,0:T(8,128)(2,1)S(1)}, u32[]{:S(2)}, u32[]{:S(2)}) collective-permute-start(bf16[8,7168]{1,0:T(8,128)(2,1)S(1)} %get-tuple-element.42.refs_0_), channel_id=1, source_target_pairs={{0,2},{1,3},{2,0},{3,1},{4,6},{5,7},{6,4},{7,5},{8,10},{9,11},{10,... | collective-permute-start | bytes 344072 | tf_op jit(solution)/shard_map/ppermute | solution.py:186
  12.7 1.5 %collective-permute-start.8 = (bf16[8,7168]{1,0:T(8,128)(2,1)S(1)}, bf16[8,7168]{1,0:T(8,128)(2,1)S(1)}, u32[]{:S(2)}, u32[]{:S(2)}) collective-permute-start(bf16[8,7168]{1,0:T(8,128)(2,1)S(1)} %get-tuple-element.43), channel_id=1, source_target_pairs={{0,6},{1,7},{2,4},{3,5},{4,2},{5,3},{6,0},{7,1},{8,14},{9,15},{10,... | collective-permute-start | bytes 344072 | tf_op jit(solution)/shard_map/ppermute | solution.py:186
  14.2 0.1 collective-permute-start.7
  14.3 3.1 %collective-permute-done.refs_0_ = bf16[8,7168]{1,0:T(8,128)(2,1)S(1)} collective-permute-done((bf16[8,7168]{1,0:T(8,128)(2,1)}, bf16[8,7168]{1,0:T(8,128)(2,1)S(1)}, u32[]{:S(2)}, u32[]{:S(2)}) %collective-permute-start) | collective-permute-done | bytes 114720 | tf_op jit(solution)/shard_map/ppermute | solution.py:186
  17.3 0.0 collective-permute-done.1.refs_1_
  17.3 0.1 split.2
  17.4 2.5 %collective-permute-start.4 = (bf16[8,7168]{1,0:T(8,128)(2,1)S(1)}, bf16[8,7168]{1,0:T(8,128)(2,1)S(1)}, u32[]{:S(2)}, u32[]{:S(2)}) collective-permute-start(bf16[8,7168]{1,0:T(8,128)(2,1)S(1)} %get-tuple-element.39), channel_id=1, source_target_pairs={{0,6},{1,7},{2,4},{3,5},{4,2},{5,3},{6,0},{7,1},{8,14},{9,15},{10,... | collective-permute-start | bytes 344072 | tf_op jit(solution)/shard_map/ppermute | solution.py:186
  19.9 0.5 collective-permute-start.3
  20.4 0.0 collective-permute-done.6.refs_1_
  20.4 0.5 collective-permute-start.2
  21.0 0.0 collective-permute-done.8.refs_3_
  21.0 0.9 %collective-permute-done.7.refs_2_ = bf16[8,7168]{1,0:T(8,128)(2,1)S(1)} collective-permute-done((bf16[8,7168]{1,0:T(8,128)(2,1)S(1)}, bf16[8,7168]{1,0:T(8,128)(2,1)S(1)}, u32[]{:S(2)}, u32[]{:S(2)}) %collective-permute-start.7) | collective-permute-done | bytes 114720 | tf_op jit(solution)/shard_map/ppermute | solution.py:186
  22.0 0.1 collective-permute-start.10
  22.0 4.2 %fetch.1 = (bf16[7168,256]{1,0:T(8,128)(2,1)S(1)}, bf16[7168,256]{1,0:T(8,128)(2,1)S(1)}, bf16[256,7168]{1,0:T(8,128)(2,1)S(1)}) custom-call(bf16[7168,256]{1,0:T(8,128)(2,1)} %refs_0_.1, bf16[7168,256]{1,0:T(8,128)(2,1)} %refs_1_.1, bf16[256,7168]{1,0:T(8,128)(2,1)} %refs_2_.1, bf16[32,7168]{1,0:T(8,128)(2,1)S(1)} %join.2.refs_3_.refs_2_), custom_call_target="tpu_custom_call" | custom-call | bytes 22020096 | tf_op jit(solution)/shard_map/fetch/pallas_call | solution.py:229
  26.3 0.0 collective-permute-done.4.refs_3_
  26.3 0.0 collective-permute-done.3.refs_2_
  26.3 0.0 collective-permute-done.2.refs_1_
  26.3 0.6 collective-permute-start.9
  26.9 0.0 collective-permute-done.10.refs_3_
  26.9 1.4 %collective-permute-done.9.refs_1_ = bf16[32,7168]{1,0:T(8,128)(2,1)S(1)} collective-permute-done((bf16[32,7168]{1,0:T(8,128)(2,1)S(1)}, bf16[32,7168]{1,0:T(8,128)(2,1)S(1)}, u32[]{:S(2)}, u32[]{:S(2)}) %collective-permute-start.9) | collective-permute-done | bytes 458784 | tf_op jit(solution)/shard_map/ppermute | solution.py:186
  28.3 1.8 %up.1 = (bf16[64,256]{1,0:T(8,128)(2,1)S(1)}, bf16[64,256]{1,0:T(8,128)(2,1)S(1)}, f32[128,256]{1,0:T(8,128)}, f32[128,256]{1,0:T(8,128)}) custom-call(bf16[32,7168]{1,0:T(8,128)(2,1)S(1)} %join.3.refs_0_, bf16[32,7168]{1,0:T(8,128)(2,1)S(1)} %collective-permute-done.9.refs_1_, bf16[32,7168]{1,0:T(8,128)(2,1)S(1)} %join.2.refs_3_.refs_2_, ...), custom_call_target="tpu_custom_call" | custom-call | flops 939524096 | tf_op jit(solution)/shard_map/up/pallas_call | solution.py:240
  30.2 0.7 %down.3 = (f32[32,7168]{1,0:T(8,128)S(1)}, bf16[32,7168]{1,0:T(8,128)(2,1)S(1)}) custom-call(bf16[64,256]{1,0:T(8,128)(2,1)S(1)} %get-tuple-element.50.hid_ref, bf16[256,7168]{1,0:T(8,128)(2,1)S(1)} %get-tuple-element.44.refs_4_.down_ref), custom_call_target="tpu_custom_call" | custom-call | flops 234881024 | tf_op jit(solution)/shard_map/down/pallas_call | solution.py:249
  30.9 0.4 collective-permute-start.12
  31.4 0.0 copy-start.1
  31.4 0.7 %down.2 = (f32[32,7168]{1,0:T(8,128)S(1)}, bf16[32,7168]{1,0:T(8,128)(2,1)S(1)}) custom-call(bf16[64,256]{1,0:T(8,128)(2,1)S(1)} %get-tuple-element.47.hid_ref, bf16[256,7168]{1,0:T(8,128)(2,1)S(1)} %get-tuple-element.44.refs_4_.down_ref), custom_call_target="tpu_custom_call" | custom-call | flops 234881024 | tf_op jit(solution)/shard_map/down/pallas_call | solution.py:249
  32.1 0.2 collective-permute-start.11
  32.3 0.5 collective-permute-done.12.core_ref
  32.8 0.1 half.2
  32.9 1.2 %collective-permute-start.13 = (bf16[8,7168]{1,0:T(8,128)(2,1)S(1)}, bf16[8,7168]{1,0:T(8,128)(2,1)S(1)}, u32[]{:S(2)}, u32[]{:S(2)}) collective-permute-start(bf16[8,7168]{1,0:T(8,128)(2,1)S(1)} %get-tuple-element.54), channel_id=1, source_target_pairs={{0,2},{1,3},{2,0},{3,1},{4,6},{5,7},{6,4},{7,5},{8,10},{9,11},{10,... | collective-permute-start | bytes 344072 | tf_op jit(solution)/shard_map/ppermute | solution.py:186
  34.1 1.0 %collective-permute-start.14 = (bf16[8,7168]{1,0:T(8,128)(2,1)S(1)}, bf16[8,7168]{1,0:T(8,128)(2,1)S(1)}, u32[]{:S(2)}, u32[]{:S(2)}) collective-permute-start(bf16[8,7168]{1,0:T(8,128)(2,1)S(1)} %get-tuple-element.55), channel_id=1, source_target_pairs={{0,4},{1,5},{2,6},{3,7},{4,0},{5,1},{6,2},{7,3},{8,12},{9,13},{10,... | collective-permute-start | bytes 344072 | tf_op jit(solution)/shard_map/ppermute | solution.py:186
  35.0 1.4 %collective-permute-start.15 = (bf16[8,7168]{1,0:T(8,128)(2,1)S(1)}, bf16[8,7168]{1,0:T(8,128)(2,1)S(1)}, u32[]{:S(2)}, u32[]{:S(2)}) collective-permute-start(bf16[8,7168]{1,0:T(8,128)(2,1)S(1)} %get-tuple-element.56), channel_id=1, source_target_pairs={{0,6},{1,7},{2,4},{3,5},{4,2},{5,3},{6,0},{7,1},{8,14},{9,15},{10,... | collective-permute-start | bytes 344072 | tf_op jit(solution)/shard_map/ppermute | solution.py:186
  36.4 2.3 %collective-permute-done.13.x_ref = bf16[8,7168]{1,0:T(8,128)(2,1)S(1)} collective-permute-done((bf16[8,7168]{1,0:T(8,128)(2,1)S(1)}, bf16[8,7168]{1,0:T(8,128)(2,1)S(1)}, u32[]{:S(2)}, u32[]{:S(2)}) %collective-permute-start.13) | collective-permute-done | bytes 114720 | tf_op jit(solution)/shard_map/ppermute | solution.py:186
  38.8 2.9 %collective-permute-done.14.y_ref = bf16[8,7168]{1,0:T(8,128)(2,1)S(1)} collective-permute-done((bf16[8,7168]{1,0:T(8,128)(2,1)S(1)}, bf16[8,7168]{1,0:T(8,128)(2,1)S(1)}, u32[]{:S(2)}, u32[]{:S(2)}) %collective-permute-start.14) | collective-permute-done | bytes 114720 | tf_op jit(solution)/shard_map/ppermute | solution.py:186
  41.6 0.0 collective-permute-done.15.d_ref
  41.6 0.1 merge.2
  41.7 0.0 collective-permute-done.11.core_ref
  41.7 0.1 half.3
  41.8 1.0 %collective-permute-start.16 = (bf16[8,7168]{1,0:T(8,128)(2,1)S(1)}, bf16[8,7168]{1,0:T(8,128)(2,1)S(1)}, u32[]{:S(2)}, u32[]{:S(2)}) collective-permute-start(bf16[8,7168]{1,0:T(8,128)(2,1)S(1)} %get-tuple-element.59), channel_id=1, source_target_pairs={{0,2},{1,3},{2,0},{3,1},{4,6},{5,7},{6,4},{7,5},{8,10},{9,11},{10,... | collective-permute-start | bytes 344072 | tf_op jit(solution)/shard_map/ppermute | solution.py:186
  42.8 0.8 %collective-permute-start.17 = (bf16[8,7168]{1,0:T(8,128)(2,1)S(1)}, bf16[8,7168]{1,0:T(8,128)(2,1)S(1)}, u32[]{:S(2)}, u32[]{:S(2)}) collective-permute-start(bf16[8,7168]{1,0:T(8,128)(2,1)S(1)} %get-tuple-element.60), channel_id=1, source_target_pairs={{0,4},{1,5},{2,6},{3,7},{4,0},{5,1},{6,2},{7,3},{8,12},{9,13},{10,... | collective-permute-start | bytes 344072 | tf_op jit(solution)/shard_map/ppermute | solution.py:186
  43.6 1.8 %collective-permute-start.18 = (bf16[8,7168]{1,0:T(8,128)(2,1)S(1)}, bf16[8,7168]{1,0:T(8,128)(2,1)S(1)}, u32[]{:S(2)}, u32[]{:S(2)}) collective-permute-start(bf16[8,7168]{1,0:T(8,128)(2,1)S(1)} %get-tuple-element.61), channel_id=1, source_target_pairs={{0,6},{1,7},{2,4},{3,5},{4,2},{5,3},{6,0},{7,1},{8,14},{9,15},{10,... | collective-permute-start | bytes 344072 | tf_op jit(solution)/shard_map/ppermute | solution.py:186
  45.4 2.3 %collective-permute-start.20 = (bf16[8,7168]{1,0:T(8,128)(2,1)S(1)}, bf16[8,7168]{1,0:T(8,128)(2,1)S(1)}, u32[]{:S(2)}, u32[]{:S(2)}) collective-permute-start(bf16[8,7168]{1,0:T(8,128)(2,1)S(1)} %get-tuple-element.57.refs_0_), channel_id=1, source_target_pairs={{0,16},{1,17},{2,18},{3,19},{4,20},{5,21},{6,22},{7,23},{8,24},{9,... | collective-permute-start | bytes 344072 | tf_op jit(solution)/shard_map/ppermute | solution.py:186
  47.6 3.4 %collective-permute-start.21 = (bf16[8,7168]{1,0:T(8,128)(2,1)S(1)}, bf16[8,7168]{1,0:T(8,128)(2,1)S(1)}, u32[]{:S(2)}, u32[]{:S(2)}) collective-permute-start(bf16[8,7168]{1,0:T(8,128)(2,1)S(1)} %get-tuple-element.64), channel_id=1, source_target_pairs={{0,24},{1,25},{2,26},{3,27},{4,28},{5,29},{6,30},{7,31},{8,16},{9,... | collective-permute-start | bytes 344072 | tf_op jit(solution)/shard_map/ppermute | solution.py:186
  51.0 0.0 collective-permute-done.16.x_ref
  51.0 0.0 collective-permute-done.17.y_ref
  51.0 0.0 collective-permute-done.18.d_ref
  51.0 0.1 merge.3
  51.1 0.6 %collective-permute-start.19 = (bf16[8,7168]{1,0:T(8,128)(2,1)S(1)}, bf16[8,7168]{1,0:T(8,128)(2,1)S(1)}, u32[]{:S(2)}, u32[]{:S(2)}) collective-permute-start(bf16[8,7168]{1,0:T(8,128)(2,1)S(1)} %get-tuple-element.63), channel_id=1, source_target_pairs={{0,8},{1,9},{2,10},{3,11},{4,12},{5,13},{6,14},{7,15},{8,0},{9,1},... | collective-permute-start | bytes 344072 | tf_op jit(solution)/shard_map/ppermute | solution.py:186
  51.8 0.0 copy-done.1
  51.8 0.1 copy.10
  51.8 3.8 %collective-permute-done.21.refs_3_ = bf16[8,7168]{1,0:T(8,128)(2,1)S(1)} collective-permute-done((bf16[8,7168]{1,0:T(8,128)(2,1)S(1)}, bf16[8,7168]{1,0:T(8,128)(2,1)S(1)}, u32[]{:S(2)}, u32[]{:S(2)}) %collective-permute-start.21) | collective-permute-done | bytes 114720 | tf_op jit(solution)/shard_map/ppermute | solution.py:186
  55.6 1.3 %collective-permute-done.20.refs_2_ = bf16[8,7168]{1,0:T(8,128)(2,1)S(1)} collective-permute-done((bf16[8,7168]{1,0:T(8,128)(2,1)S(1)}, bf16[8,7168]{1,0:T(8,128)(2,1)S(1)}, u32[]{:S(2)}, u32[]{:S(2)}) %collective-permute-start.20) | collective-permute-done | bytes 114720 | tf_op jit(solution)/shard_map/ppermute | solution.py:186
  56.9 0.4 collective-permute-done.19.refs_1_
  57.2 0.9 %combine.1 = bf16[8,7168]{1,0:T(8,128)(2,1)} custom-call(f32[8,32]{1,0:T(8,128)S(1)} %bitcast.7, bf16[8,7168]{1,0:T(8,128)(2,1)S(1)} %get-tuple-element.62.refs_0_, bf16[8,7168]{1,0:T(8,128)(2,1)S(1)} %collective-permute-done.19.refs_1_, bf16[8,7168]{1,0:T(8,128)(2,1)S(1)} %collective-permute-done.20.refs_2_, bf16[8,7168]{1,0:T(8,128)(2,1)S(1)} %collective-permute-done.21.refs_3_), custom_call_target="tpu_custom_call" | custom-call | tf_op jit(solution)/shard_map/combine/pallas_call | solution.py:282
  (2 shorter events, 0.1 us)
Async XLA Ops:
  2.3 6.5 %collective-permute-start.5 = (bf16[8,7168]{1,0:T(8,128)(2,1)}, bf16[8,7168]{1,0:T(8,128)(2,1)S(1)}, u32[]{:S(2)}, u32[]{:S(2)}) collective-permute-start(bf16[8,7168]{1,0:T(8,128)(2,1)} %get-tuple-element.41), channel_id=1, source_target_pairs={{0,8},{1,9},{2,10},{3,11},{4,12},{5,13},{6,14},{7,15},{8,0},{9,1},... | collective-permute-start | bytes 344072 | tf_op jit(solution)/shard_map/ppermute | solution.py:186
  5.4 11.9 %collective-permute-start = (bf16[8,7168]{1,0:T(8,128)(2,1)}, bf16[8,7168]{1,0:T(8,128)(2,1)S(1)}, u32[]{:S(2)}, u32[]{:S(2)}) collective-permute-start(bf16[8,7168]{1,0:T(8,128)(2,1)} %get-tuple-element.36), channel_id=1, source_target_pairs={{0,16},{1,17},{2,18},{3,19},{4,20},{5,21},{6,22},{7,23},{8,24},{9,... | collective-permute-start | bytes 344072 | tf_op jit(solution)/shard_map/ppermute | solution.py:186
  8.0 9.3 %collective-permute-start.1 = (bf16[8,7168]{1,0:T(8,128)(2,1)}, bf16[8,7168]{1,0:T(8,128)(2,1)S(1)}, u32[]{:S(2)}, u32[]{:S(2)}) collective-permute-start(bf16[8,7168]{1,0:T(8,128)(2,1)} %get-tuple-element.37), channel_id=1, source_target_pairs={{0,24},{1,25},{2,26},{3,27},{4,28},{5,29},{6,30},{7,31},{8,16},{9,... | collective-permute-start | bytes 344072 | tf_op jit(solution)/shard_map/ppermute | solution.py:186
  8.8 0.9 %copy-start = (bf16[8,7168]{1,0:T(8,128)(2,1)S(1)}, bf16[8,7168]{1,0:T(8,128)(2,1)}, u32[]{:S(2)}) copy-start(bf16[8,7168]{1,0:T(8,128)(2,1)} %get-tuple-element.40.refs_0_) | copy-start | bytes 344068
  9.8 10.7 %collective-permute-start.6 = (bf16[8,7168]{1,0:T(8,128)(2,1)S(1)}, bf16[8,7168]{1,0:T(8,128)(2,1)S(1)}, u32[]{:S(2)}, u32[]{:S(2)}) collective-permute-start(bf16[8,7168]{1,0:T(8,128)(2,1)S(1)} %get-tuple-element.42.refs_0_), channel_id=1, source_target_pairs={{0,2},{1,3},{2,0},{3,1},{4,6},{5,7},{6,4},{7,5},{8,10},{9,11},{10,... | collective-permute-start | bytes 344072 | tf_op jit(solution)/shard_map/ppermute | solution.py:186
  12.7 8.3 %collective-permute-start.8 = (bf16[8,7168]{1,0:T(8,128)(2,1)S(1)}, bf16[8,7168]{1,0:T(8,128)(2,1)S(1)}, u32[]{:S(2)}, u32[]{:S(2)}) collective-permute-start(bf16[8,7168]{1,0:T(8,128)(2,1)S(1)} %get-tuple-element.43), channel_id=1, source_target_pairs={{0,6},{1,7},{2,4},{3,5},{4,2},{5,3},{6,0},{7,1},{8,14},{9,15},{10,... | collective-permute-start | bytes 344072 | tf_op jit(solution)/shard_map/ppermute | solution.py:186
  14.2 7.7 %collective-permute-start.7 = (bf16[8,7168]{1,0:T(8,128)(2,1)S(1)}, bf16[8,7168]{1,0:T(8,128)(2,1)S(1)}, u32[]{:S(2)}, u32[]{:S(2)}) collective-permute-start(bf16[8,7168]{1,0:T(8,128)(2,1)S(1)} %get-tuple-element.43), channel_id=1, source_target_pairs={{0,4},{1,5},{2,6},{3,7},{4,0},{5,1},{6,2},{7,3},{8,12},{9,13},{10,... | collective-permute-start | bytes 344072 | tf_op jit(solution)/shard_map/ppermute | solution.py:186
  17.4 8.9 %collective-permute-start.4 = (bf16[8,7168]{1,0:T(8,128)(2,1)S(1)}, bf16[8,7168]{1,0:T(8,128)(2,1)S(1)}, u32[]{:S(2)}, u32[]{:S(2)}) collective-permute-start(bf16[8,7168]{1,0:T(8,128)(2,1)S(1)} %get-tuple-element.39), channel_id=1, source_target_pairs={{0,6},{1,7},{2,4},{3,5},{4,2},{5,3},{6,0},{7,1},{8,14},{9,15},{10,... | collective-permute-start | bytes 344072 | tf_op jit(solution)/shard_map/ppermute | solution.py:186
  19.9 6.3 %collective-permute-start.3 = (bf16[8,7168]{1,0:T(8,128)(2,1)S(1)}, bf16[8,7168]{1,0:T(8,128)(2,1)S(1)}, u32[]{:S(2)}, u32[]{:S(2)}) collective-permute-start(bf16[8,7168]{1,0:T(8,128)(2,1)S(1)} %get-tuple-element.39), channel_id=1, source_target_pairs={{0,4},{1,5},{2,6},{3,7},{4,0},{5,1},{6,2},{7,3},{8,12},{9,13},{10,... | collective-permute-start | bytes 344072 | tf_op jit(solution)/shard_map/ppermute | solution.py:186
  20.4 5.8 %collective-permute-start.2 = (bf16[8,7168]{1,0:T(8,128)(2,1)S(1)}, bf16[8,7168]{1,0:T(8,128)(2,1)S(1)}, u32[]{:S(2)}, u32[]{:S(2)}) collective-permute-start(bf16[8,7168]{1,0:T(8,128)(2,1)S(1)} %get-tuple-element.38.refs_4_.refs_0_), channel_id=1, source_target_pairs={{0,2},{1,3},{2,0},{3,1},{4,6},{5,7},{6,4},{7,5},{8,10},{9,11},{10,... | collective-permute-start | bytes 344072 | tf_op jit(solution)/shard_map/ppermute | solution.py:186
  22.0 5.0 %collective-permute-start.10 = (bf16[32,7168]{1,0:T(8,128)(2,1)S(1)}, bf16[32,7168]{1,0:T(8,128)(2,1)S(1)}, u32[]{:S(2)}, u32[]{:S(2)}) collective-permute-start(bf16[32,7168]{1,0:T(8,128)(2,1)S(1)} %join.2.refs_3_.refs_2_), channel_id=1, source_target_pairs={{0,1},{1,0},{2,3},{3,2},{4,5},{5,4},{6,7},{7,6},{8,9},{9,8},{10,11... | collective-permute-start | bytes 1376264 | tf_op jit(solution)/shard_map/ppermute | solution.py:186
  26.3 2.0 %collective-permute-start.9 = (bf16[32,7168]{1,0:T(8,128)(2,1)S(1)}, bf16[32,7168]{1,0:T(8,128)(2,1)S(1)}, u32[]{:S(2)}, u32[]{:S(2)}) collective-permute-start(bf16[32,7168]{1,0:T(8,128)(2,1)S(1)} %join.3.refs_0_), channel_id=1, source_target_pairs={{0,1},{1,0},{2,3},{3,2},{4,5},{5,4},{6,7},{7,6},{8,9},{9,8},{10,11... | collective-permute-start | bytes 1376264 | tf_op jit(solution)/shard_map/ppermute | solution.py:186
  30.9 1.9 %collective-permute-start.12 = (bf16[32,7168]{1,0:T(8,128)(2,1)S(1)}, bf16[32,7168]{1,0:T(8,128)(2,1)S(1)}, u32[]{:S(2)}, u32[]{:S(2)}) collective-permute-start(bf16[32,7168]{1,0:T(8,128)(2,1)S(1)} %get-tuple-element.52), channel_id=1, source_target_pairs={{0,1},{1,0},{2,3},{3,2},{4,5},{5,4},{6,7},{7,6},{8,9},{9,8},{10,11... | collective-permute-start | bytes 1376264 | tf_op jit(solution)/shard_map/ppermute | solution.py:186
  31.4 20.4 %copy-start.1 = (f32[32,8]{1,0:T(8,128)S(1)}, f32[32,8]{1,0:T(8,128)}, u32[]{:S(2)}) copy-start(f32[32,8]{1,0:T(8,128)} %get-tuple-element.35) | copy-start | bytes 3076
  32.1 9.6 %collective-permute-start.11 = (bf16[32,7168]{1,0:T(8,128)(2,1)S(1)}, bf16[32,7168]{1,0:T(8,128)(2,1)S(1)}, u32[]{:S(2)}, u32[]{:S(2)}) collective-permute-start(bf16[32,7168]{1,0:T(8,128)(2,1)S(1)} %get-tuple-element.49), channel_id=1, source_target_pairs={{0,1},{1,0},{2,3},{3,2},{4,5},{5,4},{6,7},{7,6},{8,9},{9,8},{10,11... | collective-permute-start | bytes 1376264 | tf_op jit(solution)/shard_map/ppermute | solution.py:186
  32.9 5.9 %collective-permute-start.13 = (bf16[8,7168]{1,0:T(8,128)(2,1)S(1)}, bf16[8,7168]{1,0:T(8,128)(2,1)S(1)}, u32[]{:S(2)}, u32[]{:S(2)}) collective-permute-start(bf16[8,7168]{1,0:T(8,128)(2,1)S(1)} %get-tuple-element.54), channel_id=1, source_target_pairs={{0,2},{1,3},{2,0},{3,1},{4,6},{5,7},{6,4},{7,5},{8,10},{9,11},{10,... | collective-permute-start | bytes 344072 | tf_op jit(solution)/shard_map/ppermute | solution.py:186
  34.1 7.6 %collective-permute-start.14 = (bf16[8,7168]{1,0:T(8,128)(2,1)S(1)}, bf16[8,7168]{1,0:T(8,128)(2,1)S(1)}, u32[]{:S(2)}, u32[]{:S(2)}) collective-permute-start(bf16[8,7168]{1,0:T(8,128)(2,1)S(1)} %get-tuple-element.55), channel_id=1, source_target_pairs={{0,4},{1,5},{2,6},{3,7},{4,0},{5,1},{6,2},{7,3},{8,12},{9,13},{10,... | collective-permute-start | bytes 344072 | tf_op jit(solution)/shard_map/ppermute | solution.py:186
  35.0 6.6 %collective-permute-start.15 = (bf16[8,7168]{1,0:T(8,128)(2,1)S(1)}, bf16[8,7168]{1,0:T(8,128)(2,1)S(1)}, u32[]{:S(2)}, u32[]{:S(2)}) collective-permute-start(bf16[8,7168]{1,0:T(8,128)(2,1)S(1)} %get-tuple-element.56), channel_id=1, source_target_pairs={{0,6},{1,7},{2,4},{3,5},{4,2},{5,3},{6,0},{7,1},{8,14},{9,15},{10,... | collective-permute-start | bytes 344072 | tf_op jit(solution)/shard_map/ppermute | solution.py:186
  41.8 9.2 %collective-permute-start.16 = (bf16[8,7168]{1,0:T(8,128)(2,1)S(1)}, bf16[8,7168]{1,0:T(8,128)(2,1)S(1)}, u32[]{:S(2)}, u32[]{:S(2)}) collective-permute-start(bf16[8,7168]{1,0:T(8,128)(2,1)S(1)} %get-tuple-element.59), channel_id=1, source_target_pairs={{0,2},{1,3},{2,0},{3,1},{4,6},{5,7},{6,4},{7,5},{8,10},{9,11},{10,... | collective-permute-start | bytes 344072 | tf_op jit(solution)/shard_map/ppermute | solution.py:186
  42.8 8.2 %collective-permute-start.17 = (bf16[8,7168]{1,0:T(8,128)(2,1)S(1)}, bf16[8,7168]{1,0:T(8,128)(2,1)S(1)}, u32[]{:S(2)}, u32[]{:S(2)}) collective-permute-start(bf16[8,7168]{1,0:T(8,128)(2,1)S(1)} %get-tuple-element.60), channel_id=1, source_target_pairs={{0,4},{1,5},{2,6},{3,7},{4,0},{5,1},{6,2},{7,3},{8,12},{9,13},{10,... | collective-permute-start | bytes 344072 | tf_op jit(solution)/shard_map/ppermute | solution.py:186
  43.6 7.4 %collective-permute-start.18 = (bf16[8,7168]{1,0:T(8,128)(2,1)S(1)}, bf16[8,7168]{1,0:T(8,128)(2,1)S(1)}, u32[]{:S(2)}, u32[]{:S(2)}) collective-permute-start(bf16[8,7168]{1,0:T(8,128)(2,1)S(1)} %get-tuple-element.61), channel_id=1, source_target_pairs={{0,6},{1,7},{2,4},{3,5},{4,2},{5,3},{6,0},{7,1},{8,14},{9,15},{10,... | collective-permute-start | bytes 344072 | tf_op jit(solution)/shard_map/ppermute | solution.py:186
  45.4 11.5 %collective-permute-start.20 = (bf16[8,7168]{1,0:T(8,128)(2,1)S(1)}, bf16[8,7168]{1,0:T(8,128)(2,1)S(1)}, u32[]{:S(2)}, u32[]{:S(2)}) collective-permute-start(bf16[8,7168]{1,0:T(8,128)(2,1)S(1)} %get-tuple-element.57.refs_0_), channel_id=1, source_target_pairs={{0,16},{1,17},{2,18},{3,19},{4,20},{5,21},{6,22},{7,23},{8,24},{9,... | collective-permute-start | bytes 344072 | tf_op jit(solution)/shard_map/ppermute | solution.py:186
  47.6 7.9 %collective-permute-start.21 = (bf16[8,7168]{1,0:T(8,128)(2,1)S(1)}, bf16[8,7168]{1,0:T(8,128)(2,1)S(1)}, u32[]{:S(2)}, u32[]{:S(2)}) collective-permute-start(bf16[8,7168]{1,0:T(8,128)(2,1)S(1)} %get-tuple-element.64), channel_id=1, source_target_pairs={{0,24},{1,25},{2,26},{3,27},{4,28},{5,29},{6,30},{7,31},{8,16},{9,... | collective-permute-start | bytes 344072 | tf_op jit(solution)/shard_map/ppermute | solution.py:186
  51.1 6.1 %collective-permute-start.19 = (bf16[8,7168]{1,0:T(8,128)(2,1)S(1)}, bf16[8,7168]{1,0:T(8,128)(2,1)S(1)}, u32[]{:S(2)}, u32[]{:S(2)}) collective-permute-start(bf16[8,7168]{1,0:T(8,128)(2,1)S(1)} %get-tuple-element.63), channel_id=1, source_target_pairs={{0,8},{1,9},{2,10},{3,11},{4,12},{5,13},{6,14},{7,15},{8,0},{9,1},... | collective-permute-start | bytes 344072 | tf_op jit(solution)/shard_map/ppermute | solution.py:186

commit v5 on v4

--- a/solution.py
+++ b/solution.py
@@ -30,6 +30,23 @@
     )
 
 
+def pieces(weights):
+    a = weights.astype(BF16)
+    b = (weights - a.astype(F32)).astype(BF16)
+    c = (weights - a.astype(F32) - b.astype(F32)).astype(BF16)
+    return a, b, c
+
+
+def across(left, right):
+    return lax.dot_general(left, right, (((0,), (0,)), ((), ())), preferred_element_type=F32)
+
+
+def lane_slice(tail, start, count):
+    lanes = tail.shape[1]
+    place = lax.broadcasted_iota(I32, (lanes, count), 0) == lax.broadcasted_iota(I32, (lanes, count), 1) + start
+    return jnp.dot(tail, jnp.where(place, 1.0, 0.0).astype(BF16), preferred_element_type=F32)
+
+
 def sweep(part, base, width, unrolled):
     step = max(t for t in (1024, 896, 512, 256, 128) if width % t == 0)
     if unrolled:
@@ -44,7 +61,7 @@
     lax.fori_loop(0, width // step, body, 0)
 
 
-def route_kernel(cells, ranges, slot_ref, *refs):
+def route_kernel(cells, count, slot_ref, *refs):
     ins, outs, held, sem = refs[:6], refs[6:-7], refs[-7:-1], refs[-1]
     copies = [pltpu.make_async_copy(a, b, sem.at[i]) for i, (a, b) in enumerate(zip(ins, held))]
     for c in copies:
@@ -78,19 +95,27 @@
     rank = jnp.dot(used, earlier.astype(F32), preferred_element_type=F32).astype(I32)
     seat = lax.broadcasted_iota(I32, (total, toks), 0) % cells
     spot = (used > 0.5) & (rank < cap_c) & (rank == seat)
-    outs[-1][...] = jnp.where(spot, weight, 0.0)
-    pack = spot.astype(F32).astype(BF16)
-    high = slots // 2
+    table = jnp.where(spot, weight, 0.0)
     block = 2 * cells
-    for i, (lo, hi) in enumerate(ranges):
-        packed = jnp.dot(pack, rows_ref[:, lo:hi], preferred_element_type=F32)
-        for z in range(high):
-            outs[i * high + z][...] = packed[z * block : (z + 1) * block].astype(BF16)
+    width = rows_ref.shape[1]
+    outs[-1][...] = table[: count * block]
+    packed = jnp.dot(spot.astype(F32).astype(BF16), rows_ref[...], preferred_element_type=F32)
+    for z, out in enumerate(outs[:-1]):
+        part = slice(z * block, (z + 1) * block)
+        out[:, :width] = packed[part].astype(BF16)
+        if z >= count:
+            lanes = out.shape[1] - width
+            place = lax.broadcasted_iota(I32, (toks, lanes), 1) - lax.broadcasted_iota(I32, (toks, lanes), 0)
+            tail = jnp.zeros((block, lanes), F32)
+            for i, piece in enumerate(pieces(table[part])):
+                shift = jnp.where(place == i * toks, 1.0, 0.0).astype(BF16)
+                tail += jnp.dot(piece, shift, preferred_element_type=F32)
+            out[:, width:] = tail.astype(BF16)
 
 
 def split_kernel(cells, count, *refs):
     own_ref, oth_ref = refs[-2:]
-    vals = [r[...].astype(F32) for r in refs[:count]]
+    vals = [r[:, : own_ref.shape[1]].astype(F32) for r in refs[:count]]
     own_ref[...] = jnp.concatenate([v[:cells] for v in vals], axis=0).astype(BF16)
     oth_ref[...] = jnp.concatenate([v[cells:] for v in vals], axis=0).astype(BF16)
 
@@ -107,16 +132,49 @@
         out[...] = (keep_ref[part, :] + core_ref[...].astype(F32)[part]).astype(out.dtype)
 
 
-def merge_kernel(cells, own_ref, x_ref, y_ref, d_ref, *outs):
+def lend_kernel(cells, keep_ref, core_ref, home_ref, *outs):
+    total = keep_ref[...] + core_ref[...].astype(F32)
+    rows = total.shape[0] // 4
+    for z, out in enumerate((home_ref,) + outs):
+        parts = [total[b * rows + z * cells : b * rows + (z + 1) * cells] for b in range(4)]
+        out[...] = jnp.concatenate(parts, axis=0).astype(out.dtype)
+
+
+def regroup_kernel(cells, count, *refs):
+    vals = [r[...].astype(F32) for r in refs[:count]]
+    for b, out in enumerate(refs[-4:]):
+        out[...] = jnp.concatenate([v[b * cells : (b + 1) * cells] for v in vals], axis=0).astype(out.dtype)
+
+
+def gathered(cells, count, own_ref, x_ref, y_ref, d_ref):
     own = own_ref[...] + x_ref[...].astype(F32)
     oth = y_ref[...].astype(F32) + d_ref[...].astype(F32)
-    for z, out in enumerate(outs):
-        part = slice(z * cells, (z + 1) * cells)
-        out[...] = jnp.concatenate([own[part], oth[part]], axis=0).astype(BF16)
+    parts = [slice(z * cells, (z + 1) * cells) for z in range(count)]
+    return [jnp.concatenate([own[p], oth[p]], axis=0).astype(BF16) for p in parts]
+
+
+def weigh_kernel(cells, count, own_ref, x_ref, y_ref, d_ref, *refs):
+    wides, outs = refs[:count], refs[-count:]
+    width, toks = own_ref.shape[1], outs[0].shape[0]
+    for z, rows in enumerate(gathered(cells, count, own_ref, x_ref, y_ref, d_ref)):
+        total = None
+        for i in range(3):
+            w = lane_slice(wides[z][:, width:], i * toks, toks).astype(BF16)
+            val = across(w, rows)
+            total = val if total is None else total + val
+        outs[z][...] = total.astype(outs[z].dtype)
+
+
+def combine_kernel(cells, count, own_ref, x_ref, y_ref, d_ref, table_ref, top_ref, out_ref):
+    rows = jnp.concatenate([v.astype(F32) for v in gathered(cells, count, own_ref, x_ref, y_ref, d_ref)], axis=0)
+    total = top_ref[...].astype(F32)
+    for piece in pieces(table_ref[...]):
+        total += across(piece, rows.astype(BF16))
+    out_ref[...] = total.astype(BF16)
 
 
 def fetch_kernel(count, *refs):
-    ins, outs, sem = refs[:count], refs[count + 1 : 2 * count + 1], refs[2 * count + 1]
+    ins, outs, sem = refs[:count], refs[-count - 1 : -1], refs[-1]
     copies = [pltpu.make_async_copy(a, b, sem.at[i]) for i, (a, b) in enumerate(zip(ins, outs))]
     for c in copies:
         c.start()
@@ -150,20 +208,6 @@
         give_ref[:, pl.ds(at, step)] = val[rows:].astype(BF16)
 
     sweep(part, 0, keep_ref.shape[1], rows <= 128)
-
-
-def combine_kernel(scale_ref, *refs):
-    out_ref = refs[-1]
-    toks = scale_ref.shape[0]
-    s = scale_ref[...]
-    a = s.astype(BF16)
-    left = s - a.astype(F32)
-    b = left.astype(BF16)
-    c = (left - b.astype(F32)).astype(BF16)
-    pieces = jnp.concatenate([v.astype(F32) for v in (a, b, c)], axis=0).astype(BF16)
-    rows = jnp.concatenate([r[...].astype(F32) for r in refs[:-1]], axis=0).astype(BF16)
-    val = jnp.dot(pieces, rows, preferred_element_type=F32)
-    out_ref[...] = (val[:toks] + val[toks : 2 * toks] + val[2 * toks :]).astype(BF16)
 
 
 def per_device(
@@ -178,7 +222,6 @@
     high = slots // 2
     fw = w_gate.shape[1]
     my_slot = lax.axis_index("node") // members
-    near, far = range(high // 2), range(high // 2, high)
     rows = high // 2 * cells
     any_ref = pl.BlockSpec(memory_space=pl.ANY)
 
@@ -186,7 +229,7 @@
         return lax.ppermute(value, "node", [(d, d ^ flip) for d in range(devices)])
 
     def over_z(block, z):
-        return block if z == 0 else send(block, 2 * members * z)
+        return send(block, 2 * members * z)
 
     def split(blocks, when):
         return call(
@@ -196,6 +239,17 @@
             "split",
         )(*blocks, *when)
 
+    def fetch(arrays, when):
+        return call(
+            functools.partial(fetch_kernel, len(arrays)),
+            [shape(w.shape, w.dtype) for w in arrays],
+            [HBM] * len(arrays) + [any_ref] * len(when),
+            "fetch",
+            moved=sum(4 * w.size for w in arrays),
+            limit=40,
+            scratch=[pltpu.SemaphoreType.DMA((len(arrays),))],
+        )(*arrays, *when)
+
     def spread(own, oth):
         d, y, x = send(oth, members + 2), send(oth, members), send(own, 2)
         return own, x, y, d
@@ -208,34 +262,33 @@
             "join",
         )(*blocks, *when)[0]
 
+    half_z = high // 2
+    block = 2 * cells
+    lanes = -(-3 * toks // 128) * 128
     inputs = (expert_ids.T, gate_weights.T, replica_pick.T, placement[None, :], capacity[None, :], hidden_in)
     route = call(
-        functools.partial(route_kernel, cells, [(0, width)]),
-        [shape((2 * cells, width), BF16)] * high + [shape((slots * cells, toks), F32)],
+        functools.partial(route_kernel, cells, half_z),
+        [shape((block, width), BF16)] * half_z
+        + [shape((block, width + lanes), BF16)] * half_z
+        + [shape((half_z * block, toks), F32)],
         [SMEM] + [HBM] * 6,
         "route",
         limit=60,
         scratch=[pltpu.VMEM(a.shape, a.dtype) for a in inputs] + [pltpu.SemaphoreType.DMA((6,))],
     )(my_slot.reshape(1).astype(I32), *inputs)
-    scale = route[-1].T
-    near_z = [over_z(route[z], z) for z in near]
-    far_z = [over_z(route[z], z) for z in far]
-    near_own, near_oth = split(near_z, ())
-    near_rows = spread(near_own, near_oth)
-    far_own, far_oth = split(far_z, ())
-    far_rows = spread(far_own, far_oth)
-    near_all = join(near_rows, (far_own,))
+    near_tab = route[-1]
+    near_z = [over_z(route[z], z) for z in range(1, half_z)]
+    far_wide = [over_z(route[z], z) for z in range(half_z, high)]
+    (home,) = fetch([route[0]], ())
+    near_own, near_oth = split([home] + near_z, ())
+    near_got = spread(near_own, near_oth)
+    (wg,) = fetch([w_gate], (near_own,))
+    far_own, far_oth = split(far_wide, (wg,))
+    far_got = spread(far_own, far_oth)
+    near_all = join(near_got, (far_own,))
     near_core = send(near_all, 1)
-    wg, wu, wd = call(
-        functools.partial(fetch_kernel, 3),
-        [shape(w.shape, BF16) for w in (w_gate, w_up, w_down)],
-        [HBM] * 4,
-        "fetch",
-        moved=6 * w_gate.size * 2,
-        limit=40,
-        scratch=[pltpu.SemaphoreType.DMA((3,))],
-    )(w_gate, w_up, w_down, near_all)
-    far_all = join(far_rows, (wd,))
+    wu, wd = fetch([w_up, w_down], (near_all,))
+    far_all = join(far_got, (wd,))
     far_core = send(far_all, 1)
     far_hid, near_hid, _, _ = call(
         functools.partial(up_kernel, 8 * rows, 8 * rows),
@@ -262,29 +315,44 @@
             "half",
         )(keep, got, *when)
 
-    def merge(own, x, y, d):
+    def gather(own, x, y, d):
         dg, yg, xg = send(d, members + 2), send(y, members), send(x, 2)
-        return call(
-            functools.partial(merge_kernel, cells),
-            [shape((2 * cells, width), BF16)] * (high // 2),
-            [VMEM] * 4,
-            "merge",
-        )(own, xg, yg, dg)
+        return own, xg, yg, dg
 
     far_keep, far_give = down(far_hid, ())
-    far_got = send(far_give, 1)
+    far_sib = send(far_give, 1)
     near_keep, near_give = down(near_hid, ())
-    near_got = send(near_give, 1)
-    far_done = merge(*half(far_keep, far_got, ()))
-    far_back = [over_z(v, z) for v, z in zip(far_done, far)]
-    near_done = merge(*half(near_keep, near_got, (far_done[0],)))
-    near_back = [over_z(v, z) for v, z in zip(near_done, near)]
+    near_sib = send(near_give, 1)
+    far_half = half(far_keep, far_sib, ())
+    lent = call(
+        functools.partial(lend_kernel, cells),
+        [shape((4 * cells, width), F32)] + [shape((4 * cells, width), BF16)] * (half_z - 1),
+        [VMEM] * 2,
+        "lend",
+    )(near_keep, near_sib)
+    near_z = [lent[0]] + [over_z(lent[z], z) for z in range(1, half_z)]
+    far_sum = call(
+        functools.partial(weigh_kernel, cells, half_z),
+        [shape((toks, width), F32)] + [shape((toks, width), BF16)] * (half_z - 1),
+        [VMEM] * (4 + half_z),
+        "weigh",
+    )(*gather(*far_half), *far_wide)
+    near_half = call(
+        functools.partial(regroup_kernel, cells, half_z),
+        [shape((rows, width), F32)] + [shape((rows, width), BF16)] * 3,
+        [VMEM] * half_z + [any_ref],
+        "regroup",
+    )(*near_z, far_sum[0])
+    top_sum = far_sum[0]
+    for z in range(1, half_z):
+        top_sum = top_sum + over_z(far_sum[z], z).astype(F32)
+    top_back = over_z(top_sum.astype(BF16), half_z)
     (mixed,) = call(
-        combine_kernel,
+        functools.partial(combine_kernel, cells, half_z),
         [shape((toks, width), BF16)],
-        [VMEM] * (1 + high),
+        [VMEM] * 6,
         "combine",
-    )(scale, *near_back, *far_back)
+    )(*gather(*near_half), near_tab, top_back)
     return mixed
 
 

time: 58.3 us -> 56.8 us (0.974)
  local copies, waits for them, and re-layouts: 0.97 us -> 2.95 us
  waiting for transfers between devices: 17.4 us -> 15.5 us
  starting transfers between devices: 28.4 us -> 26.8 us
    unnamed x4 -> x8, local copies, waits for them, and re-layouts: 0.9 us -> 2.95 us
    ppermute x22, waiting for transfers between devices: 17.4 us -> 15.5 us  [send(): return lax.ppermute(value, 'node', [(d, d ^ flip) for d in range(devices)])]
    ppermute x22, starting transfers between devices: 28.4 us -> 26.8 us  [send(): return lax.ppermute(value, 'node', [(d, d ^ flip) for d in range(devices)])]
    pallas_call x5 -> x8, Pallas kernels: 7.64 us -> 7.56 us  [the longest x3 2.68 us: fetch(): call(functools.partial(fetch_kernel, len(arrays)), [shape(w.shape, w.dtyp...]
  transfers between devices with their start and end apart: 22 -> 22, of which waited for: 10 -> 11; matrix products, arithmetic and copies ran while one was open for 0% -> 0% of each run, Pallas kernels for 9% -> 9%
where the time goes in v5:
time: 56.8 us; the launch traced here: 56.6 us
  starting transfers between devices  26.8 us (47%)
  waiting for transfers between devices  15.5 us (27%)
  Pallas kernels  11.2 us (20%)
  local copies, waits for them, and re-layouts  2.95 us (5%)
    ppermute x22, starting transfers between devices, send(): return lax.ppermute(value, 'node', [(d, d ^ flip) for d in range(devices)])  26.8 us
    ppermute x22, waiting for transfers between devices, send(): return lax.ppermute(value, 'node', [(d, d ^ flip) for d in range(devices)])  15.5 us
    unnamed x8, local copies, waits for them, and re-layouts  2.95 us
    pallas_call x3, Pallas kernels, fetch(): call(functools.partial(fetch_kernel, len(arrays)), [shape(w.shape, w.dtyp...  2.68 us
    pallas_call x1, Pallas kernels, per_device(): call(functools.partial(route_kernel, cells, half_z), [shape((block, width...  2.33 us
    pallas_call x1, Pallas kernels, per_device(): call(functools.partial(up_kernel, 8 * rows, 8 * rows), [shape((8 * rows,...  1.82 us
    pallas_call x2, Pallas kernels, down(): call(down_kernel, [shape((4 * rows, width), F32), shape((4 * rows, width)...  1.5 us
    pallas_call x1, Pallas kernels, per_device(): call(functools.partial(weigh_kernel, cells, half_z), [shape((toks, width)...  1.28 us
  transfers between devices with their start and end apart: 22, of which 11 were waited for; matrix products, arithmetic and copies ran while one was open for 0% of the time, Pallas kernels for 9%

profile of v5, /device:TPU:0, one launch (start us, length us, event | category | flops | bytes accessed | tf_op | source)
XLA Modules:
  0.0 56.6 jit_solution(10245540900410074646)
XLA Ops:
  0.0 2.3 %route.1 = (bf16[8,7168]{1,0:T(8,128)(2,1)}, bf16[8,7168]{1,0:T(8,128)(2,1)}, bf16[8,7296]{1,0:T(8,128)(2,1)}, bf16[8,7296]{1,0:T(8,128)(2,1)}, f32[16,8]{1,0:T(8,128)}) custom-call(s32[1]{0:T(128)} %bitcast.slot_ref, s32[4,8]{1,0:T(4,128)} %bitcast.6, f32[4,8]{1,0:T(4,128)} %bitcast.7, s32[4,8]{1,0:T(4,128)} %bitcast.8, s32[1,8]{1,0:T(1,128)} %bitcast.9, ...), custom_call_target="tpu_custom_call" | custom-call | tf_op jit(solution)/shard_map/route/pallas_call | solution.py:269
  2.3 3.1 %collective-permute-start.2 = (bf16[8,7168]{1,0:T(8,128)(2,1)}, bf16[8,7168]{1,0:T(8,128)(2,1)S(1)}, u32[]{:S(2)}, u32[]{:S(2)}) collective-permute-start(bf16[8,7168]{1,0:T(8,128)(2,1)} %get-tuple-element.37), channel_id=1, source_target_pairs={{0,8},{1,9},{2,10},{3,11},{4,12},{5,13},{6,14},{7,15},{8,0},{9,1},... | collective-permute-start | bytes 344072 | tf_op jit(solution)/shard_map/ppermute | solution.py:229
  5.4 2.6 %collective-permute-start = (bf16[8,7296]{1,0:T(8,128)(2,1)}, bf16[8,7296]{1,0:T(8,128)(2,1)S(1)}, u32[]{:S(2)}, u32[]{:S(2)}) collective-permute-start(bf16[8,7296]{1,0:T(8,128)(2,1)} %get-tuple-element.34), channel_id=1, source_target_pairs={{0,16},{1,17},{2,18},{3,19},{4,20},{5,21},{6,22},{7,23},{8,24},{9,... | collective-permute-start | bytes 350216 | tf_op jit(solution)/shard_map/ppermute | solution.py:229
  8.0 0.0 collective-permute-start.1
  8.0 0.0 copy-start.2
  8.0 0.9 %copy-done.2 = bf16[8,7168]{1,0:T(8,128)(2,1)S(1)} copy-done((bf16[8,7168]{1,0:T(8,128)(2,1)S(1)}, bf16[8,7168]{1,0:T(8,128)(2,1)}, u32[]{:S(2)}) %copy-start.2) | copy-done | bytes 114712
  8.9 0.1 fetch.3.refs_0_
  9.1 0.0 collective-permute-done.2.refs_1_
  9.1 0.1 split.2
  9.1 3.6 %collective-permute-start.8 = (bf16[8,7168]{1,0:T(8,128)(2,1)S(1)}, bf16[8,7168]{1,0:T(8,128)(2,1)S(1)}, u32[]{:S(2)}, u32[]{:S(2)}) collective-permute-start(bf16[8,7168]{1,0:T(8,128)(2,1)S(1)} %get-tuple-element.41), channel_id=1, source_target_pairs={{0,6},{1,7},{2,4},{3,5},{4,2},{5,3},{6,0},{7,1},{8,14},{9,15},{10,... | collective-permute-start | bytes 344072 | tf_op jit(solution)/shard_map/ppermute | solution.py:229
  12.8 0.5 collective-permute-start.7
  13.3 0.1 collective-permute-start.6
  13.4 2.0 %copy-done = bf16[7168,256]{1,0:T(8,128)(2,1)S(1)} copy-done((bf16[7168,256]{1,0:T(8,128)(2,1)S(1)}, bf16[7168,256]{1,0:T(8,128)(2,1)}, u32[]{:S(2)}) %copy-start) | copy-done | bytes 3670040
  15.5 0.3 fetch.4.refs_2_.refs_4_
  15.7 0.0 copy-start.1
  15.7 1.7 %collective-permute-done.refs_0_ = bf16[8,7296]{1,0:T(8,128)(2,1)S(1)} collective-permute-done((bf16[8,7296]{1,0:T(8,128)(2,1)}, bf16[8,7296]{1,0:T(8,128)(2,1)S(1)}, u32[]{:S(2)}, u32[]{:S(2)}) %collective-permute-start) | collective-permute-done | bytes 116768 | tf_op jit(solution)/shard_map/ppermute | solution.py:229
  17.5 0.0 collective-permute-done.1.refs_1_
  17.5 0.1 split.3
  17.6 2.5 %collective-permute-start.5 = (bf16[8,7168]{1,0:T(8,128)(2,1)S(1)}, bf16[8,7168]{1,0:T(8,128)(2,1)S(1)}, u32[]{:S(2)}, u32[]{:S(2)}) collective-permute-start(bf16[8,7168]{1,0:T(8,128)(2,1)S(1)} %get-tuple-element.40), channel_id=1, source_target_pairs={{0,6},{1,7},{2,4},{3,5},{4,2},{5,3},{6,0},{7,1},{8,14},{9,15},{10,... | collective-permute-start | bytes 344072 | tf_op jit(solution)/shard_map/ppermute | solution.py:229
  20.1 0.5 collective-permute-start.4
  20.6 0.0 collective-permute-done.8.refs_3_
  20.6 0.5 collective-permute-start.3
  21.1 0.0 collective-permute-done.7.refs_2_
  21.1 0.0 collective-permute-done.6.refs_1_
  21.2 0.1 collective-permute-start.10
  21.2 0.0 copy-done.1
  21.3 2.3 %fetch.5 = (bf16[7168,256]{1,0:T(8,128)(2,1)S(1)}, bf16[256,7168]{1,0:T(8,128)(2,1)S(1)}) custom-call(bf16[7168,256]{1,0:T(8,128)(2,1)S(1)} %copy-done.1, bf16[256,7168]{1,0:T(8,128)(2,1)} %refs_1_.1, bf16[32,7168]{1,0:T(8,128)(2,1)S(1)} %join.2.refs_2_), custom_call_target="tpu_custom_call" | custom-call | bytes 14680064 | tf_op jit(solution)/shard_map/fetch/pallas_call | solution.py:243
  23.6 0.0 collective-permute-done.5.refs_3_
  23.6 1.3 %collective-permute-done.4.refs_2_ = bf16[8,7168]{1,0:T(8,128)(2,1)S(1)} collective-permute-done((bf16[8,7168]{1,0:T(8,128)(2,1)S(1)}, bf16[8,7168]{1,0:T(8,128)(2,1)S(1)}, u32[]{:S(2)}, u32[]{:S(2)}) %collective-permute-start.4) | collective-permute-done | bytes 114720 | tf_op jit(solution)/shard_map/ppermute | solution.py:229
  24.9 0.5 collective-permute-done.3.refs_1_
  25.4 0.1 collective-permute-start.9
  25.5 0.0 collective-permute-done.10.refs_3_
  25.5 1.8 %collective-permute-done.9.refs_1_ = bf16[32,7168]{1,0:T(8,128)(2,1)S(1)} collective-permute-done((bf16[32,7168]{1,0:T(8,128)(2,1)S(1)}, bf16[32,7168]{1,0:T(8,128)(2,1)S(1)}, u32[]{:S(2)}, u32[]{:S(2)}) %collective-permute-start.9) | collective-permute-done | bytes 458784 | tf_op jit(solution)/shard_map/ppermute | solution.py:229
  27.3 1.8 %up.1 = (bf16[64,256]{1,0:T(8,128)(2,1)S(1)}, bf16[64,256]{1,0:T(8,128)(2,1)S(1)}, f32[128,256]{1,0:T(8,128)}, f32[128,256]{1,0:T(8,128)}) custom-call(bf16[32,7168]{1,0:T(8,128)(2,1)S(1)} %join.3.refs_0_, bf16[32,7168]{1,0:T(8,128)(2,1)S(1)} %collective-permute-done.9.refs_1_, bf16[32,7168]{1,0:T(8,128)(2,1)S(1)} %join.2.refs_2_, ...), custom_call_target="tpu_custom_call" | custom-call | flops 939524096 | tf_op jit(solution)/shard_map/up/pallas_call | solution.py:293
  29.1 0.7 %down.2 = (f32[32,7168]{1,0:T(8,128)S(1)}, bf16[32,7168]{1,0:T(8,128)(2,1)S(1)}) custom-call(bf16[64,256]{1,0:T(8,128)(2,1)S(1)} %get-tuple-element.44.hid_ref, bf16[256,7168]{1,0:T(8,128)(2,1)S(1)} %get-tuple-element.42.refs_4_.down_ref), custom_call_target="tpu_custom_call" | custom-call | flops 234881024 | tf_op jit(solution)/shard_map/down/pallas_call | solution.py:302
  29.9 0.2 collective-permute-start.11
  30.1 0.7 %down.3 = (f32[32,7168]{1,0:T(8,128)S(1)}, bf16[32,7168]{1,0:T(8,128)(2,1)S(1)}) custom-call(bf16[64,256]{1,0:T(8,128)(2,1)S(1)} %get-tuple-element.49.hid_ref, bf16[256,7168]{1,0:T(8,128)(2,1)S(1)} %get-tuple-element.42.refs_4_.down_ref), custom_call_target="tpu_custom_call" | custom-call | flops 234881024 | tf_op jit(solution)/shard_map/down/pallas_call | solution.py:302
  30.8 0.4 collective-permute-start.13
  31.3 0.5 collective-permute-done.11.core_ref
  31.8 0.1 lend.1
  31.9 1.9 %collective-permute-start.12 = (bf16[16,7168]{1,0:T(8,128)(2,1)S(1)}, bf16[16,7168]{1,0:T(8,128)(2,1)S(1)}, u32[]{:S(2)}, u32[]{:S(2)}) collective-permute-start(bf16[16,7168]{1,0:T(8,128)(2,1)S(1)} %get-tuple-element.48), channel_id=1, source_target_pairs={{0,8},{1,9},{2,10},{3,11},{4,12},{5,13},{6,14},{7,15},{8,0},{9,1},... | collective-permute-start | bytes 688136 | tf_op jit(solution)/shard_map/ppermute | solution.py:229
  33.8 0.0 collective-permute-done.13.core_ref
  33.8 0.1 half.1
  33.9 1.1 %collective-permute-start.14 = (bf16[8,7168]{1,0:T(8,128)(2,1)S(1)}, bf16[8,7168]{1,0:T(8,128)(2,1)S(1)}, u32[]{:S(2)}, u32[]{:S(2)}) collective-permute-start(bf16[8,7168]{1,0:T(8,128)(2,1)S(1)} %get-tuple-element.53), channel_id=1, source_target_pairs={{0,2},{1,3},{2,0},{3,1},{4,6},{5,7},{6,4},{7,5},{8,10},{9,11},{10,... | collective-permute-start | bytes 344072 | tf_op jit(solution)/shard_map/ppermute | solution.py:229
  34.9 1.1 %collective-permute-start.15 = (bf16[8,7168]{1,0:T(8,128)(2,1)S(1)}, bf16[8,7168]{1,0:T(8,128)(2,1)S(1)}, u32[]{:S(2)}, u32[]{:S(2)}) collective-permute-start(bf16[8,7168]{1,0:T(8,128)(2,1)S(1)} %get-tuple-element.54), channel_id=1, source_target_pairs={{0,4},{1,5},{2,6},{3,7},{4,0},{5,1},{6,2},{7,3},{8,12},{9,13},{10,... | collective-permute-start | bytes 344072 | tf_op jit(solution)/shard_map/ppermute | solution.py:229
  36.0 1.4 %collective-permute-start.16 = (bf16[8,7168]{1,0:T(8,128)(2,1)S(1)}, bf16[8,7168]{1,0:T(8,128)(2,1)S(1)}, u32[]{:S(2)}, u32[]{:S(2)}) collective-permute-start(bf16[8,7168]{1,0:T(8,128)(2,1)S(1)} %get-tuple-element.55), channel_id=1, source_target_pairs={{0,6},{1,7},{2,4},{3,5},{4,2},{5,3},{6,0},{7,1},{8,14},{9,15},{10,... | collective-permute-start | bytes 344072 | tf_op jit(solution)/shard_map/ppermute | solution.py:229
  37.4 2.0 %collective-permute-done.14.x_ref = bf16[8,7168]{1,0:T(8,128)(2,1)S(1)} collective-permute-done((bf16[8,7168]{1,0:T(8,128)(2,1)S(1)}, bf16[8,7168]{1,0:T(8,128)(2,1)S(1)}, u32[]{:S(2)}, u32[]{:S(2)}) %collective-permute-start.14) | collective-permute-done | bytes 114720 | tf_op jit(solution)/shard_map/ppermute | solution.py:229
  39.4 1.4 %collective-permute-done.15.y_ref = bf16[8,7168]{1,0:T(8,128)(2,1)S(1)} collective-permute-done((bf16[8,7168]{1,0:T(8,128)(2,1)S(1)}, bf16[8,7168]{1,0:T(8,128)(2,1)S(1)}, u32[]{:S(2)}, u32[]{:S(2)}) %collective-permute-start.15) | collective-permute-done | bytes 114720 | tf_op jit(solution)/shard_map/ppermute | solution.py:229
  40.8 1.5 %collective-permute-done.16.d_ref = bf16[8,7168]{1,0:T(8,128)(2,1)S(1)} collective-permute-done((bf16[8,7168]{1,0:T(8,128)(2,1)S(1)}, bf16[8,7168]{1,0:T(8,128)(2,1)S(1)}, u32[]{:S(2)}, u32[]{:S(2)}) %collective-permute-start.16) | collective-permute-done | bytes 114720 | tf_op jit(solution)/shard_map/ppermute | solution.py:229
  42.2 1.3 %weigh.1 = (f32[8,7168]{1,0:T(8,128)S(1)}, bf16[8,7168]{1,0:T(8,128)(2,1)S(1)}) custom-call(f32[8,7168]{1,0:T(8,128)S(1)} %get-tuple-element.52.own_ref, bf16[8,7168]{1,0:T(8,128)(2,1)S(1)} %collective-permute-done.14.x_ref, bf16[8,7168]{1,0:T(8,128)(2,1)S(1)} %collective-permute-done.15.y_ref, bf16[8,7168]{1,0:T(8,128)(2,1)S(1)} %collective-permute-done.16.d_ref, ...), custom_call_target="tpu_custom_call" | custom-call | tf_op jit(solution)/shard_map/weigh/pallas_call | solution.py:334
  43.5 1.3 %collective-permute-start.20 = (bf16[8,7168]{1,0:T(8,128)(2,1)S(1)}, bf16[8,7168]{1,0:T(8,128)(2,1)S(1)}, u32[]{:S(2)}, u32[]{:S(2)}) collective-permute-start(bf16[8,7168]{1,0:T(8,128)(2,1)S(1)} %get-tuple-element.62), channel_id=1, source_target_pairs={{0,8},{1,9},{2,10},{3,11},{4,12},{5,13},{6,14},{7,15},{8,0},{9,1},... | collective-permute-start | bytes 344072 | tf_op jit(solution)/shard_map/ppermute | solution.py:229
  44.9 0.0 collective-permute-done.12.refs_1_
  44.9 0.1 regroup.1
  45.0 0.9 %collective-permute-start.17 = (bf16[8,7168]{1,0:T(8,128)(2,1)S(1)}, bf16[8,7168]{1,0:T(8,128)(2,1)S(1)}, u32[]{:S(2)}, u32[]{:S(2)}) collective-permute-start(bf16[8,7168]{1,0:T(8,128)(2,1)S(1)} %get-tuple-element.58), channel_id=1, source_target_pairs={{0,2},{1,3},{2,0},{3,1},{4,6},{5,7},{6,4},{7,5},{8,10},{9,11},{10,... | collective-permute-start | bytes 344072 | tf_op jit(solution)/shard_map/ppermute | solution.py:229
  45.9 1.5 %collective-permute-start.18 = (bf16[8,7168]{1,0:T(8,128)(2,1)S(1)}, bf16[8,7168]{1,0:T(8,128)(2,1)S(1)}, u32[]{:S(2)}, u32[]{:S(2)}) collective-permute-start(bf16[8,7168]{1,0:T(8,128)(2,1)S(1)} %get-tuple-element.59), channel_id=1, source_target_pairs={{0,4},{1,5},{2,6},{3,7},{4,0},{5,1},{6,2},{7,3},{8,12},{9,13},{10,... | collective-permute-start | bytes 344072 | tf_op jit(solution)/shard_map/ppermute | solution.py:229
  47.4 1.2 %collective-permute-start.19 = (bf16[8,7168]{1,0:T(8,128)(2,1)S(1)}, bf16[8,7168]{1,0:T(8,128)(2,1)S(1)}, u32[]{:S(2)}, u32[]{:S(2)}) collective-permute-start(bf16[8,7168]{1,0:T(8,128)(2,1)S(1)} %get-tuple-element.60), channel_id=1, source_target_pairs={{0,6},{1,7},{2,4},{3,5},{4,2},{5,3},{6,0},{7,1},{8,14},{9,15},{10,... | collective-permute-start | bytes 344072 | tf_op jit(solution)/shard_map/ppermute | solution.py:229
  48.5 0.0 collective-permute-done.20
  48.6 2.2 %collective-permute-start.21 = (bf16[8,7168]{1,0:T(8,128)(2,1)S(1)}, bf16[8,7168]{1,0:T(8,128)(2,1)S(1)}, u32[]{:S(2)}, u32[]{:S(2)}) collective-permute-start(bf16[8,7168]{1,0:T(8,128)(2,1)S(1)} %add_convert_fusion), channel_id=1, source_target_pairs={{0,16},{1,17},{2,18},{3,19},{4,20},{5,21},{6,22},{7,23},{8,24},{9,... | collective-permute-start | bytes 344072 | tf_op jit(solution)/shard_map/ppermute | solution.py:229
  50.8 0.0 collective-permute-done.17.x_ref
  50.8 0.7 %collective-permute-done.18.y_ref = bf16[8,7168]{1,0:T(8,128)(2,1)S(1)} collective-permute-done((bf16[8,7168]{1,0:T(8,128)(2,1)S(1)}, bf16[8,7168]{1,0:T(8,128)(2,1)S(1)}, u32[]{:S(2)}, u32[]{:S(2)}) %collective-permute-start.18) | collective-permute-done | bytes 114720 | tf_op jit(solution)/shard_map/ppermute | solution.py:229
  51.4 1.6 %collective-permute-done.19.d_ref = bf16[8,7168]{1,0:T(8,128)(2,1)S(1)} collective-permute-done((bf16[8,7168]{1,0:T(8,128)(2,1)S(1)}, bf16[8,7168]{1,0:T(8,128)(2,1)S(1)}, u32[]{:S(2)}, u32[]{:S(2)}) %collective-permute-start.19) | collective-permute-done | bytes 114720 | tf_op jit(solution)/shard_map/ppermute | solution.py:229
  53.1 2.5 %collective-permute-done.21.top_ref = bf16[8,7168]{1,0:T(8,128)(2,1)S(1)} collective-permute-done((bf16[8,7168]{1,0:T(8,128)(2,1)S(1)}, bf16[8,7168]{1,0:T(8,128)(2,1)S(1)}, u32[]{:S(2)}, u32[]{:S(2)}) %collective-permute-start.21) | collective-permute-done | bytes 114720 | tf_op jit(solution)/shard_map/ppermute | solution.py:229
  55.6 0.0 copy-done.3
  55.6 1.0 %combine.1 = bf16[8,7168]{1,0:T(8,128)(2,1)} custom-call(f32[8,7168]{1,0:T(8,128)S(1)} %get-tuple-element.57.own_ref, bf16[8,7168]{1,0:T(8,128)(2,1)S(1)} %collective-permute-done.17.x_ref, bf16[8,7168]{1,0:T(8,128)(2,1)S(1)} %collective-permute-done.18.y_ref, bf16[8,7168]{1,0:T(8,128)(2,1)S(1)} %collective-permute-done.19.d_ref, f32[16,8]{1,0:T(8,128)S(1)} %copy-done.3, ...), custom_call_target="tpu_custom_call" | custom-call | tf_op jit(solution)/shard_map/combine/pallas_call | solution.py:350
  (5 shorter events, 0.1 us)
Async XLA Ops:
  2.3 6.7 %collective-permute-start.2 = (bf16[8,7168]{1,0:T(8,128)(2,1)}, bf16[8,7168]{1,0:T(8,128)(2,1)S(1)}, u32[]{:S(2)}, u32[]{:S(2)}) collective-permute-start(bf16[8,7168]{1,0:T(8,128)(2,1)} %get-tuple-element.37), channel_id=1, source_target_pairs={{0,8},{1,9},{2,10},{3,11},{4,12},{5,13},{6,14},{7,15},{8,0},{9,1},... | collective-permute-start | bytes 344072 | tf_op jit(solution)/shard_map/ppermute | solution.py:229
  5.4 12.1 %collective-permute-start = (bf16[8,7296]{1,0:T(8,128)(2,1)}, bf16[8,7296]{1,0:T(8,128)(2,1)S(1)}, u32[]{:S(2)}, u32[]{:S(2)}) collective-permute-start(bf16[8,7296]{1,0:T(8,128)(2,1)} %get-tuple-element.34), channel_id=1, source_target_pairs={{0,16},{1,17},{2,18},{3,19},{4,20},{5,21},{6,22},{7,23},{8,24},{9,... | collective-permute-start | bytes 350216 | tf_op jit(solution)/shard_map/ppermute | solution.py:229
  8.0 9.5 %collective-permute-start.1 = (bf16[8,7296]{1,0:T(8,128)(2,1)}, bf16[8,7296]{1,0:T(8,128)(2,1)S(1)}, u32[]{:S(2)}, u32[]{:S(2)}) collective-permute-start(bf16[8,7296]{1,0:T(8,128)(2,1)} %get-tuple-element.35), channel_id=1, source_target_pairs={{0,24},{1,25},{2,26},{3,27},{4,28},{5,29},{6,30},{7,31},{8,16},{9,... | collective-permute-start | bytes 350216 | tf_op jit(solution)/shard_map/ppermute | solution.py:229
  8.0 0.9 %copy-start.2 = (bf16[8,7168]{1,0:T(8,128)(2,1)S(1)}, bf16[8,7168]{1,0:T(8,128)(2,1)}, u32[]{:S(2)}) copy-start(bf16[8,7168]{1,0:T(8,128)(2,1)} %get-tuple-element.36.refs_0_) | copy-start | bytes 344068
  9.1 11.5 %collective-permute-start.8 = (bf16[8,7168]{1,0:T(8,128)(2,1)S(1)}, bf16[8,7168]{1,0:T(8,128)(2,1)S(1)}, u32[]{:S(2)}, u32[]{:S(2)}) collective-permute-start(bf16[8,7168]{1,0:T(8,128)(2,1)S(1)} %get-tuple-element.41), channel_id=1, source_target_pairs={{0,6},{1,7},{2,4},{3,5},{4,2},{5,3},{6,0},{7,1},{8,14},{9,15},{10,... | collective-permute-start | bytes 344072 | tf_op jit(solution)/shard_map/ppermute | solution.py:229
  12.8 8.3 %collective-permute-start.7 = (bf16[8,7168]{1,0:T(8,128)(2,1)S(1)}, bf16[8,7168]{1,0:T(8,128)(2,1)S(1)}, u32[]{:S(2)}, u32[]{:S(2)}) collective-permute-start(bf16[8,7168]{1,0:T(8,128)(2,1)S(1)} %get-tuple-element.41), channel_id=1, source_target_pairs={{0,4},{1,5},{2,6},{3,7},{4,0},{5,1},{6,2},{7,3},{8,12},{9,13},{10,... | collective-permute-start | bytes 344072 | tf_op jit(solution)/shard_map/ppermute | solution.py:229
  13.3 7.8 %collective-permute-start.6 = (bf16[8,7168]{1,0:T(8,128)(2,1)S(1)}, bf16[8,7168]{1,0:T(8,128)(2,1)S(1)}, u32[]{:S(2)}, u32[]{:S(2)}) collective-permute-start(bf16[8,7168]{1,0:T(8,128)(2,1)S(1)} %get-tuple-element.38.refs_1_.refs_0_), channel_id=1, source_target_pairs={{0,2},{1,3},{2,0},{3,1},{4,6},{5,7},{6,4},{7,5},{8,10},{9,11},{10,... | collective-permute-start | bytes 344072 | tf_op jit(solution)/shard_map/ppermute | solution.py:229
  13.4 2.0 %copy-start = (bf16[7168,256]{1,0:T(8,128)(2,1)S(1)}, bf16[7168,256]{1,0:T(8,128)(2,1)}, u32[]{:S(2)}) copy-start(bf16[7168,256]{1,0:T(8,128)(2,1)} %refs_0_.2) | copy-start | bytes 11010052
  15.7 5.5 %copy-start.1 = (bf16[7168,256]{1,0:T(8,128)(2,1)S(1)}, bf16[7168,256]{1,0:T(8,128)(2,1)}, u32[]{:S(2)}) copy-start(bf16[7168,256]{1,0:T(8,128)(2,1)} %refs_0_.3) | copy-start | bytes 11010052
  17.6 6.0 %collective-permute-start.5 = (bf16[8,7168]{1,0:T(8,128)(2,1)S(1)}, bf16[8,7168]{1,0:T(8,128)(2,1)S(1)}, u32[]{:S(2)}, u32[]{:S(2)}) collective-permute-start(bf16[8,7168]{1,0:T(8,128)(2,1)S(1)} %get-tuple-element.40), channel_id=1, source_target_pairs={{0,6},{1,7},{2,4},{3,5},{4,2},{5,3},{6,0},{7,1},{8,14},{9,15},{10,... | collective-permute-start | bytes 344072 | tf_op jit(solution)/shard_map/ppermute | solution.py:229
  20.1 4.8 %collective-permute-start.4 = (bf16[8,7168]{1,0:T(8,128)(2,1)S(1)}, bf16[8,7168]{1,0:T(8,128)(2,1)S(1)}, u32[]{:S(2)}, u32[]{:S(2)}) collective-permute-start(bf16[8,7168]{1,0:T(8,128)(2,1)S(1)} %get-tuple-element.40), channel_id=1, source_target_pairs={{0,4},{1,5},{2,6},{3,7},{4,0},{5,1},{6,2},{7,3},{8,12},{9,13},{10,... | collective-permute-start | bytes 344072 | tf_op jit(solution)/shard_map/ppermute | solution.py:229
  20.6 4.8 %collective-permute-start.3 = (bf16[8,7168]{1,0:T(8,128)(2,1)S(1)}, bf16[8,7168]{1,0:T(8,128)(2,1)S(1)}, u32[]{:S(2)}, u32[]{:S(2)}) collective-permute-start(bf16[8,7168]{1,0:T(8,128)(2,1)S(1)} %get-tuple-element.39.refs_4_.refs_0_), channel_id=1, source_target_pairs={{0,2},{1,3},{2,0},{3,1},{4,6},{5,7},{6,4},{7,5},{8,10},{9,11},{10,... | collective-permute-start | bytes 344072 | tf_op jit(solution)/shard_map/ppermute | solution.py:229
  21.2 4.3 %collective-permute-start.10 = (bf16[32,7168]{1,0:T(8,128)(2,1)S(1)}, bf16[32,7168]{1,0:T(8,128)(2,1)S(1)}, u32[]{:S(2)}, u32[]{:S(2)}) collective-permute-start(bf16[32,7168]{1,0:T(8,128)(2,1)S(1)} %join.2.refs_2_), channel_id=1, source_target_pairs={{0,1},{1,0},{2,3},{3,2},{4,5},{5,4},{6,7},{7,6},{8,9},{9,8},{10,11... | collective-permute-start | bytes 1376264 | tf_op jit(solution)/shard_map/ppermute | solution.py:229
  25.4 1.9 %collective-permute-start.9 = (bf16[32,7168]{1,0:T(8,128)(2,1)S(1)}, bf16[32,7168]{1,0:T(8,128)(2,1)S(1)}, u32[]{:S(2)}, u32[]{:S(2)}) collective-permute-start(bf16[32,7168]{1,0:T(8,128)(2,1)S(1)} %join.3.refs_0_), channel_id=1, source_target_pairs={{0,1},{1,0},{2,3},{3,2},{4,5},{5,4},{6,7},{7,6},{8,9},{9,8},{10,11... | collective-permute-start | bytes 1376264 | tf_op jit(solution)/shard_map/ppermute | solution.py:229
  29.9 1.9 %collective-permute-start.11 = (bf16[32,7168]{1,0:T(8,128)(2,1)S(1)}, bf16[32,7168]{1,0:T(8,128)(2,1)S(1)}, u32[]{:S(2)}, u32[]{:S(2)}) collective-permute-start(bf16[32,7168]{1,0:T(8,128)(2,1)S(1)} %get-tuple-element.46), channel_id=1, source_target_pairs={{0,1},{1,0},{2,3},{3,2},{4,5},{5,4},{6,7},{7,6},{8,9},{9,8},{10,11... | collective-permute-start | bytes 1376264 | tf_op jit(solution)/shard_map/ppermute | solution.py:229
  30.1 25.5 %copy-start.3 = (f32[16,8]{1,0:T(8,128)S(1)}, f32[16,8]{1,0:T(8,128)}, u32[]{:S(2)}) copy-start(f32[16,8]{1,0:T(8,128)} %get-tuple-element.61.table_ref) | copy-start | bytes 1540
  30.8 2.9 %collective-permute-start.13 = (bf16[32,7168]{1,0:T(8,128)(2,1)S(1)}, bf16[32,7168]{1,0:T(8,128)(2,1)S(1)}, u32[]{:S(2)}, u32[]{:S(2)}) collective-permute-start(bf16[32,7168]{1,0:T(8,128)(2,1)S(1)} %get-tuple-element.51), channel_id=1, source_target_pairs={{0,1},{1,0},{2,3},{3,2},{4,5},{5,4},{6,7},{7,6},{8,9},{9,8},{10,11... | collective-permute-start | bytes 1376264 | tf_op jit(solution)/shard_map/ppermute | solution.py:229
  31.9 13.0 %collective-permute-start.12 = (bf16[16,7168]{1,0:T(8,128)(2,1)S(1)}, bf16[16,7168]{1,0:T(8,128)(2,1)S(1)}, u32[]{:S(2)}, u32[]{:S(2)}) collective-permute-start(bf16[16,7168]{1,0:T(8,128)(2,1)S(1)} %get-tuple-element.48), channel_id=1, source_target_pairs={{0,8},{1,9},{2,10},{3,11},{4,12},{5,13},{6,14},{7,15},{8,0},{9,1},... | collective-permute-start | bytes 688136 | tf_op jit(solution)/shard_map/ppermute | solution.py:229
  33.9 5.6 %collective-permute-start.14 = (bf16[8,7168]{1,0:T(8,128)(2,1)S(1)}, bf16[8,7168]{1,0:T(8,128)(2,1)S(1)}, u32[]{:S(2)}, u32[]{:S(2)}) collective-permute-start(bf16[8,7168]{1,0:T(8,128)(2,1)S(1)} %get-tuple-element.53), channel_id=1, source_target_pairs={{0,2},{1,3},{2,0},{3,1},{4,6},{5,7},{6,4},{7,5},{8,10},{9,11},{10,... | collective-permute-start | bytes 344072 | tf_op jit(solution)/shard_map/ppermute | solution.py:229
  34.9 5.9 %collective-permute-start.15 = (bf16[8,7168]{1,0:T(8,128)(2,1)S(1)}, bf16[8,7168]{1,0:T(8,128)(2,1)S(1)}, u32[]{:S(2)}, u32[]{:S(2)}) collective-permute-start(bf16[8,7168]{1,0:T(8,128)(2,1)S(1)} %get-tuple-element.54), channel_id=1, source_target_pairs={{0,4},{1,5},{2,6},{3,7},{4,0},{5,1},{6,2},{7,3},{8,12},{9,13},{10,... | collective-permute-start | bytes 344072 | tf_op jit(solution)/shard_map/ppermute | solution.py:229
  36.0 6.3 %collective-permute-start.16 = (bf16[8,7168]{1,0:T(8,128)(2,1)S(1)}, bf16[8,7168]{1,0:T(8,128)(2,1)S(1)}, u32[]{:S(2)}, u32[]{:S(2)}) collective-permute-start(bf16[8,7168]{1,0:T(8,128)(2,1)S(1)} %get-tuple-element.55), channel_id=1, source_target_pairs={{0,6},{1,7},{2,4},{3,5},{4,2},{5,3},{6,0},{7,1},{8,14},{9,15},{10,... | collective-permute-start | bytes 344072 | tf_op jit(solution)/shard_map/ppermute | solution.py:229
  43.5 5.0 %collective-permute-start.20 = (bf16[8,7168]{1,0:T(8,128)(2,1)S(1)}, bf16[8,7168]{1,0:T(8,128)(2,1)S(1)}, u32[]{:S(2)}, u32[]{:S(2)}) collective-permute-start(bf16[8,7168]{1,0:T(8,128)(2,1)S(1)} %get-tuple-element.62), channel_id=1, source_target_pairs={{0,8},{1,9},{2,10},{3,11},{4,12},{5,13},{6,14},{7,15},{8,0},{9,1},... | collective-permute-start | bytes 344072 | tf_op jit(solution)/shard_map/ppermute | solution.py:229
  45.0 5.8 %collective-permute-start.17 = (bf16[8,7168]{1,0:T(8,128)(2,1)S(1)}, bf16[8,7168]{1,0:T(8,128)(2,1)S(1)}, u32[]{:S(2)}, u32[]{:S(2)}) collective-permute-start(bf16[8,7168]{1,0:T(8,128)(2,1)S(1)} %get-tuple-element.58), channel_id=1, source_target_pairs={{0,2},{1,3},{2,0},{3,1},{4,6},{5,7},{6,4},{7,5},{8,10},{9,11},{10,... | collective-permute-start | bytes 344072 | tf_op jit(solution)/shard_map/ppermute | solution.py:229
  45.9 5.6 %collective-permute-start.18 = (bf16[8,7168]{1,0:T(8,128)(2,1)S(1)}, bf16[8,7168]{1,0:T(8,128)(2,1)S(1)}, u32[]{:S(2)}, u32[]{:S(2)}) collective-permute-start(bf16[8,7168]{1,0:T(8,128)(2,1)S(1)} %get-tuple-element.59), channel_id=1, source_target_pairs={{0,4},{1,5},{2,6},{3,7},{4,0},{5,1},{6,2},{7,3},{8,12},{9,13},{10,... | collective-permute-start | bytes 344072 | tf_op jit(solution)/shard_map/ppermute | solution.py:229
  47.4 5.7 %collective-permute-start.19 = (bf16[8,7168]{1,0:T(8,128)(2,1)S(1)}, bf16[8,7168]{1,0:T(8,128)(2,1)S(1)}, u32[]{:S(2)}, u32[]{:S(2)}) collective-permute-start(bf16[8,7168]{1,0:T(8,128)(2,1)S(1)} %get-tuple-element.60), channel_id=1, source_target_pairs={{0,6},{1,7},{2,4},{3,5},{4,2},{5,3},{6,0},{7,1},{8,14},{9,15},{10,... | collective-permute-start | bytes 344072 | tf_op jit(solution)/shard_map/ppermute | solution.py:229
  48.6 7.0 %collective-permute-start.21 = (bf16[8,7168]{1,0:T(8,128)(2,1)S(1)}, bf16[8,7168]{1,0:T(8,128)(2,1)S(1)}, u32[]{:S(2)}, u32[]{:S(2)}) collective-permute-start(bf16[8,7168]{1,0:T(8,128)(2,1)S(1)} %add_convert_fusion), channel_id=1, source_target_pairs={{0,16},{1,17},{2,18},{3,19},{4,20},{5,21},{6,22},{7,23},{8,24},{9,... | collective-permute-start | bytes 344072 | tf_op jit(solution)/shard_map/ppermute | solution.py:229

commit v6 on v5

--- a/solution.py
+++ b/solution.py
@@ -39,12 +39,6 @@
 
 def across(left, right):
     return lax.dot_general(left, right, (((0,), (0,)), ((), ())), preferred_element_type=F32)
-
-
-def lane_slice(tail, start, count):
-    lanes = tail.shape[1]
-    place = lax.broadcasted_iota(I32, (lanes, count), 0) == lax.broadcasted_iota(I32, (lanes, count), 1) + start
-    return jnp.dot(tail, jnp.where(place, 1.0, 0.0).astype(BF16), preferred_element_type=F32)
 
 
 def sweep(part, base, width, unrolled):
@@ -98,7 +92,9 @@
     table = jnp.where(spot, weight, 0.0)
     block = 2 * cells
     width = rows_ref.shape[1]
-    outs[-1][...] = table[: count * block]
+    n = count * block
+    eye = jnp.where(lax.broadcasted_iota(I32, (n, n), 0) == lax.broadcasted_iota(I32, (n, n), 1), 1.0, 0.0).astype(BF16)
+    outs[-1][...] = jnp.concatenate([across(piece, eye) for piece in pieces(table[:n])], axis=0)
     packed = jnp.dot(spot.astype(F32).astype(BF16), rows_ref[...], preferred_element_type=F32)
     for z, out in enumerate(outs[:-1]):
         part = slice(z * block, (z + 1) * block)
@@ -146,6 +142,11 @@
         out[...] = jnp.concatenate([v[b * cells : (b + 1) * cells] for v in vals], axis=0).astype(out.dtype)
 
 
+def weighted(weights, groups):
+    rows = jnp.concatenate([g.astype(F32) for g in groups], axis=0).astype(BF16)
+    return jnp.dot(weights.astype(BF16), rows, preferred_element_type=F32)
+
+
 def gathered(cells, count, own_ref, x_ref, y_ref, d_ref):
     own = own_ref[...] + x_ref[...].astype(F32)
     oth = y_ref[...].astype(F32) + d_ref[...].astype(F32)
@@ -155,22 +156,23 @@
 
 def weigh_kernel(cells, count, own_ref, x_ref, y_ref, d_ref, *refs):
     wides, outs = refs[:count], refs[-count:]
-    width, toks = own_ref.shape[1], outs[0].shape[0]
-    for z, rows in enumerate(gathered(cells, count, own_ref, x_ref, y_ref, d_ref)):
-        total = None
-        for i in range(3):
-            w = lane_slice(wides[z][:, width:], i * toks, toks).astype(BF16)
-            val = across(w, rows)
-            total = val if total is None else total + val
-        outs[z][...] = total.astype(outs[z].dtype)
+    width, toks, block = own_ref.shape[1], outs[0].shape[0], 2 * cells
+    left = []
+    for z, wide in enumerate(wides):
+        place = lax.broadcasted_iota(I32, (block, count * block), 1) - lax.broadcasted_iota(I32, (block, count * block), 0)
+        shift = jnp.where(place == z * block, 1.0, 0.0).astype(BF16)
+        left.append(across(wide[:, width:], shift)[: 3 * toks])
+    val = weighted(jnp.concatenate(left, axis=0), gathered(cells, count, own_ref, x_ref, y_ref, d_ref))
+    for z, out in enumerate(outs):
+        a, b, c = (val[(3 * z + i) * toks : (3 * z + i + 1) * toks] for i in range(3))
+        out[...] = (a + b + c).astype(out.dtype)
 
 
 def combine_kernel(cells, count, own_ref, x_ref, y_ref, d_ref, table_ref, top_ref, out_ref):
-    rows = jnp.concatenate([v.astype(F32) for v in gathered(cells, count, own_ref, x_ref, y_ref, d_ref)], axis=0)
-    total = top_ref[...].astype(F32)
-    for piece in pieces(table_ref[...]):
-        total += across(piece, rows.astype(BF16))
-    out_ref[...] = total.astype(BF16)
+    toks = out_ref.shape[0]
+    val = weighted(table_ref[...], gathered(cells, count, own_ref, x_ref, y_ref, d_ref))
+    total = val[:toks] + val[toks : 2 * toks] + val[2 * toks :]
+    out_ref[...] = (total + top_ref[...].astype(F32)).astype(BF16)
 
 
 def fetch_kernel(count, *refs):
@@ -270,7 +272,7 @@
         functools.partial(route_kernel, cells, half_z),
         [shape((block, width), BF16)] * half_z
         + [shape((block, width + lanes), BF16)] * half_z
-        + [shape((half_z * block, toks), F32)],
+        + [shape((3 * toks, half_z * block), F32)],
         [SMEM] + [HBM] * 6,
         "route",
         limit=60,

time: 56.8 us -> 56 us (0.986)
  Pallas kernels: 11.2 us -> 10.3 us
    pallas_call x1, Pallas kernels: 1.28 us -> 0.5 us  [per_device(): call(functools.partial(weigh_kernel, cells, half_z), [shape((toks, width)...]
  transfers between devices with their start and end apart: 22 -> 22, of which waited for: 11 -> 11; matrix products, arithmetic and copies ran while one was open for 0% -> 0% of each run, Pallas kernels for 9% -> 8%
where the time goes in v6:
time: 56 us; the launch traced here: 55.8 us
  starting transfers between devices  26.8 us (48%)
  waiting for transfers between devices  15.5 us (28%)
  Pallas kernels  10.3 us (18%)
  local copies, waits for them, and re-layouts  2.95 us (5%)
    ppermute x22, starting transfers between devices, send(): return lax.ppermute(value, 'node', [(d, d ^ flip) for d in range(devices)])  26.8 us
    ppermute x22, waiting for transfers between devices, send(): return lax.ppermute(value, 'node', [(d, d ^ flip) for d in range(devices)])  15.5 us
    unnamed x8, local copies, waits for them, and re-layouts  2.95 us
    pallas_call x3, Pallas kernels, fetch(): call(functools.partial(fetch_kernel, len(arrays)), [shape(w.shape, w.dtyp...  2.68 us
    pallas_call x1, Pallas kernels, per_device(): call(functools.partial(route_kernel, cells, half_z), [shape((block, width...  2.4 us
    pallas_call x1, Pallas kernels, per_device(): call(functools.partial(up_kernel, 8 * rows, 8 * rows), [shape((8 * rows,...  1.81 us
    pallas_call x2, Pallas kernels, down(): call(down_kernel, [shape((4 * rows, width), F32), shape((4 * rows, width)...  1.5 us
  transfers between devices with their start and end apart: 22, of which 11 were waited for; matrix products, arithmetic and copies ran while one was open for 0% of the time, Pallas kernels for 8%

profile of v6, /device:TPU:0, one launch (start us, length us, event | category | flops | bytes accessed | tf_op | source)
XLA Modules:
  0.0 55.8 jit_solution(10315813050301917113)
XLA Ops:
  0.0 2.4 %route.1 = (bf16[8,7168]{1,0:T(8,128)(2,1)}, bf16[8,7168]{1,0:T(8,128)(2,1)}, bf16[8,7296]{1,0:T(8,128)(2,1)}, bf16[8,7296]{1,0:T(8,128)(2,1)}, f32[24,16]{1,0:T(8,128)}) custom-call(s32[1]{0:T(128)} %bitcast.slot_ref, s32[4,8]{1,0:T(4,128)} %bitcast.6, f32[4,8]{1,0:T(4,128)} %bitcast.7, s32[4,8]{1,0:T(4,128)} %bitcast.8, s32[1,8]{1,0:T(1,128)} %bitcast.9, ...), custom_call_target="tpu_custom_call" | custom-call | tf_op jit(solution)/shard_map/route/pallas_call | solution.py:271
  2.4 3.1 %collective-permute-start.2 = (bf16[8,7168]{1,0:T(8,128)(2,1)}, bf16[8,7168]{1,0:T(8,128)(2,1)S(1)}, u32[]{:S(2)}, u32[]{:S(2)}) collective-permute-start(bf16[8,7168]{1,0:T(8,128)(2,1)} %get-tuple-element.37), channel_id=1, source_target_pairs={{0,8},{1,9},{2,10},{3,11},{4,12},{5,13},{6,14},{7,15},{8,0},{9,1},... | collective-permute-start | bytes 344072 | tf_op jit(solution)/shard_map/ppermute | solution.py:231
  5.5 2.6 %collective-permute-start = (bf16[8,7296]{1,0:T(8,128)(2,1)}, bf16[8,7296]{1,0:T(8,128)(2,1)S(1)}, u32[]{:S(2)}, u32[]{:S(2)}) collective-permute-start(bf16[8,7296]{1,0:T(8,128)(2,1)} %get-tuple-element.34), channel_id=1, source_target_pairs={{0,16},{1,17},{2,18},{3,19},{4,20},{5,21},{6,22},{7,23},{8,24},{9,... | collective-permute-start | bytes 350216 | tf_op jit(solution)/shard_map/ppermute | solution.py:231
  8.1 0.0 collective-permute-start.1
  8.1 0.0 copy-start.2
  8.1 0.9 %copy-done.2 = bf16[8,7168]{1,0:T(8,128)(2,1)S(1)} copy-done((bf16[8,7168]{1,0:T(8,128)(2,1)S(1)}, bf16[8,7168]{1,0:T(8,128)(2,1)}, u32[]{:S(2)}) %copy-start.2) | copy-done | bytes 114712
  9.0 0.1 fetch.3.refs_0_
  9.1 0.0 collective-permute-done.2.refs_1_
  9.1 0.1 split.2
  9.2 3.6 %collective-permute-start.8 = (bf16[8,7168]{1,0:T(8,128)(2,1)S(1)}, bf16[8,7168]{1,0:T(8,128)(2,1)S(1)}, u32[]{:S(2)}, u32[]{:S(2)}) collective-permute-start(bf16[8,7168]{1,0:T(8,128)(2,1)S(1)} %get-tuple-element.41), channel_id=1, source_target_pairs={{0,6},{1,7},{2,4},{3,5},{4,2},{5,3},{6,0},{7,1},{8,14},{9,15},{10,... | collective-permute-start | bytes 344072 | tf_op jit(solution)/shard_map/ppermute | solution.py:231
  12.9 0.5 collective-permute-start.7
  13.4 0.1 collective-permute-start.6
  13.5 2.0 %copy-done = bf16[7168,256]{1,0:T(8,128)(2,1)S(1)} copy-done((bf16[7168,256]{1,0:T(8,128)(2,1)S(1)}, bf16[7168,256]{1,0:T(8,128)(2,1)}, u32[]{:S(2)}) %copy-start) | copy-done | bytes 3670040
  15.5 0.3 fetch.4.refs_2_.refs_4_
  15.8 0.0 copy-start.1
  15.8 1.7 %collective-permute-done.refs_0_ = bf16[8,7296]{1,0:T(8,128)(2,1)S(1)} collective-permute-done((bf16[8,7296]{1,0:T(8,128)(2,1)}, bf16[8,7296]{1,0:T(8,128)(2,1)S(1)}, u32[]{:S(2)}, u32[]{:S(2)}) %collective-permute-start) | collective-permute-done | bytes 116768 | tf_op jit(solution)/shard_map/ppermute | solution.py:231
  17.6 0.0 collective-permute-done.1.refs_1_
  17.6 0.1 split.3
  17.6 2.5 %collective-permute-start.5 = (bf16[8,7168]{1,0:T(8,128)(2,1)S(1)}, bf16[8,7168]{1,0:T(8,128)(2,1)S(1)}, u32[]{:S(2)}, u32[]{:S(2)}) collective-permute-start(bf16[8,7168]{1,0:T(8,128)(2,1)S(1)} %get-tuple-element.40), channel_id=1, source_target_pairs={{0,6},{1,7},{2,4},{3,5},{4,2},{5,3},{6,0},{7,1},{8,14},{9,15},{10,... | collective-permute-start | bytes 344072 | tf_op jit(solution)/shard_map/ppermute | solution.py:231
  20.2 0.5 collective-permute-start.4
  20.7 0.0 collective-permute-done.8.refs_3_
  20.7 0.5 collective-permute-start.3
  21.2 0.0 collective-permute-done.7.refs_2_
  21.2 0.0 collective-permute-done.6.refs_1_
  21.2 0.1 collective-permute-start.10
  21.3 0.0 copy-done.1
  21.3 2.3 %fetch.5 = (bf16[7168,256]{1,0:T(8,128)(2,1)S(1)}, bf16[256,7168]{1,0:T(8,128)(2,1)S(1)}) custom-call(bf16[7168,256]{1,0:T(8,128)(2,1)S(1)} %copy-done.1, bf16[256,7168]{1,0:T(8,128)(2,1)} %refs_1_.1, bf16[32,7168]{1,0:T(8,128)(2,1)S(1)} %join.2.refs_2_), custom_call_target="tpu_custom_call" | custom-call | bytes 14680064 | tf_op jit(solution)/shard_map/fetch/pallas_call | solution.py:245
  23.6 0.0 collective-permute-done.5.refs_3_
  23.6 1.3 %collective-permute-done.4.refs_2_ = bf16[8,7168]{1,0:T(8,128)(2,1)S(1)} collective-permute-done((bf16[8,7168]{1,0:T(8,128)(2,1)S(1)}, bf16[8,7168]{1,0:T(8,128)(2,1)S(1)}, u32[]{:S(2)}, u32[]{:S(2)}) %collective-permute-start.4) | collective-permute-done | bytes 114720 | tf_op jit(solution)/shard_map/ppermute | solution.py:231
  24.9 0.5 collective-permute-done.3.refs_1_
  25.5 0.1 collective-permute-start.9
  25.6 0.0 collective-permute-done.10.refs_3_
  25.6 1.8 %collective-permute-done.9.refs_1_ = bf16[32,7168]{1,0:T(8,128)(2,1)S(1)} collective-permute-done((bf16[32,7168]{1,0:T(8,128)(2,1)S(1)}, bf16[32,7168]{1,0:T(8,128)(2,1)S(1)}, u32[]{:S(2)}, u32[]{:S(2)}) %collective-permute-start.9) | collective-permute-done | bytes 458784 | tf_op jit(solution)/shard_map/ppermute | solution.py:231
  27.4 1.8 %up.1 = (bf16[64,256]{1,0:T(8,128)(2,1)S(1)}, bf16[64,256]{1,0:T(8,128)(2,1)S(1)}, f32[128,256]{1,0:T(8,128)}, f32[128,256]{1,0:T(8,128)}) custom-call(bf16[32,7168]{1,0:T(8,128)(2,1)S(1)} %join.3.refs_0_, bf16[32,7168]{1,0:T(8,128)(2,1)S(1)} %collective-permute-done.9.refs_1_, bf16[32,7168]{1,0:T(8,128)(2,1)S(1)} %join.2.refs_2_, ...), custom_call_target="tpu_custom_call" | custom-call | flops 939524096 | tf_op jit(solution)/shard_map/up/pallas_call | solution.py:295
  29.2 0.7 %down.2 = (f32[32,7168]{1,0:T(8,128)S(1)}, bf16[32,7168]{1,0:T(8,128)(2,1)S(1)}) custom-call(bf16[64,256]{1,0:T(8,128)(2,1)S(1)} %get-tuple-element.44.hid_ref, bf16[256,7168]{1,0:T(8,128)(2,1)S(1)} %get-tuple-element.42.refs_4_.down_ref), custom_call_target="tpu_custom_call" | custom-call | flops 234881024 | tf_op jit(solution)/shard_map/down/pallas_call | solution.py:304
  29.9 0.2 collective-permute-start.11
  30.2 0.7 %down.3 = (f32[32,7168]{1,0:T(8,128)S(1)}, bf16[32,7168]{1,0:T(8,128)(2,1)S(1)}) custom-call(bf16[64,256]{1,0:T(8,128)(2,1)S(1)} %get-tuple-element.49.hid_ref, bf16[256,7168]{1,0:T(8,128)(2,1)S(1)} %get-tuple-element.42.refs_4_.down_ref), custom_call_target="tpu_custom_call" | custom-call | flops 234881024 | tf_op jit(solution)/shard_map/down/pallas_call | solution.py:304
  30.9 0.4 collective-permute-start.13
  31.3 0.5 collective-permute-done.11.core_ref
  31.8 0.1 lend.1
  32.0 1.9 %collective-permute-start.12 = (bf16[16,7168]{1,0:T(8,128)(2,1)S(1)}, bf16[16,7168]{1,0:T(8,128)(2,1)S(1)}, u32[]{:S(2)}, u32[]{:S(2)}) collective-permute-start(bf16[16,7168]{1,0:T(8,128)(2,1)S(1)} %get-tuple-element.48), channel_id=1, source_target_pairs={{0,8},{1,9},{2,10},{3,11},{4,12},{5,13},{6,14},{7,15},{8,0},{9,1},... | collective-permute-start | bytes 688136 | tf_op jit(solution)/shard_map/ppermute | solution.py:231
  33.8 0.0 collective-permute-done.13.core_ref
  33.8 0.1 half.1
  33.9 1.0 %collective-permute-start.14 = (bf16[8,7168]{1,0:T(8,128)(2,1)S(1)}, bf16[8,7168]{1,0:T(8,128)(2,1)S(1)}, u32[]{:S(2)}, u32[]{:S(2)}) collective-permute-start(bf16[8,7168]{1,0:T(8,128)(2,1)S(1)} %get-tuple-element.53), channel_id=1, source_target_pairs={{0,2},{1,3},{2,0},{3,1},{4,6},{5,7},{6,4},{7,5},{8,10},{9,11},{10,... | collective-permute-start | bytes 344072 | tf_op jit(solution)/shard_map/ppermute | solution.py:231
  35.0 1.1 %collective-permute-start.15 = (bf16[8,7168]{1,0:T(8,128)(2,1)S(1)}, bf16[8,7168]{1,0:T(8,128)(2,1)S(1)}, u32[]{:S(2)}, u32[]{:S(2)}) collective-permute-start(bf16[8,7168]{1,0:T(8,128)(2,1)S(1)} %get-tuple-element.54), channel_id=1, source_target_pairs={{0,4},{1,5},{2,6},{3,7},{4,0},{5,1},{6,2},{7,3},{8,12},{9,13},{10,... | collective-permute-start | bytes 344072 | tf_op jit(solution)/shard_map/ppermute | solution.py:231
  36.0 1.4 %collective-permute-start.16 = (bf16[8,7168]{1,0:T(8,128)(2,1)S(1)}, bf16[8,7168]{1,0:T(8,128)(2,1)S(1)}, u32[]{:S(2)}, u32[]{:S(2)}) collective-permute-start(bf16[8,7168]{1,0:T(8,128)(2,1)S(1)} %get-tuple-element.55), channel_id=1, source_target_pairs={{0,6},{1,7},{2,4},{3,5},{4,2},{5,3},{6,0},{7,1},{8,14},{9,15},{10,... | collective-permute-start | bytes 344072 | tf_op jit(solution)/shard_map/ppermute | solution.py:231
  37.5 2.0 %collective-permute-done.14.x_ref = bf16[8,7168]{1,0:T(8,128)(2,1)S(1)} collective-permute-done((bf16[8,7168]{1,0:T(8,128)(2,1)S(1)}, bf16[8,7168]{1,0:T(8,128)(2,1)S(1)}, u32[]{:S(2)}, u32[]{:S(2)}) %collective-permute-start.14) | collective-permute-done | bytes 114720 | tf_op jit(solution)/shard_map/ppermute | solution.py:231
  39.5 1.3 %collective-permute-done.15.y_ref = bf16[8,7168]{1,0:T(8,128)(2,1)S(1)} collective-permute-done((bf16[8,7168]{1,0:T(8,128)(2,1)S(1)}, bf16[8,7168]{1,0:T(8,128)(2,1)S(1)}, u32[]{:S(2)}, u32[]{:S(2)}) %collective-permute-start.15) | collective-permute-done | bytes 114720 | tf_op jit(solution)/shard_map/ppermute | solution.py:231
  40.8 1.5 %collective-permute-done.16.d_ref = bf16[8,7168]{1,0:T(8,128)(2,1)S(1)} collective-permute-done((bf16[8,7168]{1,0:T(8,128)(2,1)S(1)}, bf16[8,7168]{1,0:T(8,128)(2,1)S(1)}, u32[]{:S(2)}, u32[]{:S(2)}) %collective-permute-start.16) | collective-permute-done | bytes 114720 | tf_op jit(solution)/shard_map/ppermute | solution.py:231
  42.3 0.5 weigh.1
  42.8 1.3 %collective-permute-start.20 = (bf16[8,7168]{1,0:T(8,128)(2,1)S(1)}, bf16[8,7168]{1,0:T(8,128)(2,1)S(1)}, u32[]{:S(2)}, u32[]{:S(2)}) collective-permute-start(bf16[8,7168]{1,0:T(8,128)(2,1)S(1)} %get-tuple-element.62), channel_id=1, source_target_pairs={{0,8},{1,9},{2,10},{3,11},{4,12},{5,13},{6,14},{7,15},{8,0},{9,1},... | collective-permute-start | bytes 344072 | tf_op jit(solution)/shard_map/ppermute | solution.py:231
  44.2 0.0 collective-permute-done.12.refs_1_
  44.2 0.1 regroup.1
  44.3 0.9 %collective-permute-start.17 = (bf16[8,7168]{1,0:T(8,128)(2,1)S(1)}, bf16[8,7168]{1,0:T(8,128)(2,1)S(1)}, u32[]{:S(2)}, u32[]{:S(2)}) collective-permute-start(bf16[8,7168]{1,0:T(8,128)(2,1)S(1)} %get-tuple-element.58), channel_id=1, source_target_pairs={{0,2},{1,3},{2,0},{3,1},{4,6},{5,7},{6,4},{7,5},{8,10},{9,11},{10,... | collective-permute-start | bytes 344072 | tf_op jit(solution)/shard_map/ppermute | solution.py:231
  45.1 1.5 %collective-permute-start.18 = (bf16[8,7168]{1,0:T(8,128)(2,1)S(1)}, bf16[8,7168]{1,0:T(8,128)(2,1)S(1)}, u32[]{:S(2)}, u32[]{:S(2)}) collective-permute-start(bf16[8,7168]{1,0:T(8,128)(2,1)S(1)} %get-tuple-element.59), channel_id=1, source_target_pairs={{0,4},{1,5},{2,6},{3,7},{4,0},{5,1},{6,2},{7,3},{8,12},{9,13},{10,... | collective-permute-start | bytes 344072 | tf_op jit(solution)/shard_map/ppermute | solution.py:231
  46.7 1.2 %collective-permute-start.19 = (bf16[8,7168]{1,0:T(8,128)(2,1)S(1)}, bf16[8,7168]{1,0:T(8,128)(2,1)S(1)}, u32[]{:S(2)}, u32[]{:S(2)}) collective-permute-start(bf16[8,7168]{1,0:T(8,128)(2,1)S(1)} %get-tuple-element.60), channel_id=1, source_target_pairs={{0,6},{1,7},{2,4},{3,5},{4,2},{5,3},{6,0},{7,1},{8,14},{9,15},{10,... | collective-permute-start | bytes 344072 | tf_op jit(solution)/shard_map/ppermute | solution.py:231
  47.8 0.0 collective-permute-done.20
  47.9 2.2 %collective-permute-start.21 = (bf16[8,7168]{1,0:T(8,128)(2,1)S(1)}, bf16[8,7168]{1,0:T(8,128)(2,1)S(1)}, u32[]{:S(2)}, u32[]{:S(2)}) collective-permute-start(bf16[8,7168]{1,0:T(8,128)(2,1)S(1)} %add_convert_fusion), channel_id=1, source_target_pairs={{0,16},{1,17},{2,18},{3,19},{4,20},{5,21},{6,22},{7,23},{8,24},{9,... | collective-permute-start | bytes 344072 | tf_op jit(solution)/shard_map/ppermute | solution.py:231
  50.0 0.0 collective-permute-done.17.x_ref
  50.1 0.6 %collective-permute-done.18.y_ref = bf16[8,7168]{1,0:T(8,128)(2,1)S(1)} collective-permute-done((bf16[8,7168]{1,0:T(8,128)(2,1)S(1)}, bf16[8,7168]{1,0:T(8,128)(2,1)S(1)}, u32[]{:S(2)}, u32[]{:S(2)}) %collective-permute-start.18) | collective-permute-done | bytes 114720 | tf_op jit(solution)/shard_map/ppermute | solution.py:231
  50.7 1.7 %collective-permute-done.19.d_ref = bf16[8,7168]{1,0:T(8,128)(2,1)S(1)} collective-permute-done((bf16[8,7168]{1,0:T(8,128)(2,1)S(1)}, bf16[8,7168]{1,0:T(8,128)(2,1)S(1)}, u32[]{:S(2)}, u32[]{:S(2)}) %collective-permute-start.19) | collective-permute-done | bytes 114720 | tf_op jit(solution)/shard_map/ppermute | solution.py:231
  52.4 2.5 %collective-permute-done.21.top_ref = bf16[8,7168]{1,0:T(8,128)(2,1)S(1)} collective-permute-done((bf16[8,7168]{1,0:T(8,128)(2,1)S(1)}, bf16[8,7168]{1,0:T(8,128)(2,1)S(1)}, u32[]{:S(2)}, u32[]{:S(2)}) %collective-permute-start.21) | collective-permute-done | bytes 114720 | tf_op jit(solution)/shard_map/ppermute | solution.py:231
  54.8 0.0 copy-done.3
  54.8 0.9 %combine.1 = bf16[8,7168]{1,0:T(8,128)(2,1)} custom-call(f32[8,7168]{1,0:T(8,128)S(1)} %get-tuple-element.57.own_ref, bf16[8,7168]{1,0:T(8,128)(2,1)S(1)} %collective-permute-done.17.x_ref, bf16[8,7168]{1,0:T(8,128)(2,1)S(1)} %collective-permute-done.18.y_ref, bf16[8,7168]{1,0:T(8,128)(2,1)S(1)} %collective-permute-done.19.d_ref, f32[24,16]{1,0:T(8,128)S(1)} %copy-done.3, ...), custom_call_target="tpu_custom_call" | custom-call | tf_op jit(solution)/shard_map/combine/pallas_call | solution.py:352
  (5 shorter events, 0.1 us)
Async XLA Ops:
  2.4 6.7 %collective-permute-start.2 = (bf16[8,7168]{1,0:T(8,128)(2,1)}, bf16[8,7168]{1,0:T(8,128)(2,1)S(1)}, u32[]{:S(2)}, u32[]{:S(2)}) collective-permute-start(bf16[8,7168]{1,0:T(8,128)(2,1)} %get-tuple-element.37), channel_id=1, source_target_pairs={{0,8},{1,9},{2,10},{3,11},{4,12},{5,13},{6,14},{7,15},{8,0},{9,1},... | collective-permute-start | bytes 344072 | tf_op jit(solution)/shard_map/ppermute | solution.py:231
  5.5 12.1 %collective-permute-start = (bf16[8,7296]{1,0:T(8,128)(2,1)}, bf16[8,7296]{1,0:T(8,128)(2,1)S(1)}, u32[]{:S(2)}, u32[]{:S(2)}) collective-permute-start(bf16[8,7296]{1,0:T(8,128)(2,1)} %get-tuple-element.34), channel_id=1, source_target_pairs={{0,16},{1,17},{2,18},{3,19},{4,20},{5,21},{6,22},{7,23},{8,24},{9,... | collective-permute-start | bytes 350216 | tf_op jit(solution)/shard_map/ppermute | solution.py:231
  8.1 9.5 %collective-permute-start.1 = (bf16[8,7296]{1,0:T(8,128)(2,1)}, bf16[8,7296]{1,0:T(8,128)(2,1)S(1)}, u32[]{:S(2)}, u32[]{:S(2)}) collective-permute-start(bf16[8,7296]{1,0:T(8,128)(2,1)} %get-tuple-element.35), channel_id=1, source_target_pairs={{0,24},{1,25},{2,26},{3,27},{4,28},{5,29},{6,30},{7,31},{8,16},{9,... | collective-permute-start | bytes 350216 | tf_op jit(solution)/shard_map/ppermute | solution.py:231
  8.1 0.9 %copy-start.2 = (bf16[8,7168]{1,0:T(8,128)(2,1)S(1)}, bf16[8,7168]{1,0:T(8,128)(2,1)}, u32[]{:S(2)}) copy-start(bf16[8,7168]{1,0:T(8,128)(2,1)} %get-tuple-element.36.refs_0_) | copy-start | bytes 344068
  9.2 11.4 %collective-permute-start.8 = (bf16[8,7168]{1,0:T(8,128)(2,1)S(1)}, bf16[8,7168]{1,0:T(8,128)(2,1)S(1)}, u32[]{:S(2)}, u32[]{:S(2)}) collective-permute-start(bf16[8,7168]{1,0:T(8,128)(2,1)S(1)} %get-tuple-element.41), channel_id=1, source_target_pairs={{0,6},{1,7},{2,4},{3,5},{4,2},{5,3},{6,0},{7,1},{8,14},{9,15},{10,... | collective-permute-start | bytes 344072 | tf_op jit(solution)/shard_map/ppermute | solution.py:231
  12.9 8.3 %collective-permute-start.7 = (bf16[8,7168]{1,0:T(8,128)(2,1)S(1)}, bf16[8,7168]{1,0:T(8,128)(2,1)S(1)}, u32[]{:S(2)}, u32[]{:S(2)}) collective-permute-start(bf16[8,7168]{1,0:T(8,128)(2,1)S(1)} %get-tuple-element.41), channel_id=1, source_target_pairs={{0,4},{1,5},{2,6},{3,7},{4,0},{5,1},{6,2},{7,3},{8,12},{9,13},{10,... | collective-permute-start | bytes 344072 | tf_op jit(solution)/shard_map/ppermute | solution.py:231
  13.4 7.8 %collective-permute-start.6 = (bf16[8,7168]{1,0:T(8,128)(2,1)S(1)}, bf16[8,7168]{1,0:T(8,128)(2,1)S(1)}, u32[]{:S(2)}, u32[]{:S(2)}) collective-permute-start(bf16[8,7168]{1,0:T(8,128)(2,1)S(1)} %get-tuple-element.38.refs_1_.refs_0_), channel_id=1, source_target_pairs={{0,2},{1,3},{2,0},{3,1},{4,6},{5,7},{6,4},{7,5},{8,10},{9,11},{10,... | collective-permute-start | bytes 344072 | tf_op jit(solution)/shard_map/ppermute | solution.py:231
  13.5 2.0 %copy-start = (bf16[7168,256]{1,0:T(8,128)(2,1)S(1)}, bf16[7168,256]{1,0:T(8,128)(2,1)}, u32[]{:S(2)}) copy-start(bf16[7168,256]{1,0:T(8,128)(2,1)} %refs_0_.2) | copy-start | bytes 11010052
  15.8 5.5 %copy-start.1 = (bf16[7168,256]{1,0:T(8,128)(2,1)S(1)}, bf16[7168,256]{1,0:T(8,128)(2,1)}, u32[]{:S(2)}) copy-start(bf16[7168,256]{1,0:T(8,128)(2,1)} %refs_0_.3) | copy-start | bytes 11010052
  17.6 6.0 %collective-permute-start.5 = (bf16[8,7168]{1,0:T(8,128)(2,1)S(1)}, bf16[8,7168]{1,0:T(8,128)(2,1)S(1)}, u32[]{:S(2)}, u32[]{:S(2)}) collective-permute-start(bf16[8,7168]{1,0:T(8,128)(2,1)S(1)} %get-tuple-element.40), channel_id=1, source_target_pairs={{0,6},{1,7},{2,4},{3,5},{4,2},{5,3},{6,0},{7,1},{8,14},{9,15},{10,... | collective-permute-start | bytes 344072 | tf_op jit(solution)/shard_map/ppermute | solution.py:231
  20.2 4.8 %collective-permute-start.4 = (bf16[8,7168]{1,0:T(8,128)(2,1)S(1)}, bf16[8,7168]{1,0:T(8,128)(2,1)S(1)}, u32[]{:S(2)}, u32[]{:S(2)}) collective-permute-start(bf16[8,7168]{1,0:T(8,128)(2,1)S(1)} %get-tuple-element.40), channel_id=1, source_target_pairs={{0,4},{1,5},{2,6},{3,7},{4,0},{5,1},{6,2},{7,3},{8,12},{9,13},{10,... | collective-permute-start | bytes 344072 | tf_op jit(solution)/shard_map/ppermute | solution.py:231
  20.7 4.8 %collective-permute-start.3 = (bf16[8,7168]{1,0:T(8,128)(2,1)S(1)}, bf16[8,7168]{1,0:T(8,128)(2,1)S(1)}, u32[]{:S(2)}, u32[]{:S(2)}) collective-permute-start(bf16[8,7168]{1,0:T(8,128)(2,1)S(1)} %get-tuple-element.39.refs_4_.refs_0_), channel_id=1, source_target_pairs={{0,2},{1,3},{2,0},{3,1},{4,6},{5,7},{6,4},{7,5},{8,10},{9,11},{10,... | collective-permute-start | bytes 344072 | tf_op jit(solution)/shard_map/ppermute | solution.py:231
  21.2 4.3 %collective-permute-start.10 = (bf16[32,7168]{1,0:T(8,128)(2,1)S(1)}, bf16[32,7168]{1,0:T(8,128)(2,1)S(1)}, u32[]{:S(2)}, u32[]{:S(2)}) collective-permute-start(bf16[32,7168]{1,0:T(8,128)(2,1)S(1)} %join.2.refs_2_), channel_id=1, source_target_pairs={{0,1},{1,0},{2,3},{3,2},{4,5},{5,4},{6,7},{7,6},{8,9},{9,8},{10,11... | collective-permute-start | bytes 1376264 | tf_op jit(solution)/shard_map/ppermute | solution.py:231
  25.5 1.9 %collective-permute-start.9 = (bf16[32,7168]{1,0:T(8,128)(2,1)S(1)}, bf16[32,7168]{1,0:T(8,128)(2,1)S(1)}, u32[]{:S(2)}, u32[]{:S(2)}) collective-permute-start(bf16[32,7168]{1,0:T(8,128)(2,1)S(1)} %join.3.refs_0_), channel_id=1, source_target_pairs={{0,1},{1,0},{2,3},{3,2},{4,5},{5,4},{6,7},{7,6},{8,9},{9,8},{10,11... | collective-permute-start | bytes 1376264 | tf_op jit(solution)/shard_map/ppermute | solution.py:231
  29.9 1.9 %collective-permute-start.11 = (bf16[32,7168]{1,0:T(8,128)(2,1)S(1)}, bf16[32,7168]{1,0:T(8,128)(2,1)S(1)}, u32[]{:S(2)}, u32[]{:S(2)}) collective-permute-start(bf16[32,7168]{1,0:T(8,128)(2,1)S(1)} %get-tuple-element.46), channel_id=1, source_target_pairs={{0,1},{1,0},{2,3},{3,2},{4,5},{5,4},{6,7},{7,6},{8,9},{9,8},{10,11... | collective-permute-start | bytes 1376264 | tf_op jit(solution)/shard_map/ppermute | solution.py:231
  30.1 24.7 %copy-start.3 = (f32[24,16]{1,0:T(8,128)S(1)}, f32[24,16]{1,0:T(8,128)}, u32[]{:S(2)}) copy-start(f32[24,16]{1,0:T(8,128)} %get-tuple-element.61.table_ref) | copy-start | bytes 4612
  30.9 2.9 %collective-permute-start.13 = (bf16[32,7168]{1,0:T(8,128)(2,1)S(1)}, bf16[32,7168]{1,0:T(8,128)(2,1)S(1)}, u32[]{:S(2)}, u32[]{:S(2)}) collective-permute-start(bf16[32,7168]{1,0:T(8,128)(2,1)S(1)} %get-tuple-element.51), channel_id=1, source_target_pairs={{0,1},{1,0},{2,3},{3,2},{4,5},{5,4},{6,7},{7,6},{8,9},{9,8},{10,11... | collective-permute-start | bytes 1376264 | tf_op jit(solution)/shard_map/ppermute | solution.py:231
  32.0 12.2 %collective-permute-start.12 = (bf16[16,7168]{1,0:T(8,128)(2,1)S(1)}, bf16[16,7168]{1,0:T(8,128)(2,1)S(1)}, u32[]{:S(2)}, u32[]{:S(2)}) collective-permute-start(bf16[16,7168]{1,0:T(8,128)(2,1)S(1)} %get-tuple-element.48), channel_id=1, source_target_pairs={{0,8},{1,9},{2,10},{3,11},{4,12},{5,13},{6,14},{7,15},{8,0},{9,1},... | collective-permute-start | bytes 688136 | tf_op jit(solution)/shard_map/ppermute | solution.py:231
  33.9 5.6 %collective-permute-start.14 = (bf16[8,7168]{1,0:T(8,128)(2,1)S(1)}, bf16[8,7168]{1,0:T(8,128)(2,1)S(1)}, u32[]{:S(2)}, u32[]{:S(2)}) collective-permute-start(bf16[8,7168]{1,0:T(8,128)(2,1)S(1)} %get-tuple-element.53), channel_id=1, source_target_pairs={{0,2},{1,3},{2,0},{3,1},{4,6},{5,7},{6,4},{7,5},{8,10},{9,11},{10,... | collective-permute-start | bytes 344072 | tf_op jit(solution)/shard_map/ppermute | solution.py:231
  35.0 5.9 %collective-permute-start.15 = (bf16[8,7168]{1,0:T(8,128)(2,1)S(1)}, bf16[8,7168]{1,0:T(8,128)(2,1)S(1)}, u32[]{:S(2)}, u32[]{:S(2)}) collective-permute-start(bf16[8,7168]{1,0:T(8,128)(2,1)S(1)} %get-tuple-element.54), channel_id=1, source_target_pairs={{0,4},{1,5},{2,6},{3,7},{4,0},{5,1},{6,2},{7,3},{8,12},{9,13},{10,... | collective-permute-start | bytes 344072 | tf_op jit(solution)/shard_map/ppermute | solution.py:231
  36.0 6.3 %collective-permute-start.16 = (bf16[8,7168]{1,0:T(8,128)(2,1)S(1)}, bf16[8,7168]{1,0:T(8,128)(2,1)S(1)}, u32[]{:S(2)}, u32[]{:S(2)}) collective-permute-start(bf16[8,7168]{1,0:T(8,128)(2,1)S(1)} %get-tuple-element.55), channel_id=1, source_target_pairs={{0,6},{1,7},{2,4},{3,5},{4,2},{5,3},{6,0},{7,1},{8,14},{9,15},{10,... | collective-permute-start | bytes 344072 | tf_op jit(solution)/shard_map/ppermute | solution.py:231
  42.8 5.0 %collective-permute-start.20 = (bf16[8,7168]{1,0:T(8,128)(2,1)S(1)}, bf16[8,7168]{1,0:T(8,128)(2,1)S(1)}, u32[]{:S(2)}, u32[]{:S(2)}) collective-permute-start(bf16[8,7168]{1,0:T(8,128)(2,1)S(1)} %get-tuple-element.62), channel_id=1, source_target_pairs={{0,8},{1,9},{2,10},{3,11},{4,12},{5,13},{6,14},{7,15},{8,0},{9,1},... | collective-permute-start | bytes 344072 | tf_op jit(solution)/shard_map/ppermute | solution.py:231
  44.3 5.8 %collective-permute-start.17 = (bf16[8,7168]{1,0:T(8,128)(2,1)S(1)}, bf16[8,7168]{1,0:T(8,128)(2,1)S(1)}, u32[]{:S(2)}, u32[]{:S(2)}) collective-permute-start(bf16[8,7168]{1,0:T(8,128)(2,1)S(1)} %get-tuple-element.58), channel_id=1, source_target_pairs={{0,2},{1,3},{2,0},{3,1},{4,6},{5,7},{6,4},{7,5},{8,10},{9,11},{10,... | collective-permute-start | bytes 344072 | tf_op jit(solution)/shard_map/ppermute | solution.py:231
  45.1 5.5 %collective-permute-start.18 = (bf16[8,7168]{1,0:T(8,128)(2,1)S(1)}, bf16[8,7168]{1,0:T(8,128)(2,1)S(1)}, u32[]{:S(2)}, u32[]{:S(2)}) collective-permute-start(bf16[8,7168]{1,0:T(8,128)(2,1)S(1)} %get-tuple-element.59), channel_id=1, source_target_pairs={{0,4},{1,5},{2,6},{3,7},{4,0},{5,1},{6,2},{7,3},{8,12},{9,13},{10,... | collective-permute-start | bytes 344072 | tf_op jit(solution)/shard_map/ppermute | solution.py:231
  46.7 5.7 %collective-permute-start.19 = (bf16[8,7168]{1,0:T(8,128)(2,1)S(1)}, bf16[8,7168]{1,0:T(8,128)(2,1)S(1)}, u32[]{:S(2)}, u32[]{:S(2)}) collective-permute-start(bf16[8,7168]{1,0:T(8,128)(2,1)S(1)} %get-tuple-element.60), channel_id=1, source_target_pairs={{0,6},{1,7},{2,4},{3,5},{4,2},{5,3},{6,0},{7,1},{8,14},{9,15},{10,... | collective-permute-start | bytes 344072 | tf_op jit(solution)/shard_map/ppermute | solution.py:231
  47.9 7.0 %collective-permute-start.21 = (bf16[8,7168]{1,0:T(8,128)(2,1)S(1)}, bf16[8,7168]{1,0:T(8,128)(2,1)S(1)}, u32[]{:S(2)}, u32[]{:S(2)}) collective-permute-start(bf16[8,7168]{1,0:T(8,128)(2,1)S(1)} %add_convert_fusion), channel_id=1, source_target_pairs={{0,16},{1,17},{2,18},{3,19},{4,20},{5,21},{6,22},{7,23},{8,24},{9,... | collective-permute-start | bytes 344072 | tf_op jit(solution)/shard_map/ppermute | solution.py:231

commit v7 on v6

--- a/solution.py
+++ b/solution.py
@@ -17,12 +17,12 @@
     return jax.ShapeDtypeStruct(dims, dtype)
 
 
-def call(kernel, outs, ins, name, flops=0, moved=0, limit=24, scratch=()):
+def call(kernel, outs, ins, name, flops=0, moved=0, limit=24, scratch=(), out=VMEM):
     return pl.pallas_call(
         kernel,
         out_shape=outs,
         in_specs=ins,
-        out_specs=[VMEM] * len(outs),
+        out_specs=[out] * len(outs),
         scratch_shapes=list(scratch),
         compiler_params=pltpu.CompilerParams(vmem_limit_bytes=limit << 20),
         cost_estimate=pl.CostEstimate(flops=flops, bytes_accessed=moved, transcendentals=0),
@@ -56,11 +56,12 @@
 
 
 def route_kernel(cells, count, slot_ref, *refs):
-    ins, outs, held, sem = refs[:6], refs[6:-7], refs[-7:-1], refs[-1]
-    copies = [pltpu.make_async_copy(a, b, sem.at[i]) for i, (a, b) in enumerate(zip(ins, held))]
+    ins, held, sems = refs[:6], refs[-8:-2], refs[-2:]
+    dests, outs = refs[6 : 6 + (len(refs) - 14) // 2], refs[6 + (len(refs) - 14) // 2 : -8]
+    copies = [pltpu.make_async_copy(a, b, sems[0].at[i]) for i, (a, b) in enumerate(zip(ins, held))]
     for c in copies:
         c.start()
-    for c in copies:
+    for c in copies[:-1]:
         c.wait()
     ids_ref, gate_ref, pick_ref, place_ref, cap_ref, rows_ref = held
     top, toks = ids_ref.shape
@@ -95,10 +96,8 @@
     n = count * block
     eye = jnp.where(lax.broadcasted_iota(I32, (n, n), 0) == lax.broadcasted_iota(I32, (n, n), 1), 1.0, 0.0).astype(BF16)
     outs[-1][...] = jnp.concatenate([across(piece, eye) for piece in pieces(table[:n])], axis=0)
-    packed = jnp.dot(spot.astype(F32).astype(BF16), rows_ref[...], preferred_element_type=F32)
     for z, out in enumerate(outs[:-1]):
         part = slice(z * block, (z + 1) * block)
-        out[:, :width] = packed[part].astype(BF16)
         if z >= count:
             lanes = out.shape[1] - width
             place = lax.broadcasted_iota(I32, (toks, lanes), 1) - lax.broadcasted_iota(I32, (toks, lanes), 0)
@@ -107,6 +106,16 @@
                 shift = jnp.where(place == i * toks, 1.0, 0.0).astype(BF16)
                 tail += jnp.dot(piece, shift, preferred_element_type=F32)
             out[:, width:] = tail.astype(BF16)
+    copies[-1].wait()
+    pack = spot.astype(F32).astype(BF16)
+    back = [pltpu.make_async_copy(a, b, sems[1].at[i]) for i, (a, b) in enumerate(zip(outs, dests))]
+    back[-1].start()
+    packed = jnp.dot(pack, rows_ref[...], preferred_element_type=F32)
+    for z, out in enumerate(outs[:-1]):
+        out[:, :width] = packed[z * block : (z + 1) * block].astype(BF16)
+        back[z].start()
+    for c in back:
+        c.wait()
 
 
 def split_kernel(cells, count, *refs):
@@ -131,13 +140,15 @@
 def lend_kernel(cells, keep_ref, core_ref, home_ref, *outs):
     total = keep_ref[...] + core_ref[...].astype(F32)
     rows = total.shape[0] // 4
-    for z, out in enumerate((home_ref,) + outs):
-        parts = [total[b * rows + z * cells : b * rows + (z + 1) * cells] for b in range(4)]
+    for i, out in enumerate((home_ref,) + outs):
+        z, blocks = (0, range(4)) if i == 0 else ((i + 1) // 2, ((0, 1), (2, 3))[(i - 1) % 2])
+        parts = [total[b * rows + z * cells : b * rows + (z + 1) * cells] for b in blocks]
         out[...] = jnp.concatenate(parts, axis=0).astype(out.dtype)
 
 
 def regroup_kernel(cells, count, *refs):
-    vals = [r[...].astype(F32) for r in refs[:count]]
+    ins = [r[...].astype(F32) for r in refs[: 2 * count - 1]]
+    vals = ins[:1] + [jnp.concatenate(ins[i : i + 2], axis=0) for i in range(1, 2 * count - 1, 2)]
     for b, out in enumerate(refs[-4:]):
         out[...] = jnp.concatenate([v[b * cells : (b + 1) * cells] for v in vals], axis=0).astype(out.dtype)
 
@@ -201,15 +212,16 @@
     near_hid[...] = hid[far:]
 
 
-def down_kernel(hid_ref, down_ref, keep_ref, give_ref):
-    rows = keep_ref.shape[0]
+def down_kernel(far_ref, near_ref, down_ref, *outs):
+    hid = jnp.concatenate([far_ref[...], near_ref[...]], axis=0)
+    rows = outs[0].shape[0]
 
     def part(at, wat, step):
-        val = jnp.dot(hid_ref[...], down_ref[:, pl.ds(wat, step)], preferred_element_type=F32)
-        keep_ref[:, pl.ds(at, step)] = val[:rows]
-        give_ref[:, pl.ds(at, step)] = val[rows:].astype(BF16)
-
-    sweep(part, 0, keep_ref.shape[1], rows <= 128)
+        val = jnp.dot(hid, down_ref[:, pl.ds(wat, step)], preferred_element_type=F32)
+        for i, out in enumerate(outs):
+            out[:, pl.ds(at, step)] = val[i * rows : (i + 1) * rows].astype(out.dtype)
+
+    sweep(part, 0, outs[0].shape[1], rows <= 128)
 
 
 def per_device(
@@ -268,15 +280,21 @@
     block = 2 * cells
     lanes = -(-3 * toks // 128) * 128
     inputs = (expert_ids.T, gate_weights.T, replica_pick.T, placement[None, :], capacity[None, :], hidden_in)
+    made = (
+        [shape((block, width), BF16)] * half_z
+        + [shape((block, width + lanes), BF16)] * half_z
+        + [shape((3 * toks, half_z * block), F32)]
+    )
     route = call(
         functools.partial(route_kernel, cells, half_z),
-        [shape((block, width), BF16)] * half_z
-        + [shape((block, width + lanes), BF16)] * half_z
-        + [shape((3 * toks, half_z * block), F32)],
+        made,
         [SMEM] + [HBM] * 6,
         "route",
         limit=60,
-        scratch=[pltpu.VMEM(a.shape, a.dtype) for a in inputs] + [pltpu.SemaphoreType.DMA((6,))],
+        scratch=[pltpu.VMEM(a.shape, a.dtype) for a in made]
+        + [pltpu.VMEM(a.shape, a.dtype) for a in inputs]
+        + [pltpu.SemaphoreType.DMA((6,)), pltpu.SemaphoreType.DMA((len(made),))],
+        out=HBM,
     )(my_slot.reshape(1).astype(I32), *inputs)
     near_tab = route[-1]
     near_z = [over_z(route[z], z) for z in range(1, half_z)]
@@ -300,15 +318,6 @@
         flops=64 * rows * fw * width,
     )(far_all, far_core, near_all, near_core, wg, wu)
 
-    def down(hid, when):
-        return call(
-            down_kernel,
-            [shape((4 * rows, width), F32), shape((4 * rows, width), BF16)],
-            [VMEM] * 2 + [any_ref] * len(when),
-            "down",
-            flops=16 * rows * fw * width,
-        )(hid, wd, *when)
-
     def half(keep, got, when):
         return call(
             half_kernel,
@@ -321,18 +330,23 @@
         dg, yg, xg = send(d, members + 2), send(y, members), send(x, 2)
         return own, xg, yg, dg
 
-    far_keep, far_give = down(far_hid, ())
+    far_keep, far_give, near_keep, near_give = call(
+        down_kernel,
+        [shape((4 * rows, width), F32), shape((4 * rows, width), BF16)] * 2,
+        [VMEM] * 3,
+        "down",
+        flops=32 * rows * fw * width,
+    )(far_hid, near_hid, wd)
     far_sib = send(far_give, 1)
-    near_keep, near_give = down(near_hid, ())
     near_sib = send(near_give, 1)
     far_half = half(far_keep, far_sib, ())
     lent = call(
         functools.partial(lend_kernel, cells),
-        [shape((4 * cells, width), F32)] + [shape((4 * cells, width), BF16)] * (half_z - 1),
+        [shape((4 * cells, width), F32)] + [shape((2 * cells, width), BF16)] * (2 * half_z - 2),
         [VMEM] * 2,
         "lend",
     )(near_keep, near_sib)
-    near_z = [lent[0]] + [over_z(lent[z], z) for z in range(1, half_z)]
+    near_z = [lent[0]] + [over_z(lent[i], (i + 1) // 2) for i in range(1, 2 * half_z - 1)]
     far_sum = call(
         functools.partial(weigh_kernel, cells, half_z),
         [shape((toks, width), F32)] + [shape((toks, width), BF16)] * (half_z - 1),
@@ -342,7 +356,7 @@
     near_half = call(
         functools.partial(regroup_kernel, cells, half_z),
         [shape((rows, width), F32)] + [shape((rows, width), BF16)] * 3,
-        [VMEM] * half_z + [any_ref],
+        [VMEM] * (2 * half_z - 1) + [any_ref],
         "regroup",
     )(*near_z, far_sum[0])
     top_sum = far_sum[0]

time: 56 us -> 54.6 us (0.975)
  waiting for transfers between devices: 15.5 us -> 14.1 us
  starting transfers between devices: 26.8 us -> 27.7 us
  Pallas kernels: 10.3 us -> 9.41 us
    ppermute x22 -> x23, waiting for transfers between devices: 15.5 us -> 14.1 us  [send(): return lax.ppermute(value, 'node', [(d, d ^ flip) for d in range(devices)])]
    pallas_call x3 -> x2, Pallas kernels: 3.9 us -> 2.97 us  [the longest x1 2.32 us: per_device(): call(functools.partial(route_kernel, cells, half_z), made, [SMEM] + [HBM]...]
    ppermute x22 -> x23, starting transfers between devices: 26.8 us -> 27.7 us  [send(): return lax.ppermute(value, 'node', [(d, d ^ flip) for d in range(devices)])]
  transfers between devices with their start and end apart: 22 -> 23, of which waited for: 11 -> 11; matrix products, arithmetic and copies ran while one was open for 0% -> 0% of each run, Pallas kernels for 8% -> 7%
where the time goes in v7:
time: 54.6 us; the launch traced here: 54.4 us
  starting transfers between devices  27.7 us (51%)
  waiting for transfers between devices  14.1 us (26%)
  Pallas kernels  9.41 us (17%)
  local copies, waits for them, and re-layouts  2.95 us (5%)
    ppermute x23, starting transfers between devices, send(): return lax.ppermute(value, 'node', [(d, d ^ flip) for d in range(devices)])  27.7 us
    ppermute x23, waiting for transfers between devices, send(): return lax.ppermute(value, 'node', [(d, d ^ flip) for d in range(devices)])  14.1 us
    unnamed x8, local copies, waits for them, and re-layouts  2.95 us
    pallas_call x3, Pallas kernels, fetch(): call(functools.partial(fetch_kernel, len(arrays)), [shape(w.shape, w.dtyp...  2.68 us
    pallas_call x1, Pallas kernels, per_device(): call(functools.partial(route_kernel, cells, half_z), made, [SMEM] + [HBM]...  2.32 us
    pallas_call x1, Pallas kernels, per_device(): call(functools.partial(up_kernel, 8 * rows, 8 * rows), [shape((8 * rows,...  1.82 us
  transfers between devices with their start and end apart: 23, of which 11 were waited for; matrix products, arithmetic and copies ran while one was open for 0% of the time, Pallas kernels for 7%

profile of v7, /device:TPU:0, one launch (start us, length us, event | category | flops | bytes accessed | tf_op | source)
XLA Modules:
  0.0 54.4 jit_solution(11076366111175280930)
XLA Ops:
  0.0 2.3 %route.1 = (bf16[8,7168]{1,0:T(8,128)(2,1)}, bf16[8,7168]{1,0:T(8,128)(2,1)}, bf16[8,7296]{1,0:T(8,128)(2,1)}, bf16[8,7296]{1,0:T(8,128)(2,1)}, f32[24,16]{1,0:T(8,128)}) custom-call(s32[1]{0:T(128)} %bitcast.slot_ref, s32[4,8]{1,0:T(4,128)} %bitcast.6, f32[4,8]{1,0:T(4,128)} %bitcast.7, s32[4,8]{1,0:T(4,128)} %bitcast.8, s32[1,8]{1,0:T(1,128)} %bitcast.9, ...), custom_call_target="tpu_custom_call" | custom-call | tf_op jit(solution)/shard_map/route/pallas_call | solution.py:288
  2.3 3.1 %collective-permute-start.2 = (bf16[8,7168]{1,0:T(8,128)(2,1)}, bf16[8,7168]{1,0:T(8,128)(2,1)S(1)}, u32[]{:S(2)}, u32[]{:S(2)}) collective-permute-start(bf16[8,7168]{1,0:T(8,128)(2,1)} %get-tuple-element.38), channel_id=1, source_target_pairs={{0,8},{1,9},{2,10},{3,11},{4,12},{5,13},{6,14},{7,15},{8,0},{9,1},... | collective-permute-start | bytes 344072 | tf_op jit(solution)/shard_map/ppermute | solution.py:243
  5.4 2.6 %collective-permute-start = (bf16[8,7296]{1,0:T(8,128)(2,1)}, bf16[8,7296]{1,0:T(8,128)(2,1)S(1)}, u32[]{:S(2)}, u32[]{:S(2)}) collective-permute-start(bf16[8,7296]{1,0:T(8,128)(2,1)} %get-tuple-element.35), channel_id=1, source_target_pairs={{0,16},{1,17},{2,18},{3,19},{4,20},{5,21},{6,22},{7,23},{8,24},{9,... | collective-permute-start | bytes 350216 | tf_op jit(solution)/shard_map/ppermute | solution.py:243
  8.0 0.0 collective-permute-start.1
  8.0 0.9 %copy-done.2 = bf16[8,7168]{1,0:T(8,128)(2,1)S(1)} copy-done((bf16[8,7168]{1,0:T(8,128)(2,1)S(1)}, bf16[8,7168]{1,0:T(8,128)(2,1)}, u32[]{:S(2)}) %copy-start.2) | copy-done | bytes 114712
  8.9 0.1 fetch.3.refs_0_
  9.0 0.0 collective-permute-done.2.refs_1_
  9.1 0.1 split.2
  9.1 3.6 %collective-permute-start.8 = (bf16[8,7168]{1,0:T(8,128)(2,1)S(1)}, bf16[8,7168]{1,0:T(8,128)(2,1)S(1)}, u32[]{:S(2)}, u32[]{:S(2)}) collective-permute-start(bf16[8,7168]{1,0:T(8,128)(2,1)S(1)} %get-tuple-element.42), channel_id=1, source_target_pairs={{0,6},{1,7},{2,4},{3,5},{4,2},{5,3},{6,0},{7,1},{8,14},{9,15},{10,... | collective-permute-start | bytes 344072 | tf_op jit(solution)/shard_map/ppermute | solution.py:243
  12.8 0.5 collective-permute-start.7
  13.3 0.1 collective-permute-start.6
  13.4 2.0 %copy-done = bf16[7168,256]{1,0:T(8,128)(2,1)S(1)} copy-done((bf16[7168,256]{1,0:T(8,128)(2,1)S(1)}, bf16[7168,256]{1,0:T(8,128)(2,1)}, u32[]{:S(2)}) %copy-start) | copy-done | bytes 3670040
  15.5 0.3 fetch.4.refs_2_.refs_4_
  15.7 0.0 copy-start.1
  15.7 1.7 %collective-permute-done.refs_0_ = bf16[8,7296]{1,0:T(8,128)(2,1)S(1)} collective-permute-done((bf16[8,7296]{1,0:T(8,128)(2,1)}, bf16[8,7296]{1,0:T(8,128)(2,1)S(1)}, u32[]{:S(2)}, u32[]{:S(2)}) %collective-permute-start) | collective-permute-done | bytes 116768 | tf_op jit(solution)/shard_map/ppermute | solution.py:243
  17.5 0.0 collective-permute-done.1.refs_1_
  17.5 0.1 split.3
  17.6 2.5 %collective-permute-start.5 = (bf16[8,7168]{1,0:T(8,128)(2,1)S(1)}, bf16[8,7168]{1,0:T(8,128)(2,1)S(1)}, u32[]{:S(2)}, u32[]{:S(2)}) collective-permute-start(bf16[8,7168]{1,0:T(8,128)(2,1)S(1)} %get-tuple-element.41), channel_id=1, source_target_pairs={{0,6},{1,7},{2,4},{3,5},{4,2},{5,3},{6,0},{7,1},{8,14},{9,15},{10,... | collective-permute-start | bytes 344072 | tf_op jit(solution)/shard_map/ppermute | solution.py:243
  20.1 0.5 collective-permute-start.4
  20.6 0.0 collective-permute-done.8.refs_3_
  20.6 0.5 collective-permute-start.3
  21.1 0.0 collective-permute-done.7.refs_2_
  21.1 0.0 collective-permute-done.6.refs_1_
  21.2 0.1 collective-permute-start.10
  21.2 0.0 copy-done.1
  21.2 2.3 %fetch.5 = (bf16[7168,256]{1,0:T(8,128)(2,1)S(1)}, bf16[256,7168]{1,0:T(8,128)(2,1)S(1)}) custom-call(bf16[7168,256]{1,0:T(8,128)(2,1)S(1)} %copy-done.1, bf16[256,7168]{1,0:T(8,128)(2,1)} %refs_1_.1, bf16[32,7168]{1,0:T(8,128)(2,1)S(1)} %join.2.refs_2_), custom_call_target="tpu_custom_call" | custom-call | bytes 14680064 | tf_op jit(solution)/shard_map/fetch/pallas_call | solution.py:257
  23.6 0.0 collective-permute-done.5.refs_3_
  23.6 1.3 %collective-permute-done.4.refs_2_ = bf16[8,7168]{1,0:T(8,128)(2,1)S(1)} collective-permute-done((bf16[8,7168]{1,0:T(8,128)(2,1)S(1)}, bf16[8,7168]{1,0:T(8,128)(2,1)S(1)}, u32[]{:S(2)}, u32[]{:S(2)}) %collective-permute-start.4) | collective-permute-done | bytes 114720 | tf_op jit(solution)/shard_map/ppermute | solution.py:243
  24.9 0.5 collective-permute-done.3.refs_1_
  25.4 0.1 collective-permute-start.9
  25.5 0.0 collective-permute-done.10.refs_3_
  25.5 1.8 %collective-permute-done.9.refs_1_ = bf16[32,7168]{1,0:T(8,128)(2,1)S(1)} collective-permute-done((bf16[32,7168]{1,0:T(8,128)(2,1)S(1)}, bf16[32,7168]{1,0:T(8,128)(2,1)S(1)}, u32[]{:S(2)}, u32[]{:S(2)}) %collective-permute-start.9) | collective-permute-done | bytes 458784 | tf_op jit(solution)/shard_map/ppermute | solution.py:243
  27.3 1.8 %up.1 = (bf16[64,256]{1,0:T(8,128)(2,1)S(1)}, bf16[64,256]{1,0:T(8,128)(2,1)S(1)}, f32[128,256]{1,0:T(8,128)}, f32[128,256]{1,0:T(8,128)}) custom-call(bf16[32,7168]{1,0:T(8,128)(2,1)S(1)} %join.3.refs_0_, bf16[32,7168]{1,0:T(8,128)(2,1)S(1)} %collective-permute-done.9.refs_1_, bf16[32,7168]{1,0:T(8,128)(2,1)S(1)} %join.2.refs_2_, ...), custom_call_target="tpu_custom_call" | custom-call | flops 939524096 | tf_op jit(solution)/shard_map/up/pallas_call | solution.py:313
  29.1 0.7 %down.1 = (f32[32,7168]{1,0:T(8,128)S(1)}, bf16[32,7168]{1,0:T(8,128)(2,1)S(1)}, f32[32,7168]{1,0:T(8,128)S(1)}, bf16[32,7168]{1,0:T(8,128)(2,1)S(1)}) custom-call(bf16[64,256]{1,0:T(8,128)(2,1)S(1)} %get-tuple-element.45.far_ref, bf16[64,256]{1,0:T(8,128)(2,1)S(1)} %get-tuple-element.46.near_ref, bf16[256,7168]{1,0:T(8,128)(2,1)S(1)} %get-tuple-element.43.refs_4_.down_ref), custom_call_target="tpu_custom_call" | custom-call | flops 469762048 | tf_op jit(solution)/shard_map/down/pallas_call | solution.py:333
  29.8 0.2 collective-permute-start.14
  30.0 0.4 collective-permute-start.11
  30.3 1.3 %collective-permute-done.14.core_ref = bf16[32,7168]{1,0:T(8,128)(2,1)S(1)} collective-permute-done((bf16[32,7168]{1,0:T(8,128)(2,1)S(1)}, bf16[32,7168]{1,0:T(8,128)(2,1)S(1)}, u32[]{:S(2)}, u32[]{:S(2)}) %collective-permute-start.14) | collective-permute-done | bytes 458784 | tf_op jit(solution)/shard_map/ppermute | solution.py:243
  31.7 0.1 half.1
  31.7 0.8 %collective-permute-start.15 = (bf16[8,7168]{1,0:T(8,128)(2,1)S(1)}, bf16[8,7168]{1,0:T(8,128)(2,1)S(1)}, u32[]{:S(2)}, u32[]{:S(2)}) collective-permute-start(bf16[8,7168]{1,0:T(8,128)(2,1)S(1)} %get-tuple-element.55), channel_id=1, source_target_pairs={{0,2},{1,3},{2,0},{3,1},{4,6},{5,7},{6,4},{7,5},{8,10},{9,11},{10,... | collective-permute-start | bytes 344072 | tf_op jit(solution)/shard_map/ppermute | solution.py:243
  32.6 1.3 %collective-permute-start.16 = (bf16[8,7168]{1,0:T(8,128)(2,1)S(1)}, bf16[8,7168]{1,0:T(8,128)(2,1)S(1)}, u32[]{:S(2)}, u32[]{:S(2)}) collective-permute-start(bf16[8,7168]{1,0:T(8,128)(2,1)S(1)} %get-tuple-element.56), channel_id=1, source_target_pairs={{0,4},{1,5},{2,6},{3,7},{4,0},{5,1},{6,2},{7,3},{8,12},{9,13},{10,... | collective-permute-start | bytes 344072 | tf_op jit(solution)/shard_map/ppermute | solution.py:243
  33.9 1.4 %collective-permute-start.17 = (bf16[8,7168]{1,0:T(8,128)(2,1)S(1)}, bf16[8,7168]{1,0:T(8,128)(2,1)S(1)}, u32[]{:S(2)}, u32[]{:S(2)}) collective-permute-start(bf16[8,7168]{1,0:T(8,128)(2,1)S(1)} %get-tuple-element.57), channel_id=1, source_target_pairs={{0,6},{1,7},{2,4},{3,5},{4,2},{5,3},{6,0},{7,1},{8,14},{9,15},{10,... | collective-permute-start | bytes 344072 | tf_op jit(solution)/shard_map/ppermute | solution.py:243
  35.3 0.0 collective-permute-done.11.core_ref
  35.3 0.1 lend.1
  35.4 1.9 %collective-permute-start.12 = (bf16[8,7168]{1,0:T(8,128)(2,1)S(1)}, bf16[8,7168]{1,0:T(8,128)(2,1)S(1)}, u32[]{:S(2)}, u32[]{:S(2)}) collective-permute-start(bf16[8,7168]{1,0:T(8,128)(2,1)S(1)} %get-tuple-element.50), channel_id=1, source_target_pairs={{0,8},{1,9},{2,10},{3,11},{4,12},{5,13},{6,14},{7,15},{8,0},{9,1},... | collective-permute-start | bytes 344072 | tf_op jit(solution)/shard_map/ppermute | solution.py:243
  37.3 0.2 collective-permute-start.13
  37.5 0.3 collective-permute-done.15.x_ref
  37.8 1.0 %collective-permute-done.16.y_ref = bf16[8,7168]{1,0:T(8,128)(2,1)S(1)} collective-permute-done((bf16[8,7168]{1,0:T(8,128)(2,1)S(1)}, bf16[8,7168]{1,0:T(8,128)(2,1)S(1)}, u32[]{:S(2)}, u32[]{:S(2)}) %collective-permute-start.16) | collective-permute-done | bytes 114720 | tf_op jit(solution)/shard_map/ppermute | solution.py:243
  38.8 1.6 %collective-permute-done.17.d_ref = bf16[8,7168]{1,0:T(8,128)(2,1)S(1)} collective-permute-done((bf16[8,7168]{1,0:T(8,128)(2,1)S(1)}, bf16[8,7168]{1,0:T(8,128)(2,1)S(1)}, u32[]{:S(2)}, u32[]{:S(2)}) %collective-permute-start.17) | collective-permute-done | bytes 114720 | tf_op jit(solution)/shard_map/ppermute | solution.py:243
  40.4 0.5 weigh.1
  40.9 1.9 %collective-permute-start.21 = (bf16[8,7168]{1,0:T(8,128)(2,1)S(1)}, bf16[8,7168]{1,0:T(8,128)(2,1)S(1)}, u32[]{:S(2)}, u32[]{:S(2)}) collective-permute-start(bf16[8,7168]{1,0:T(8,128)(2,1)S(1)} %get-tuple-element.64), channel_id=1, source_target_pairs={{0,8},{1,9},{2,10},{3,11},{4,12},{5,13},{6,14},{7,15},{8,0},{9,1},... | collective-permute-start | bytes 344072 | tf_op jit(solution)/shard_map/ppermute | solution.py:243
  42.8 0.0 collective-permute-done.12.refs_1_
  42.8 0.0 collective-permute-done.13.refs_2_
  42.8 0.1 regroup.1
  42.9 1.4 %collective-permute-start.18 = (bf16[8,7168]{1,0:T(8,128)(2,1)S(1)}, bf16[8,7168]{1,0:T(8,128)(2,1)S(1)}, u32[]{:S(2)}, u32[]{:S(2)}) collective-permute-start(bf16[8,7168]{1,0:T(8,128)(2,1)S(1)} %get-tuple-element.60), channel_id=1, source_target_pairs={{0,2},{1,3},{2,0},{3,1},{4,6},{5,7},{6,4},{7,5},{8,10},{9,11},{10,... | collective-permute-start | bytes 344072 | tf_op jit(solution)/shard_map/ppermute | solution.py:243
  44.3 1.0 %collective-permute-start.19 = (bf16[8,7168]{1,0:T(8,128)(2,1)S(1)}, bf16[8,7168]{1,0:T(8,128)(2,1)S(1)}, u32[]{:S(2)}, u32[]{:S(2)}) collective-permute-start(bf16[8,7168]{1,0:T(8,128)(2,1)S(1)} %get-tuple-element.61), channel_id=1, source_target_pairs={{0,4},{1,5},{2,6},{3,7},{4,0},{5,1},{6,2},{7,3},{8,12},{9,13},{10,... | collective-permute-start | bytes 344072 | tf_op jit(solution)/shard_map/ppermute | solution.py:243
  45.3 1.2 %collective-permute-start.20 = (bf16[8,7168]{1,0:T(8,128)(2,1)S(1)}, bf16[8,7168]{1,0:T(8,128)(2,1)S(1)}, u32[]{:S(2)}, u32[]{:S(2)}) collective-permute-start(bf16[8,7168]{1,0:T(8,128)(2,1)S(1)} %get-tuple-element.62), channel_id=1, source_target_pairs={{0,6},{1,7},{2,4},{3,5},{4,2},{5,3},{6,0},{7,1},{8,14},{9,15},{10,... | collective-permute-start | bytes 344072 | tf_op jit(solution)/shard_map/ppermute | solution.py:243
  46.5 0.0 collective-permute-done.21
  46.5 2.4 %collective-permute-start.22 = (bf16[8,7168]{1,0:T(8,128)(2,1)S(1)}, bf16[8,7168]{1,0:T(8,128)(2,1)S(1)}, u32[]{:S(2)}, u32[]{:S(2)}) collective-permute-start(bf16[8,7168]{1,0:T(8,128)(2,1)S(1)} %add_convert_fusion), channel_id=1, source_target_pairs={{0,16},{1,17},{2,18},{3,19},{4,20},{5,21},{6,22},{7,23},{8,24},{9,... | collective-permute-start | bytes 344072 | tf_op jit(solution)/shard_map/ppermute | solution.py:243
  48.9 0.0 collective-permute-done.18.x_ref
  48.9 0.2 collective-permute-done.19.y_ref
  49.1 1.9 %collective-permute-done.20.d_ref = bf16[8,7168]{1,0:T(8,128)(2,1)S(1)} collective-permute-done((bf16[8,7168]{1,0:T(8,128)(2,1)S(1)}, bf16[8,7168]{1,0:T(8,128)(2,1)S(1)}, u32[]{:S(2)}, u32[]{:S(2)}) %collective-permute-start.20) | collective-permute-done | bytes 114720 | tf_op jit(solution)/shard_map/ppermute | solution.py:243
  51.0 2.5 %collective-permute-done.22.top_ref = bf16[8,7168]{1,0:T(8,128)(2,1)S(1)} collective-permute-done((bf16[8,7168]{1,0:T(8,128)(2,1)S(1)}, bf16[8,7168]{1,0:T(8,128)(2,1)S(1)}, u32[]{:S(2)}, u32[]{:S(2)}) %collective-permute-start.22) | collective-permute-done | bytes 114720 | tf_op jit(solution)/shard_map/ppermute | solution.py:243
  53.5 0.0 copy-done.3
  53.5 0.9 %combine.1 = bf16[8,7168]{1,0:T(8,128)(2,1)} custom-call(f32[8,7168]{1,0:T(8,128)S(1)} %get-tuple-element.59.own_ref, bf16[8,7168]{1,0:T(8,128)(2,1)S(1)} %collective-permute-done.18.x_ref, bf16[8,7168]{1,0:T(8,128)(2,1)S(1)} %collective-permute-done.19.y_ref, bf16[8,7168]{1,0:T(8,128)(2,1)S(1)} %collective-permute-done.20.d_ref, f32[24,16]{1,0:T(8,128)S(1)} %copy-done.3, ...), custom_call_target="tpu_custom_call" | custom-call | tf_op jit(solution)/shard_map/combine/pallas_call | solution.py:366
  (6 shorter events, 0.1 us)
Async XLA Ops:
  2.3 6.7 %collective-permute-start.2 = (bf16[8,7168]{1,0:T(8,128)(2,1)}, bf16[8,7168]{1,0:T(8,128)(2,1)S(1)}, u32[]{:S(2)}, u32[]{:S(2)}) collective-permute-start(bf16[8,7168]{1,0:T(8,128)(2,1)} %get-tuple-element.38), channel_id=1, source_target_pairs={{0,8},{1,9},{2,10},{3,11},{4,12},{5,13},{6,14},{7,15},{8,0},{9,1},... | collective-permute-start | bytes 344072 | tf_op jit(solution)/shard_map/ppermute | solution.py:243
  5.4 12.1 %collective-permute-start = (bf16[8,7296]{1,0:T(8,128)(2,1)}, bf16[8,7296]{1,0:T(8,128)(2,1)S(1)}, u32[]{:S(2)}, u32[]{:S(2)}) collective-permute-start(bf16[8,7296]{1,0:T(8,128)(2,1)} %get-tuple-element.35), channel_id=1, source_target_pairs={{0,16},{1,17},{2,18},{3,19},{4,20},{5,21},{6,22},{7,23},{8,24},{9,... | collective-permute-start | bytes 350216 | tf_op jit(solution)/shard_map/ppermute | solution.py:243
  8.0 9.5 %collective-permute-start.1 = (bf16[8,7296]{1,0:T(8,128)(2,1)}, bf16[8,7296]{1,0:T(8,128)(2,1)S(1)}, u32[]{:S(2)}, u32[]{:S(2)}) collective-permute-start(bf16[8,7296]{1,0:T(8,128)(2,1)} %get-tuple-element.36), channel_id=1, source_target_pairs={{0,24},{1,25},{2,26},{3,27},{4,28},{5,29},{6,30},{7,31},{8,16},{9,... | collective-permute-start | bytes 350216 | tf_op jit(solution)/shard_map/ppermute | solution.py:243
  8.0 0.9 %copy-start.2 = (bf16[8,7168]{1,0:T(8,128)(2,1)S(1)}, bf16[8,7168]{1,0:T(8,128)(2,1)}, u32[]{:S(2)}) copy-start(bf16[8,7168]{1,0:T(8,128)(2,1)} %get-tuple-element.37.refs_0_) | copy-start | bytes 344068
  9.1 11.5 %collective-permute-start.8 = (bf16[8,7168]{1,0:T(8,128)(2,1)S(1)}, bf16[8,7168]{1,0:T(8,128)(2,1)S(1)}, u32[]{:S(2)}, u32[]{:S(2)}) collective-permute-start(bf16[8,7168]{1,0:T(8,128)(2,1)S(1)} %get-tuple-element.42), channel_id=1, source_target_pairs={{0,6},{1,7},{2,4},{3,5},{4,2},{5,3},{6,0},{7,1},{8,14},{9,15},{10,... | collective-permute-start | bytes 344072 | tf_op jit(solution)/shard_map/ppermute | solution.py:243
  12.8 8.3 %collective-permute-start.7 = (bf16[8,7168]{1,0:T(8,128)(2,1)S(1)}, bf16[8,7168]{1,0:T(8,128)(2,1)S(1)}, u32[]{:S(2)}, u32[]{:S(2)}) collective-permute-start(bf16[8,7168]{1,0:T(8,128)(2,1)S(1)} %get-tuple-element.42), channel_id=1, source_target_pairs={{0,4},{1,5},{2,6},{3,7},{4,0},{5,1},{6,2},{7,3},{8,12},{9,13},{10,... | collective-permute-start | bytes 344072 | tf_op jit(solution)/shard_map/ppermute | solution.py:243
  13.3 7.8 %collective-permute-start.6 = (bf16[8,7168]{1,0:T(8,128)(2,1)S(1)}, bf16[8,7168]{1,0:T(8,128)(2,1)S(1)}, u32[]{:S(2)}, u32[]{:S(2)}) collective-permute-start(bf16[8,7168]{1,0:T(8,128)(2,1)S(1)} %get-tuple-element.39.refs_1_.refs_0_), channel_id=1, source_target_pairs={{0,2},{1,3},{2,0},{3,1},{4,6},{5,7},{6,4},{7,5},{8,10},{9,11},{10,... | collective-permute-start | bytes 344072 | tf_op jit(solution)/shard_map/ppermute | solution.py:243
  13.4 2.0 %copy-start = (bf16[7168,256]{1,0:T(8,128)(2,1)S(1)}, bf16[7168,256]{1,0:T(8,128)(2,1)}, u32[]{:S(2)}) copy-start(bf16[7168,256]{1,0:T(8,128)(2,1)} %refs_0_.2) | copy-start | bytes 11010052
  15.7 5.5 %copy-start.1 = (bf16[7168,256]{1,0:T(8,128)(2,1)S(1)}, bf16[7168,256]{1,0:T(8,128)(2,1)}, u32[]{:S(2)}) copy-start(bf16[7168,256]{1,0:T(8,128)(2,1)} %refs_0_.3) | copy-start | bytes 11010052
  17.6 6.0 %collective-permute-start.5 = (bf16[8,7168]{1,0:T(8,128)(2,1)S(1)}, bf16[8,7168]{1,0:T(8,128)(2,1)S(1)}, u32[]{:S(2)}, u32[]{:S(2)}) collective-permute-start(bf16[8,7168]{1,0:T(8,128)(2,1)S(1)} %get-tuple-element.41), channel_id=1, source_target_pairs={{0,6},{1,7},{2,4},{3,5},{4,2},{5,3},{6,0},{7,1},{8,14},{9,15},{10,... | collective-permute-start | bytes 344072 | tf_op jit(solution)/shard_map/ppermute | solution.py:243
  20.1 4.8 %collective-permute-start.4 = (bf16[8,7168]{1,0:T(8,128)(2,1)S(1)}, bf16[8,7168]{1,0:T(8,128)(2,1)S(1)}, u32[]{:S(2)}, u32[]{:S(2)}) collective-permute-start(bf16[8,7168]{1,0:T(8,128)(2,1)S(1)} %get-tuple-element.41), channel_id=1, source_target_pairs={{0,4},{1,5},{2,6},{3,7},{4,0},{5,1},{6,2},{7,3},{8,12},{9,13},{10,... | collective-permute-start | bytes 344072 | tf_op jit(solution)/shard_map/ppermute | solution.py:243
  20.6 4.8 %collective-permute-start.3 = (bf16[8,7168]{1,0:T(8,128)(2,1)S(1)}, bf16[8,7168]{1,0:T(8,128)(2,1)S(1)}, u32[]{:S(2)}, u32[]{:S(2)}) collective-permute-start(bf16[8,7168]{1,0:T(8,128)(2,1)S(1)} %get-tuple-element.40.refs_4_.refs_0_), channel_id=1, source_target_pairs={{0,2},{1,3},{2,0},{3,1},{4,6},{5,7},{6,4},{7,5},{8,10},{9,11},{10,... | collective-permute-start | bytes 344072 | tf_op jit(solution)/shard_map/ppermute | solution.py:243
  21.2 4.3 %collective-permute-start.10 = (bf16[32,7168]{1,0:T(8,128)(2,1)S(1)}, bf16[32,7168]{1,0:T(8,128)(2,1)S(1)}, u32[]{:S(2)}, u32[]{:S(2)}) collective-permute-start(bf16[32,7168]{1,0:T(8,128)(2,1)S(1)} %join.2.refs_2_), channel_id=1, source_target_pairs={{0,1},{1,0},{2,3},{3,2},{4,5},{5,4},{6,7},{7,6},{8,9},{9,8},{10,11... | collective-permute-start | bytes 1376264 | tf_op jit(solution)/shard_map/ppermute | solution.py:243
  25.4 1.9 %collective-permute-start.9 = (bf16[32,7168]{1,0:T(8,128)(2,1)S(1)}, bf16[32,7168]{1,0:T(8,128)(2,1)S(1)}, u32[]{:S(2)}, u32[]{:S(2)}) collective-permute-start(bf16[32,7168]{1,0:T(8,128)(2,1)S(1)} %join.3.refs_0_), channel_id=1, source_target_pairs={{0,1},{1,0},{2,3},{3,2},{4,5},{5,4},{6,7},{7,6},{8,9},{9,8},{10,11... | collective-permute-start | bytes 1376264 | tf_op jit(solution)/shard_map/ppermute | solution.py:243
  29.1 24.4 %copy-start.3 = (f32[24,16]{1,0:T(8,128)S(1)}, f32[24,16]{1,0:T(8,128)}, u32[]{:S(2)}) copy-start(f32[24,16]{1,0:T(8,128)} %get-tuple-element.63.table_ref) | copy-start | bytes 4612
  29.8 1.9 %collective-permute-start.14 = (bf16[32,7168]{1,0:T(8,128)(2,1)S(1)}, bf16[32,7168]{1,0:T(8,128)(2,1)S(1)}, u32[]{:S(2)}, u32[]{:S(2)}) collective-permute-start(bf16[32,7168]{1,0:T(8,128)(2,1)S(1)} %get-tuple-element.53), channel_id=1, source_target_pairs={{0,1},{1,0},{2,3},{3,2},{4,5},{5,4},{6,7},{7,6},{8,9},{9,8},{10,11... | collective-permute-start | bytes 1376264 | tf_op jit(solution)/shard_map/ppermute | solution.py:243
  30.0 5.3 %collective-permute-start.11 = (bf16[32,7168]{1,0:T(8,128)(2,1)S(1)}, bf16[32,7168]{1,0:T(8,128)(2,1)S(1)}, u32[]{:S(2)}, u32[]{:S(2)}) collective-permute-start(bf16[32,7168]{1,0:T(8,128)(2,1)S(1)} %get-tuple-element.48), channel_id=1, source_target_pairs={{0,1},{1,0},{2,3},{3,2},{4,5},{5,4},{6,7},{7,6},{8,9},{9,8},{10,11... | collective-permute-start | bytes 1376264 | tf_op jit(solution)/shard_map/ppermute | solution.py:243
  31.7 6.1 %collective-permute-start.15 = (bf16[8,7168]{1,0:T(8,128)(2,1)S(1)}, bf16[8,7168]{1,0:T(8,128)(2,1)S(1)}, u32[]{:S(2)}, u32[]{:S(2)}) collective-permute-start(bf16[8,7168]{1,0:T(8,128)(2,1)S(1)} %get-tuple-element.55), channel_id=1, source_target_pairs={{0,2},{1,3},{2,0},{3,1},{4,6},{5,7},{6,4},{7,5},{8,10},{9,11},{10,... | collective-permute-start | bytes 344072 | tf_op jit(solution)/shard_map/ppermute | solution.py:243
  32.6 6.2 %collective-permute-start.16 = (bf16[8,7168]{1,0:T(8,128)(2,1)S(1)}, bf16[8,7168]{1,0:T(8,128)(2,1)S(1)}, u32[]{:S(2)}, u32[]{:S(2)}) collective-permute-start(bf16[8,7168]{1,0:T(8,128)(2,1)S(1)} %get-tuple-element.56), channel_id=1, source_target_pairs={{0,4},{1,5},{2,6},{3,7},{4,0},{5,1},{6,2},{7,3},{8,12},{9,13},{10,... | collective-permute-start | bytes 344072 | tf_op jit(solution)/shard_map/ppermute | solution.py:243
  33.9 6.5 %collective-permute-start.17 = (bf16[8,7168]{1,0:T(8,128)(2,1)S(1)}, bf16[8,7168]{1,0:T(8,128)(2,1)S(1)}, u32[]{:S(2)}, u32[]{:S(2)}) collective-permute-start(bf16[8,7168]{1,0:T(8,128)(2,1)S(1)} %get-tuple-element.57), channel_id=1, source_target_pairs={{0,6},{1,7},{2,4},{3,5},{4,2},{5,3},{6,0},{7,1},{8,14},{9,15},{10,... | collective-permute-start | bytes 344072 | tf_op jit(solution)/shard_map/ppermute | solution.py:243
  35.4 7.4 %collective-permute-start.12 = (bf16[8,7168]{1,0:T(8,128)(2,1)S(1)}, bf16[8,7168]{1,0:T(8,128)(2,1)S(1)}, u32[]{:S(2)}, u32[]{:S(2)}) collective-permute-start(bf16[8,7168]{1,0:T(8,128)(2,1)S(1)} %get-tuple-element.50), channel_id=1, source_target_pairs={{0,8},{1,9},{2,10},{3,11},{4,12},{5,13},{6,14},{7,15},{8,0},{9,1},... | collective-permute-start | bytes 344072 | tf_op jit(solution)/shard_map/ppermute | solution.py:243
  37.3 5.5 %collective-permute-start.13 = (bf16[8,7168]{1,0:T(8,128)(2,1)S(1)}, bf16[8,7168]{1,0:T(8,128)(2,1)S(1)}, u32[]{:S(2)}, u32[]{:S(2)}) collective-permute-start(bf16[8,7168]{1,0:T(8,128)(2,1)S(1)} %get-tuple-element.51), channel_id=1, source_target_pairs={{0,8},{1,9},{2,10},{3,11},{4,12},{5,13},{6,14},{7,15},{8,0},{9,1},... | collective-permute-start | bytes 344072 | tf_op jit(solution)/shard_map/ppermute | solution.py:243
  40.9 5.6 %collective-permute-start.21 = (bf16[8,7168]{1,0:T(8,128)(2,1)S(1)}, bf16[8,7168]{1,0:T(8,128)(2,1)S(1)}, u32[]{:S(2)}, u32[]{:S(2)}) collective-permute-start(bf16[8,7168]{1,0:T(8,128)(2,1)S(1)} %get-tuple-element.64), channel_id=1, source_target_pairs={{0,8},{1,9},{2,10},{3,11},{4,12},{5,13},{6,14},{7,15},{8,0},{9,1},... | collective-permute-start | bytes 344072 | tf_op jit(solution)/shard_map/ppermute | solution.py:243
  42.9 6.0 %collective-permute-start.18 = (bf16[8,7168]{1,0:T(8,128)(2,1)S(1)}, bf16[8,7168]{1,0:T(8,128)(2,1)S(1)}, u32[]{:S(2)}, u32[]{:S(2)}) collective-permute-start(bf16[8,7168]{1,0:T(8,128)(2,1)S(1)} %get-tuple-element.60), channel_id=1, source_target_pairs={{0,2},{1,3},{2,0},{3,1},{4,6},{5,7},{6,4},{7,5},{8,10},{9,11},{10,... | collective-permute-start | bytes 344072 | tf_op jit(solution)/shard_map/ppermute | solution.py:243
  44.3 4.8 %collective-permute-start.19 = (bf16[8,7168]{1,0:T(8,128)(2,1)S(1)}, bf16[8,7168]{1,0:T(8,128)(2,1)S(1)}, u32[]{:S(2)}, u32[]{:S(2)}) collective-permute-start(bf16[8,7168]{1,0:T(8,128)(2,1)S(1)} %get-tuple-element.61), channel_id=1, source_target_pairs={{0,4},{1,5},{2,6},{3,7},{4,0},{5,1},{6,2},{7,3},{8,12},{9,13},{10,... | collective-permute-start | bytes 344072 | tf_op jit(solution)/shard_map/ppermute | solution.py:243
  45.3 5.7 %collective-permute-start.20 = (bf16[8,7168]{1,0:T(8,128)(2,1)S(1)}, bf16[8,7168]{1,0:T(8,128)(2,1)S(1)}, u32[]{:S(2)}, u32[]{:S(2)}) collective-permute-start(bf16[8,7168]{1,0:T(8,128)(2,1)S(1)} %get-tuple-element.62), channel_id=1, source_target_pairs={{0,6},{1,7},{2,4},{3,5},{4,2},{5,3},{6,0},{7,1},{8,14},{9,15},{10,... | collective-permute-start | bytes 344072 | tf_op jit(solution)/shard_map/ppermute | solution.py:243
  46.5 7.0 %collective-permute-start.22 = (bf16[8,7168]{1,0:T(8,128)(2,1)S(1)}, bf16[8,7168]{1,0:T(8,128)(2,1)S(1)}, u32[]{:S(2)}, u32[]{:S(2)}) collective-permute-start(bf16[8,7168]{1,0:T(8,128)(2,1)S(1)} %add_convert_fusion), channel_id=1, source_target_pairs={{0,16},{1,17},{2,18},{3,19},{4,20},{5,21},{6,22},{7,23},{8,24},{9,... | collective-permute-start | bytes 344072 | tf_op jit(solution)/shard_map/ppermute | solution.py:243

commit v8 on v7

--- a/solution.py
+++ b/solution.py
@@ -179,11 +179,14 @@
         out[...] = (a + b + c).astype(out.dtype)
 
 
-def combine_kernel(cells, count, own_ref, x_ref, y_ref, d_ref, table_ref, top_ref, out_ref):
+def combine_kernel(cells, count, own_ref, x_ref, y_ref, d_ref, table_ref, out_ref):
     toks = out_ref.shape[0]
     val = weighted(table_ref[...], gathered(cells, count, own_ref, x_ref, y_ref, d_ref))
-    total = val[:toks] + val[toks : 2 * toks] + val[2 * toks :]
-    out_ref[...] = (total + top_ref[...].astype(F32)).astype(BF16)
+    out_ref[...] = val[:toks] + val[toks : 2 * toks] + val[2 * toks :]
+
+
+def finish_kernel(near_ref, top_ref, out_ref):
+    out_ref[...] = (near_ref[...] + top_ref[...].astype(F32)).astype(BF16)
 
 
 def fetch_kernel(count, *refs):
@@ -363,12 +366,13 @@
     for z in range(1, half_z):
         top_sum = top_sum + over_z(far_sum[z], z).astype(F32)
     top_back = over_z(top_sum.astype(BF16), half_z)
-    (mixed,) = call(
+    (near_part,) = call(
         functools.partial(combine_kernel, cells, half_z),
-        [shape((toks, width), BF16)],
-        [VMEM] * 6,
+        [shape((toks, width), F32)],
+        [VMEM] * 5,
         "combine",
-    )(*gather(*near_half), near_tab, top_back)
+    )(*gather(*near_half), near_tab)
+    (mixed,) = call(finish_kernel, [shape((toks, width), BF16)], [VMEM] * 2, "finish")(near_part, top_back)
     return mixed
 
 

time: 54.6 us -> 54.4 us (level)
    pallas_call x0 -> x1, Pallas kernels: none -> 0.67 us  [per_device(): call(finish_kernel, [shape((toks, width), BF16)], [VMEM] * 2, 'finish')]
    pallas_call x1, Pallas kernels: 0.91 us -> 0.26 us  [per_device(): call(functools.partial(combine_kernel, cells, half_z), [shape((toks, widt...]
where the time goes in v8:
time: 54.4 us; the launch traced here: 54.1 us
  starting transfers between devices  27.7 us (51%)
  waiting for transfers between devices  13.9 us (26%)
  Pallas kernels  9.43 us (17%)
  local copies, waits for them, and re-layouts  2.95 us (5%)
    ppermute x23, starting transfers between devices, send(): return lax.ppermute(value, 'node', [(d, d ^ flip) for d in range(devices)])  27.7 us
    ppermute x23, waiting for transfers between devices, send(): return lax.ppermute(value, 'node', [(d, d ^ flip) for d in range(devices)])  13.9 us
    unnamed x8, local copies, waits for them, and re-layouts  2.95 us
    pallas_call x3, Pallas kernels, fetch(): call(functools.partial(fetch_kernel, len(arrays)), [shape(w.shape, w.dtyp...  2.68 us
    pallas_call x1, Pallas kernels, per_device(): call(functools.partial(route_kernel, cells, half_z), made, [SMEM] + [HBM]...  2.32 us
    pallas_call x1, Pallas kernels, per_device(): call(functools.partial(up_kernel, 8 * rows, 8 * rows), [shape((8 * rows,...  1.82 us
  transfers between devices with their start and end apart: 23, of which 11 were waited for; matrix products, arithmetic and copies ran while one was open for 0% of the time, Pallas kernels for 7%

profile of v8, /device:TPU:0, one launch (start us, length us, event | category | flops | bytes accessed | tf_op | source)
XLA Modules:
  0.0 54.1 jit_solution(2358099664468104813)
XLA Ops:
  0.0 2.3 %route.1 = (bf16[8,7168]{1,0:T(8,128)(2,1)}, bf16[8,7168]{1,0:T(8,128)(2,1)}, bf16[8,7296]{1,0:T(8,128)(2,1)}, bf16[8,7296]{1,0:T(8,128)(2,1)}, f32[24,16]{1,0:T(8,128)}) custom-call(s32[1]{0:T(128)} %bitcast.slot_ref, s32[4,8]{1,0:T(4,128)} %bitcast.6, f32[4,8]{1,0:T(4,128)} %bitcast.7, s32[4,8]{1,0:T(4,128)} %bitcast.8, s32[1,8]{1,0:T(1,128)} %bitcast.9, ...), custom_call_target="tpu_custom_call" | custom-call | tf_op jit(solution)/shard_map/route/pallas_call | solution.py:291
  2.3 3.1 %collective-permute-start.2 = (bf16[8,7168]{1,0:T(8,128)(2,1)}, bf16[8,7168]{1,0:T(8,128)(2,1)S(1)}, u32[]{:S(2)}, u32[]{:S(2)}) collective-permute-start(bf16[8,7168]{1,0:T(8,128)(2,1)} %get-tuple-element.38), channel_id=1, source_target_pairs={{0,8},{1,9},{2,10},{3,11},{4,12},{5,13},{6,14},{7,15},{8,0},{9,1},... | collective-permute-start | bytes 344072 | tf_op jit(solution)/shard_map/ppermute | solution.py:246
  5.4 2.6 %collective-permute-start = (bf16[8,7296]{1,0:T(8,128)(2,1)}, bf16[8,7296]{1,0:T(8,128)(2,1)S(1)}, u32[]{:S(2)}, u32[]{:S(2)}) collective-permute-start(bf16[8,7296]{1,0:T(8,128)(2,1)} %get-tuple-element.35), channel_id=1, source_target_pairs={{0,16},{1,17},{2,18},{3,19},{4,20},{5,21},{6,22},{7,23},{8,24},{9,... | collective-permute-start | bytes 350216 | tf_op jit(solution)/shard_map/ppermute | solution.py:246
  8.0 0.0 collective-permute-start.1
  8.0 0.9 %copy-done.2 = bf16[8,7168]{1,0:T(8,128)(2,1)S(1)} copy-done((bf16[8,7168]{1,0:T(8,128)(2,1)S(1)}, bf16[8,7168]{1,0:T(8,128)(2,1)}, u32[]{:S(2)}) %copy-start.2) | copy-done | bytes 114712
  8.9 0.1 fetch.3.refs_0_
  9.0 0.0 collective-permute-done.2.refs_1_
  9.1 0.1 split.2
  9.1 3.6 %collective-permute-start.8 = (bf16[8,7168]{1,0:T(8,128)(2,1)S(1)}, bf16[8,7168]{1,0:T(8,128)(2,1)S(1)}, u32[]{:S(2)}, u32[]{:S(2)}) collective-permute-start(bf16[8,7168]{1,0:T(8,128)(2,1)S(1)} %get-tuple-element.42), channel_id=1, source_target_pairs={{0,6},{1,7},{2,4},{3,5},{4,2},{5,3},{6,0},{7,1},{8,14},{9,15},{10,... | collective-permute-start | bytes 344072 | tf_op jit(solution)/shard_map/ppermute | solution.py:246
  12.8 0.5 collective-permute-start.7
  13.3 0.1 collective-permute-start.6
  13.4 2.0 %copy-done = bf16[7168,256]{1,0:T(8,128)(2,1)S(1)} copy-done((bf16[7168,256]{1,0:T(8,128)(2,1)S(1)}, bf16[7168,256]{1,0:T(8,128)(2,1)}, u32[]{:S(2)}) %copy-start) | copy-done | bytes 3670040
  15.5 0.3 fetch.4.refs_2_.refs_4_
  15.7 0.0 copy-start.1
  15.7 1.7 %collective-permute-done.refs_0_ = bf16[8,7296]{1,0:T(8,128)(2,1)S(1)} collective-permute-done((bf16[8,7296]{1,0:T(8,128)(2,1)}, bf16[8,7296]{1,0:T(8,128)(2,1)S(1)}, u32[]{:S(2)}, u32[]{:S(2)}) %collective-permute-start) | collective-permute-done | bytes 116768 | tf_op jit(solution)/shard_map/ppermute | solution.py:246
  17.5 0.0 collective-permute-done.1.refs_1_
  17.5 0.1 split.3
  17.6 2.5 %collective-permute-start.5 = (bf16[8,7168]{1,0:T(8,128)(2,1)S(1)}, bf16[8,7168]{1,0:T(8,128)(2,1)S(1)}, u32[]{:S(2)}, u32[]{:S(2)}) collective-permute-start(bf16[8,7168]{1,0:T(8,128)(2,1)S(1)} %get-tuple-element.41), channel_id=1, source_target_pairs={{0,6},{1,7},{2,4},{3,5},{4,2},{5,3},{6,0},{7,1},{8,14},{9,15},{10,... | collective-permute-start | bytes 344072 | tf_op jit(solution)/shard_map/ppermute | solution.py:246
  20.1 0.5 collective-permute-start.4
  20.6 0.0 collective-permute-done.8.refs_3_
  20.6 0.5 collective-permute-start.3
  21.1 0.0 collective-permute-done.7.refs_2_
  21.1 0.0 collective-permute-done.6.refs_1_
  21.2 0.1 collective-permute-start.10
  21.2 0.0 copy-done.1
  21.2 2.3 %fetch.5 = (bf16[7168,256]{1,0:T(8,128)(2,1)S(1)}, bf16[256,7168]{1,0:T(8,128)(2,1)S(1)}) custom-call(bf16[7168,256]{1,0:T(8,128)(2,1)S(1)} %copy-done.1, bf16[256,7168]{1,0:T(8,128)(2,1)} %refs_1_.1, bf16[32,7168]{1,0:T(8,128)(2,1)S(1)} %join.2.refs_2_), custom_call_target="tpu_custom_call" | custom-call | bytes 14680064 | tf_op jit(solution)/shard_map/fetch/pallas_call | solution.py:260
  23.6 0.0 collective-permute-done.5.refs_3_
  23.6 1.3 %collective-permute-done.4.refs_2_ = bf16[8,7168]{1,0:T(8,128)(2,1)S(1)} collective-permute-done((bf16[8,7168]{1,0:T(8,128)(2,1)S(1)}, bf16[8,7168]{1,0:T(8,128)(2,1)S(1)}, u32[]{:S(2)}, u32[]{:S(2)}) %collective-permute-start.4) | collective-permute-done | bytes 114720 | tf_op jit(solution)/shard_map/ppermute | solution.py:246
  24.9 0.5 collective-permute-done.3.refs_1_
  25.4 0.1 collective-permute-start.9
  25.5 0.0 collective-permute-done.10.refs_3_
  25.5 1.8 %collective-permute-done.9.refs_1_ = bf16[32,7168]{1,0:T(8,128)(2,1)S(1)} collective-permute-done((bf16[32,7168]{1,0:T(8,128)(2,1)S(1)}, bf16[32,7168]{1,0:T(8,128)(2,1)S(1)}, u32[]{:S(2)}, u32[]{:S(2)}) %collective-permute-start.9) | collective-permute-done | bytes 458784 | tf_op jit(solution)/shard_map/ppermute | solution.py:246
  27.3 1.8 %up.1 = (bf16[64,256]{1,0:T(8,128)(2,1)S(1)}, bf16[64,256]{1,0:T(8,128)(2,1)S(1)}, f32[128,256]{1,0:T(8,128)}, f32[128,256]{1,0:T(8,128)}) custom-call(bf16[32,7168]{1,0:T(8,128)(2,1)S(1)} %join.3.refs_0_, bf16[32,7168]{1,0:T(8,128)(2,1)S(1)} %collective-permute-done.9.refs_1_, bf16[32,7168]{1,0:T(8,128)(2,1)S(1)} %join.2.refs_2_, ...), custom_call_target="tpu_custom_call" | custom-call | flops 939524096 | tf_op jit(solution)/shard_map/up/pallas_call | solution.py:316
  29.1 0.7 %down.1 = (f32[32,7168]{1,0:T(8,128)S(1)}, bf16[32,7168]{1,0:T(8,128)(2,1)S(1)}, f32[32,7168]{1,0:T(8,128)S(1)}, bf16[32,7168]{1,0:T(8,128)(2,1)S(1)}) custom-call(bf16[64,256]{1,0:T(8,128)(2,1)S(1)} %get-tuple-element.45.far_ref, bf16[64,256]{1,0:T(8,128)(2,1)S(1)} %get-tuple-element.46.near_ref, bf16[256,7168]{1,0:T(8,128)(2,1)S(1)} %get-tuple-element.43.refs_4_.down_ref), custom_call_target="tpu_custom_call" | custom-call | flops 469762048 | tf_op jit(solution)/shard_map/down/pallas_call | solution.py:336
  29.8 0.2 collective-permute-start.14
  30.0 0.4 collective-permute-start.11
  30.3 1.3 %collective-permute-done.14.core_ref = bf16[32,7168]{1,0:T(8,128)(2,1)S(1)} collective-permute-done((bf16[32,7168]{1,0:T(8,128)(2,1)S(1)}, bf16[32,7168]{1,0:T(8,128)(2,1)S(1)}, u32[]{:S(2)}, u32[]{:S(2)}) %collective-permute-start.14) | collective-permute-done | bytes 458784 | tf_op jit(solution)/shard_map/ppermute | solution.py:246
  31.7 0.1 half.1
  31.7 0.8 %collective-permute-start.15 = (bf16[8,7168]{1,0:T(8,128)(2,1)S(1)}, bf16[8,7168]{1,0:T(8,128)(2,1)S(1)}, u32[]{:S(2)}, u32[]{:S(2)}) collective-permute-start(bf16[8,7168]{1,0:T(8,128)(2,1)S(1)} %get-tuple-element.55), channel_id=1, source_target_pairs={{0,2},{1,3},{2,0},{3,1},{4,6},{5,7},{6,4},{7,5},{8,10},{9,11},{10,... | collective-permute-start | bytes 344072 | tf_op jit(solution)/shard_map/ppermute | solution.py:246
  32.6 1.3 %collective-permute-start.16 = (bf16[8,7168]{1,0:T(8,128)(2,1)S(1)}, bf16[8,7168]{1,0:T(8,128)(2,1)S(1)}, u32[]{:S(2)}, u32[]{:S(2)}) collective-permute-start(bf16[8,7168]{1,0:T(8,128)(2,1)S(1)} %get-tuple-element.56), channel_id=1, source_target_pairs={{0,4},{1,5},{2,6},{3,7},{4,0},{5,1},{6,2},{7,3},{8,12},{9,13},{10,... | collective-permute-start | bytes 344072 | tf_op jit(solution)/shard_map/ppermute | solution.py:246
  33.9 1.4 %collective-permute-start.17 = (bf16[8,7168]{1,0:T(8,128)(2,1)S(1)}, bf16[8,7168]{1,0:T(8,128)(2,1)S(1)}, u32[]{:S(2)}, u32[]{:S(2)}) collective-permute-start(bf16[8,7168]{1,0:T(8,128)(2,1)S(1)} %get-tuple-element.57), channel_id=1, source_target_pairs={{0,6},{1,7},{2,4},{3,5},{4,2},{5,3},{6,0},{7,1},{8,14},{9,15},{10,... | collective-permute-start | bytes 344072 | tf_op jit(solution)/shard_map/ppermute | solution.py:246
  35.3 0.0 collective-permute-done.11.core_ref
  35.3 0.1 lend.1
  35.4 1.9 %collective-permute-start.12 = (bf16[8,7168]{1,0:T(8,128)(2,1)S(1)}, bf16[8,7168]{1,0:T(8,128)(2,1)S(1)}, u32[]{:S(2)}, u32[]{:S(2)}) collective-permute-start(bf16[8,7168]{1,0:T(8,128)(2,1)S(1)} %get-tuple-element.50), channel_id=1, source_target_pairs={{0,8},{1,9},{2,10},{3,11},{4,12},{5,13},{6,14},{7,15},{8,0},{9,1},... | collective-permute-start | bytes 344072 | tf_op jit(solution)/shard_map/ppermute | solution.py:246
  37.3 0.2 collective-permute-start.13
  37.5 0.3 collective-permute-done.15.x_ref
  37.8 1.0 %collective-permute-done.16.y_ref = bf16[8,7168]{1,0:T(8,128)(2,1)S(1)} collective-permute-done((bf16[8,7168]{1,0:T(8,128)(2,1)S(1)}, bf16[8,7168]{1,0:T(8,128)(2,1)S(1)}, u32[]{:S(2)}, u32[]{:S(2)}) %collective-permute-start.16) | collective-permute-done | bytes 114720 | tf_op jit(solution)/shard_map/ppermute | solution.py:246
  38.8 1.6 %collective-permute-done.17.d_ref = bf16[8,7168]{1,0:T(8,128)(2,1)S(1)} collective-permute-done((bf16[8,7168]{1,0:T(8,128)(2,1)S(1)}, bf16[8,7168]{1,0:T(8,128)(2,1)S(1)}, u32[]{:S(2)}, u32[]{:S(2)}) %collective-permute-start.17) | collective-permute-done | bytes 114720 | tf_op jit(solution)/shard_map/ppermute | solution.py:246
  40.4 0.5 weigh.1
  40.9 1.9 %collective-permute-start.21 = (bf16[8,7168]{1,0:T(8,128)(2,1)S(1)}, bf16[8,7168]{1,0:T(8,128)(2,1)S(1)}, u32[]{:S(2)}, u32[]{:S(2)}) collective-permute-start(bf16[8,7168]{1,0:T(8,128)(2,1)S(1)} %get-tuple-element.64), channel_id=1, source_target_pairs={{0,8},{1,9},{2,10},{3,11},{4,12},{5,13},{6,14},{7,15},{8,0},{9,1},... | collective-permute-start | bytes 344072 | tf_op jit(solution)/shard_map/ppermute | solution.py:246
  42.8 0.0 collective-permute-done.12.refs_1_
  42.8 0.0 collective-permute-done.13.refs_2_
  42.8 0.1 regroup.1
  42.9 1.4 %collective-permute-start.18 = (bf16[8,7168]{1,0:T(8,128)(2,1)S(1)}, bf16[8,7168]{1,0:T(8,128)(2,1)S(1)}, u32[]{:S(2)}, u32[]{:S(2)}) collective-permute-start(bf16[8,7168]{1,0:T(8,128)(2,1)S(1)} %get-tuple-element.60), channel_id=1, source_target_pairs={{0,2},{1,3},{2,0},{3,1},{4,6},{5,7},{6,4},{7,5},{8,10},{9,11},{10,... | collective-permute-start | bytes 344072 | tf_op jit(solution)/shard_map/ppermute | solution.py:246
  44.3 1.0 %collective-permute-start.19 = (bf16[8,7168]{1,0:T(8,128)(2,1)S(1)}, bf16[8,7168]{1,0:T(8,128)(2,1)S(1)}, u32[]{:S(2)}, u32[]{:S(2)}) collective-permute-start(bf16[8,7168]{1,0:T(8,128)(2,1)S(1)} %get-tuple-element.61), channel_id=1, source_target_pairs={{0,4},{1,5},{2,6},{3,7},{4,0},{5,1},{6,2},{7,3},{8,12},{9,13},{10,... | collective-permute-start | bytes 344072 | tf_op jit(solution)/shard_map/ppermute | solution.py:246
  45.3 1.2 %collective-permute-start.20 = (bf16[8,7168]{1,0:T(8,128)(2,1)S(1)}, bf16[8,7168]{1,0:T(8,128)(2,1)S(1)}, u32[]{:S(2)}, u32[]{:S(2)}) collective-permute-start(bf16[8,7168]{1,0:T(8,128)(2,1)S(1)} %get-tuple-element.62), channel_id=1, source_target_pairs={{0,6},{1,7},{2,4},{3,5},{4,2},{5,3},{6,0},{7,1},{8,14},{9,15},{10,... | collective-permute-start | bytes 344072 | tf_op jit(solution)/shard_map/ppermute | solution.py:246
  46.5 0.0 collective-permute-done.21
  46.5 2.4 %collective-permute-start.22 = (bf16[8,7168]{1,0:T(8,128)(2,1)S(1)}, bf16[8,7168]{1,0:T(8,128)(2,1)S(1)}, u32[]{:S(2)}, u32[]{:S(2)}) collective-permute-start(bf16[8,7168]{1,0:T(8,128)(2,1)S(1)} %add_convert_fusion), channel_id=1, source_target_pairs={{0,16},{1,17},{2,18},{3,19},{4,20},{5,21},{6,22},{7,23},{8,24},{9,... | collective-permute-start | bytes 344072 | tf_op jit(solution)/shard_map/ppermute | solution.py:246
  48.9 0.0 collective-permute-done.18.x_ref
  48.9 0.2 collective-permute-done.19.y_ref
  49.1 1.9 %collective-permute-done.20.d_ref = bf16[8,7168]{1,0:T(8,128)(2,1)S(1)} collective-permute-done((bf16[8,7168]{1,0:T(8,128)(2,1)S(1)}, bf16[8,7168]{1,0:T(8,128)(2,1)S(1)}, u32[]{:S(2)}, u32[]{:S(2)}) %collective-permute-start.20) | collective-permute-done | bytes 114720 | tf_op jit(solution)/shard_map/ppermute | solution.py:246
  51.0 0.3 combine.1.near_ref
  51.3 2.2 %collective-permute-done.22.top_ref = bf16[8,7168]{1,0:T(8,128)(2,1)S(1)} collective-permute-done((bf16[8,7168]{1,0:T(8,128)(2,1)S(1)}, bf16[8,7168]{1,0:T(8,128)(2,1)S(1)}, u32[]{:S(2)}, u32[]{:S(2)}) %collective-permute-start.22) | collective-permute-done | bytes 114720 | tf_op jit(solution)/shard_map/ppermute | solution.py:246
  53.5 0.7 %finish.1 = bf16[8,7168]{1,0:T(8,128)(2,1)} custom-call(f32[8,7168]{1,0:T(8,128)S(1)} %combine.1.near_ref, bf16[8,7168]{1,0:T(8,128)(2,1)S(1)} %collective-permute-done.22.top_ref), custom_call_target="tpu_custom_call" | custom-call | tf_op jit(solution)/shard_map/finish/pallas_call | solution.py:375
  (7 shorter events, 0.1 us)
Async XLA Ops:
  2.3 6.7 %collective-permute-start.2 = (bf16[8,7168]{1,0:T(8,128)(2,1)}, bf16[8,7168]{1,0:T(8,128)(2,1)S(1)}, u32[]{:S(2)}, u32[]{:S(2)}) collective-permute-start(bf16[8,7168]{1,0:T(8,128)(2,1)} %get-tuple-element.38), channel_id=1, source_target_pairs={{0,8},{1,9},{2,10},{3,11},{4,12},{5,13},{6,14},{7,15},{8,0},{9,1},... | collective-permute-start | bytes 344072 | tf_op jit(solution)/shard_map/ppermute | solution.py:246
  5.4 12.1 %collective-permute-start = (bf16[8,7296]{1,0:T(8,128)(2,1)}, bf16[8,7296]{1,0:T(8,128)(2,1)S(1)}, u32[]{:S(2)}, u32[]{:S(2)}) collective-permute-start(bf16[8,7296]{1,0:T(8,128)(2,1)} %get-tuple-element.35), channel_id=1, source_target_pairs={{0,16},{1,17},{2,18},{3,19},{4,20},{5,21},{6,22},{7,23},{8,24},{9,... | collective-permute-start | bytes 350216 | tf_op jit(solution)/shard_map/ppermute | solution.py:246
  8.0 9.5 %collective-permute-start.1 = (bf16[8,7296]{1,0:T(8,128)(2,1)}, bf16[8,7296]{1,0:T(8,128)(2,1)S(1)}, u32[]{:S(2)}, u32[]{:S(2)}) collective-permute-start(bf16[8,7296]{1,0:T(8,128)(2,1)} %get-tuple-element.36), channel_id=1, source_target_pairs={{0,24},{1,25},{2,26},{3,27},{4,28},{5,29},{6,30},{7,31},{8,16},{9,... | collective-permute-start | bytes 350216 | tf_op jit(solution)/shard_map/ppermute | solution.py:246
  8.0 0.9 %copy-start.2 = (bf16[8,7168]{1,0:T(8,128)(2,1)S(1)}, bf16[8,7168]{1,0:T(8,128)(2,1)}, u32[]{:S(2)}) copy-start(bf16[8,7168]{1,0:T(8,128)(2,1)} %get-tuple-element.37.refs_0_) | copy-start | bytes 344068
  9.1 11.5 %collective-permute-start.8 = (bf16[8,7168]{1,0:T(8,128)(2,1)S(1)}, bf16[8,7168]{1,0:T(8,128)(2,1)S(1)}, u32[]{:S(2)}, u32[]{:S(2)}) collective-permute-start(bf16[8,7168]{1,0:T(8,128)(2,1)S(1)} %get-tuple-element.42), channel_id=1, source_target_pairs={{0,6},{1,7},{2,4},{3,5},{4,2},{5,3},{6,0},{7,1},{8,14},{9,15},{10,... | collective-permute-start | bytes 344072 | tf_op jit(solution)/shard_map/ppermute | solution.py:246
  12.8 8.3 %collective-permute-start.7 = (bf16[8,7168]{1,0:T(8,128)(2,1)S(1)}, bf16[8,7168]{1,0:T(8,128)(2,1)S(1)}, u32[]{:S(2)}, u32[]{:S(2)}) collective-permute-start(bf16[8,7168]{1,0:T(8,128)(2,1)S(1)} %get-tuple-element.42), channel_id=1, source_target_pairs={{0,4},{1,5},{2,6},{3,7},{4,0},{5,1},{6,2},{7,3},{8,12},{9,13},{10,... | collective-permute-start | bytes 344072 | tf_op jit(solution)/shard_map/ppermute | solution.py:246
  13.3 7.8 %collective-permute-start.6 = (bf16[8,7168]{1,0:T(8,128)(2,1)S(1)}, bf16[8,7168]{1,0:T(8,128)(2,1)S(1)}, u32[]{:S(2)}, u32[]{:S(2)}) collective-permute-start(bf16[8,7168]{1,0:T(8,128)(2,1)S(1)} %get-tuple-element.39.refs_1_.refs_0_), channel_id=1, source_target_pairs={{0,2},{1,3},{2,0},{3,1},{4,6},{5,7},{6,4},{7,5},{8,10},{9,11},{10,... | collective-permute-start | bytes 344072 | tf_op jit(solution)/shard_map/ppermute | solution.py:246
  13.4 2.0 %copy-start = (bf16[7168,256]{1,0:T(8,128)(2,1)S(1)}, bf16[7168,256]{1,0:T(8,128)(2,1)}, u32[]{:S(2)}) copy-start(bf16[7168,256]{1,0:T(8,128)(2,1)} %refs_0_.2) | copy-start | bytes 11010052
  15.7 5.5 %copy-start.1 = (bf16[7168,256]{1,0:T(8,128)(2,1)S(1)}, bf16[7168,256]{1,0:T(8,128)(2,1)}, u32[]{:S(2)}) copy-start(bf16[7168,256]{1,0:T(8,128)(2,1)} %refs_0_.3) | copy-start | bytes 11010052
  17.6 6.0 %collective-permute-start.5 = (bf16[8,7168]{1,0:T(8,128)(2,1)S(1)}, bf16[8,7168]{1,0:T(8,128)(2,1)S(1)}, u32[]{:S(2)}, u32[]{:S(2)}) collective-permute-start(bf16[8,7168]{1,0:T(8,128)(2,1)S(1)} %get-tuple-element.41), channel_id=1, source_target_pairs={{0,6},{1,7},{2,4},{3,5},{4,2},{5,3},{6,0},{7,1},{8,14},{9,15},{10,... | collective-permute-start | bytes 344072 | tf_op jit(solution)/shard_map/ppermute | solution.py:246
  20.1 4.8 %collective-permute-start.4 = (bf16[8,7168]{1,0:T(8,128)(2,1)S(1)}, bf16[8,7168]{1,0:T(8,128)(2,1)S(1)}, u32[]{:S(2)}, u32[]{:S(2)}) collective-permute-start(bf16[8,7168]{1,0:T(8,128)(2,1)S(1)} %get-tuple-element.41), channel_id=1, source_target_pairs={{0,4},{1,5},{2,6},{3,7},{4,0},{5,1},{6,2},{7,3},{8,12},{9,13},{10,... | collective-permute-start | bytes 344072 | tf_op jit(solution)/shard_map/ppermute | solution.py:246
  20.6 4.8 %collective-permute-start.3 = (bf16[8,7168]{1,0:T(8,128)(2,1)S(1)}, bf16[8,7168]{1,0:T(8,128)(2,1)S(1)}, u32[]{:S(2)}, u32[]{:S(2)}) collective-permute-start(bf16[8,7168]{1,0:T(8,128)(2,1)S(1)} %get-tuple-element.40.refs_4_.refs_0_), channel_id=1, source_target_pairs={{0,2},{1,3},{2,0},{3,1},{4,6},{5,7},{6,4},{7,5},{8,10},{9,11},{10,... | collective-permute-start | bytes 344072 | tf_op jit(solution)/shard_map/ppermute | solution.py:246
  21.2 4.3 %collective-permute-start.10 = (bf16[32,7168]{1,0:T(8,128)(2,1)S(1)}, bf16[32,7168]{1,0:T(8,128)(2,1)S(1)}, u32[]{:S(2)}, u32[]{:S(2)}) collective-permute-start(bf16[32,7168]{1,0:T(8,128)(2,1)S(1)} %join.2.refs_2_), channel_id=1, source_target_pairs={{0,1},{1,0},{2,3},{3,2},{4,5},{5,4},{6,7},{7,6},{8,9},{9,8},{10,11... | collective-permute-start | bytes 1376264 | tf_op jit(solution)/shard_map/ppermute | solution.py:246
  25.4 1.9 %collective-permute-start.9 = (bf16[32,7168]{1,0:T(8,128)(2,1)S(1)}, bf16[32,7168]{1,0:T(8,128)(2,1)S(1)}, u32[]{:S(2)}, u32[]{:S(2)}) collective-permute-start(bf16[32,7168]{1,0:T(8,128)(2,1)S(1)} %join.3.refs_0_), channel_id=1, source_target_pairs={{0,1},{1,0},{2,3},{3,2},{4,5},{5,4},{6,7},{7,6},{8,9},{9,8},{10,11... | collective-permute-start | bytes 1376264 | tf_op jit(solution)/shard_map/ppermute | solution.py:246
  29.1 21.9 %copy-start.3 = (f32[24,16]{1,0:T(8,128)S(1)}, f32[24,16]{1,0:T(8,128)}, u32[]{:S(2)}) copy-start(f32[24,16]{1,0:T(8,128)} %get-tuple-element.63.table_ref) | copy-start | bytes 4612
  29.8 1.9 %collective-permute-start.14 = (bf16[32,7168]{1,0:T(8,128)(2,1)S(1)}, bf16[32,7168]{1,0:T(8,128)(2,1)S(1)}, u32[]{:S(2)}, u32[]{:S(2)}) collective-permute-start(bf16[32,7168]{1,0:T(8,128)(2,1)S(1)} %get-tuple-element.53), channel_id=1, source_target_pairs={{0,1},{1,0},{2,3},{3,2},{4,5},{5,4},{6,7},{7,6},{8,9},{9,8},{10,11... | collective-permute-start | bytes 1376264 | tf_op jit(solution)/shard_map/ppermute | solution.py:246
  30.0 5.3 %collective-permute-start.11 = (bf16[32,7168]{1,0:T(8,128)(2,1)S(1)}, bf16[32,7168]{1,0:T(8,128)(2,1)S(1)}, u32[]{:S(2)}, u32[]{:S(2)}) collective-permute-start(bf16[32,7168]{1,0:T(8,128)(2,1)S(1)} %get-tuple-element.48), channel_id=1, source_target_pairs={{0,1},{1,0},{2,3},{3,2},{4,5},{5,4},{6,7},{7,6},{8,9},{9,8},{10,11... | collective-permute-start | bytes 1376264 | tf_op jit(solution)/shard_map/ppermute | solution.py:246
  31.7 6.1 %collective-permute-start.15 = (bf16[8,7168]{1,0:T(8,128)(2,1)S(1)}, bf16[8,7168]{1,0:T(8,128)(2,1)S(1)}, u32[]{:S(2)}, u32[]{:S(2)}) collective-permute-start(bf16[8,7168]{1,0:T(8,128)(2,1)S(1)} %get-tuple-element.55), channel_id=1, source_target_pairs={{0,2},{1,3},{2,0},{3,1},{4,6},{5,7},{6,4},{7,5},{8,10},{9,11},{10,... | collective-permute-start | bytes 344072 | tf_op jit(solution)/shard_map/ppermute | solution.py:246
  32.6 6.2 %collective-permute-start.16 = (bf16[8,7168]{1,0:T(8,128)(2,1)S(1)}, bf16[8,7168]{1,0:T(8,128)(2,1)S(1)}, u32[]{:S(2)}, u32[]{:S(2)}) collective-permute-start(bf16[8,7168]{1,0:T(8,128)(2,1)S(1)} %get-tuple-element.56), channel_id=1, source_target_pairs={{0,4},{1,5},{2,6},{3,7},{4,0},{5,1},{6,2},{7,3},{8,12},{9,13},{10,... | collective-permute-start | bytes 344072 | tf_op jit(solution)/shard_map/ppermute | solution.py:246
  33.9 6.5 %collective-permute-start.17 = (bf16[8,7168]{1,0:T(8,128)(2,1)S(1)}, bf16[8,7168]{1,0:T(8,128)(2,1)S(1)}, u32[]{:S(2)}, u32[]{:S(2)}) collective-permute-start(bf16[8,7168]{1,0:T(8,128)(2,1)S(1)} %get-tuple-element.57), channel_id=1, source_target_pairs={{0,6},{1,7},{2,4},{3,5},{4,2},{5,3},{6,0},{7,1},{8,14},{9,15},{10,... | collective-permute-start | bytes 344072 | tf_op jit(solution)/shard_map/ppermute | solution.py:246
  35.4 7.4 %collective-permute-start.12 = (bf16[8,7168]{1,0:T(8,128)(2,1)S(1)}, bf16[8,7168]{1,0:T(8,128)(2,1)S(1)}, u32[]{:S(2)}, u32[]{:S(2)}) collective-permute-start(bf16[8,7168]{1,0:T(8,128)(2,1)S(1)} %get-tuple-element.50), channel_id=1, source_target_pairs={{0,8},{1,9},{2,10},{3,11},{4,12},{5,13},{6,14},{7,15},{8,0},{9,1},... | collective-permute-start | bytes 344072 | tf_op jit(solution)/shard_map/ppermute | solution.py:246
  37.3 5.5 %collective-permute-start.13 = (bf16[8,7168]{1,0:T(8,128)(2,1)S(1)}, bf16[8,7168]{1,0:T(8,128)(2,1)S(1)}, u32[]{:S(2)}, u32[]{:S(2)}) collective-permute-start(bf16[8,7168]{1,0:T(8,128)(2,1)S(1)} %get-tuple-element.51), channel_id=1, source_target_pairs={{0,8},{1,9},{2,10},{3,11},{4,12},{5,13},{6,14},{7,15},{8,0},{9,1},... | collective-permute-start | bytes 344072 | tf_op jit(solution)/shard_map/ppermute | solution.py:246
  40.9 5.6 %collective-permute-start.21 = (bf16[8,7168]{1,0:T(8,128)(2,1)S(1)}, bf16[8,7168]{1,0:T(8,128)(2,1)S(1)}, u32[]{:S(2)}, u32[]{:S(2)}) collective-permute-start(bf16[8,7168]{1,0:T(8,128)(2,1)S(1)} %get-tuple-element.64), channel_id=1, source_target_pairs={{0,8},{1,9},{2,10},{3,11},{4,12},{5,13},{6,14},{7,15},{8,0},{9,1},... | collective-permute-start | bytes 344072 | tf_op jit(solution)/shard_map/ppermute | solution.py:246
  42.9 6.0 %collective-permute-start.18 = (bf16[8,7168]{1,0:T(8,128)(2,1)S(1)}, bf16[8,7168]{1,0:T(8,128)(2,1)S(1)}, u32[]{:S(2)}, u32[]{:S(2)}) collective-permute-start(bf16[8,7168]{1,0:T(8,128)(2,1)S(1)} %get-tuple-element.60), channel_id=1, source_target_pairs={{0,2},{1,3},{2,0},{3,1},{4,6},{5,7},{6,4},{7,5},{8,10},{9,11},{10,... | collective-permute-start | bytes 344072 | tf_op jit(solution)/shard_map/ppermute | solution.py:246
  44.3 4.8 %collective-permute-start.19 = (bf16[8,7168]{1,0:T(8,128)(2,1)S(1)}, bf16[8,7168]{1,0:T(8,128)(2,1)S(1)}, u32[]{:S(2)}, u32[]{:S(2)}) collective-permute-start(bf16[8,7168]{1,0:T(8,128)(2,1)S(1)} %get-tuple-element.61), channel_id=1, source_target_pairs={{0,4},{1,5},{2,6},{3,7},{4,0},{5,1},{6,2},{7,3},{8,12},{9,13},{10,... | collective-permute-start | bytes 344072 | tf_op jit(solution)/shard_map/ppermute | solution.py:246
  45.3 5.7 %collective-permute-start.20 = (bf16[8,7168]{1,0:T(8,128)(2,1)S(1)}, bf16[8,7168]{1,0:T(8,128)(2,1)S(1)}, u32[]{:S(2)}, u32[]{:S(2)}) collective-permute-start(bf16[8,7168]{1,0:T(8,128)(2,1)S(1)} %get-tuple-element.62), channel_id=1, source_target_pairs={{0,6},{1,7},{2,4},{3,5},{4,2},{5,3},{6,0},{7,1},{8,14},{9,15},{10,... | collective-permute-start | bytes 344072 | tf_op jit(solution)/shard_map/ppermute | solution.py:246
  46.5 7.0 %collective-permute-start.22 = (bf16[8,7168]{1,0:T(8,128)(2,1)S(1)}, bf16[8,7168]{1,0:T(8,128)(2,1)S(1)}, u32[]{:S(2)}, u32[]{:S(2)}) collective-permute-start(bf16[8,7168]{1,0:T(8,128)(2,1)S(1)} %add_convert_fusion), channel_id=1, source_target_pairs={{0,16},{1,17},{2,18},{3,19},{4,20},{5,21},{6,22},{7,23},{8,24},{9,... | collective-permute-start | bytes 344072 | tf_op jit(solution)/shard_map/ppermute | solution.py:246
